TPU v7x, 32 devices: a whole 2x2x4 slice. The times are simulated.
32 devices in a mesh: groups: 2 (over y), ctx: 16 (over z, x, core).
Axes of the slice: x: 2, y: 2, z: 4, core: 2. Of those that a mesh axis runs over, the one named last changes fastest.
Arguments:
- values: bfloat16 [2048, 4096], P(None, ('groups', 'ctx')), parts along dimension 1, may hold values from -6 to 6
- keys: bfloat16 [2048, 4096], P(None, ('groups', 'ctx')), parts along dimension 1, may hold values from -6 to 6
- queries: bfloat16 [2048, 4096], P(None, ('groups', 'ctx')), parts along dimension 1, may hold values from -6 to 6
- grad_out: bfloat16 [2048, 4096], P(None, ('groups', 'ctx')), parts along dimension 1, may hold values from -6 to 6
- filters: float32 [2048, 2048], P(None, 'ctx'), may hold values from -4 to 4, as said below
Outputs:
- grad_values: bfloat16 [2048, 4096], P(None, ('groups', 'ctx')), parts along dimension 1
- grad_keys: bfloat16 [2048, 4096], P(None, ('groups', 'ctx')), parts along dimension 1
- grad_queries: bfloat16 [2048, 4096], P(None, ('groups', 'ctx')), parts along dimension 1
- grad_filters: float32 [2048, 4096], P(None, ('groups', 'ctx')), parts along dimension 1
There are 2 independent parts, one for each index of `groups`. A program takes and returns all parts, laid end to end along the dimension named above; an argument that names none is the same for every part. Nothing has to cross between parts.
Inputs may be any that keep to these rules, and one draw needn't show every extreme that they name: `filters`: each channel's filter decays along its taps at a rate of its own.
All inputs are finite; a program needn't handle non-finite values.
Results may differ from a plain program's by a relative error of at most 0.0092.
Values may be sent and summed in bfloat16 or wider, within the bound.
No kernel may reach another device: no remote copies, remote signals or barrier semaphores. Data moves between devices by JAX's collectives and lax.ppermute only.
A program may use at most 64 MiB of HBM per device.

v0:
```python
import math

import jax
import jax.numpy as jnp
import numpy as np
from jax import lax
from jax.experimental import pallas as pl
from jax.experimental.pallas import tpu as pltpu
from jax.sharding import PartitionSpec as P

TILE = 16


def leaf_angles(count, theta=math.pi / 2):
    if count == 1:
        return [theta]
    half = theta / 2
    return leaf_angles(count // 2, half) + leaf_angles(count // 2, half + math.pi)


def evaluate(points, theta):
    count = len(points)
    if count == 1:
        return points
    half, phi = count // 2, theta / 2
    c, s = math.cos(phi), math.sin(phi)
    first, second = [], []
    for low, high in zip(points[:half], points[half:]):
        if low[1] is None:
            turned_re, turned_im = high[0] * c, high[0] * -s
            first.append((low[0] + turned_re, turned_im))
            second.append((low[0] - turned_re, -turned_im))
        else:
            turned_re = high[0] * c + high[1] * s
            turned_im = high[1] * c - high[0] * s
            first.append((low[0] + turned_re, low[1] + turned_im))
            second.append((low[0] - turned_re, low[1] - turned_im))
    return evaluate(first, phi) + evaluate(second, phi + math.pi)


def interpolate(values, theta, top=True):
    count = len(values)
    if count == 1:
        return values
    half, phi = count // 2, theta / 2
    c, s = math.cos(phi), math.sin(phi)
    first = interpolate(values[:half], phi, False)
    second = interpolate(values[half:], phi + math.pi, False)
    low, high = [], []
    for (a_re, a_im), (b_re, b_im) in zip(first, second):
        gap_re, gap_im = a_re - b_re, a_im - b_im
        if top:
            low.append(a_re + b_re)
            high.append(gap_re * c - gap_im * s)
        else:
            low.append((a_re + b_re, a_im + b_im))
            high.append((gap_re * c - gap_im * s, gap_re * s + gap_im * c))
    return low + high


def make_tables(shards, width):
    angles = np.array(leaf_angles(shards))
    turn = np.outer(angles, np.arange(width)) / width
    scale = 1.0 / (shards * width)
    twist = np.stack(
        [np.cos(turn), np.sin(turn), np.cos(turn) * scale, np.sin(turn) * scale], axis=1
    ).astype(np.float32)
    wave = np.outer(np.arange(width), np.arange(width)) % width * (2 * math.pi / width)
    c, s = np.cos(wave), np.sin(wave)
    ahead = np.block([[c, -s], [s, c]])
    return twist, jnp.asarray(ahead, jnp.bfloat16), jnp.asarray(ahead.T, jnp.bfloat16)


def gate_kernel(value_ref, key_ref, query_ref, cot_ref, filter_ref, out_ref):
    out_ref[0, 0] = (
        value_ref[...].astype(jnp.float32) * key_ref[...].astype(jnp.float32)
    ).astype(jnp.bfloat16)
    out_ref[0, 1] = (
        cot_ref[...].astype(jnp.float32) * query_ref[...].astype(jnp.float32)
    ).astype(jnp.bfloat16)
    out_ref[0, 2] = filter_ref[...].astype(jnp.bfloat16)


def spectral_kernel(sig_ref, twist_ref, ahead_ref, back_ref, out_ref, turned_ref):
    shards, _, tile, width = sig_ref.shape
    specs = []
    for which in range(3):
        points = [(sig_ref[b, which].astype(jnp.float32), None) for b in range(shards)]
        for k, (re, im) in enumerate(evaluate(points, math.pi / 2)):
            c, s = twist_ref[k, 0:1, :], twist_ref[k, 1:2, :]
            rows = slice(k * tile, (k + 1) * tile)
            turned_ref[which, rows, :width] = (re * c + im * s).astype(jnp.bfloat16)
            turned_ref[which, rows, width:] = (im * c - re * s).astype(jnp.bfloat16)
        spec = jnp.dot(turned_ref[which], ahead_ref[...], preferred_element_type=jnp.float32)
        specs.append((spec[:, :width], spec[:, width:]))
    (m_re, m_im), (g_re, g_im), (f_re, f_im) = specs
    results = (
        (f_re * m_re - f_im * m_im, f_re * m_im + f_im * m_re),
        (f_re * g_re + f_im * g_im, f_re * g_im - f_im * g_re),
        (g_re * m_re + g_im * m_im, g_im * m_re - g_re * m_im),
    )
    for which, (re, im) in enumerate(results):
        both = jnp.concatenate([re.astype(jnp.bfloat16), im.astype(jnp.bfloat16)], axis=1)
        back = jnp.dot(both, back_ref[...], preferred_element_type=jnp.float32)
        values = []
        for k in range(shards):
            rows = slice(k * tile, (k + 1) * tile)
            re, im = back[rows, :width], back[rows, width:]
            c, s = twist_ref[k, 2:3, :], twist_ref[k, 3:4, :]
            values.append((re * c - im * s, re * s + im * c))
        for b, part in enumerate(interpolate(values, math.pi / 2)):
            out_ref[b, which] = part.astype(jnp.bfloat16)


def ungate_kernel(part_ref, value_ref, key_ref, cot_ref, gv_ref, gk_ref, gq_ref, gf_ref):
    conv = part_ref[0, 0].astype(jnp.float32)
    grad = part_ref[0, 1].astype(jnp.float32)
    gv_ref[...] = (grad * key_ref[...].astype(jnp.float32)).astype(jnp.bfloat16)
    gk_ref[...] = (grad * value_ref[...].astype(jnp.float32)).astype(jnp.bfloat16)
    gq_ref[...] = (cot_ref[...].astype(jnp.float32) * conv).astype(jnp.bfloat16)
    gf_ref[...] = part_ref[0, 2].astype(jnp.float32)


def shards(values, keys, queries, grad_out, filters):
    count = lax.axis_size("ctx")
    channels, width = values.shape
    chunk = channels // count
    twist, ahead, back = make_tables(count, width)
    rows = pl.BlockSpec((chunk, width), lambda i: (i, 0))
    packed = pl.BlockSpec((1, 3, chunk, width), lambda i: (i, 0, 0, 0))
    sent = pl.pallas_call(
        gate_kernel,
        grid=(count,),
        in_specs=[rows] * 5,
        out_specs=packed,
        out_shape=jax.ShapeDtypeStruct((count, 3, chunk, width), jnp.bfloat16),
    )(values, keys, queries, grad_out, filters)
    held = lax.all_to_all(sent, "ctx", split_axis=0, concat_axis=0, tiled=True)
    whole = lambda *shape: pl.BlockSpec(shape, lambda i: (0,) * len(shape))
    lanes = pl.BlockSpec((count, 3, TILE, width), lambda i: (0, 0, i, 0))
    made = pl.pallas_call(
        spectral_kernel,
        grid=(chunk // TILE,),
        in_specs=[
            lanes,
            whole(count, 4, width),
            whole(2 * width, 2 * width),
            whole(2 * width, 2 * width),
        ],
        out_specs=lanes,
        out_shape=jax.ShapeDtypeStruct((count, 3, chunk, width), jnp.bfloat16),
        scratch_shapes=[pltpu.VMEM((3, count * TILE, 2 * width), jnp.bfloat16)],
        compiler_params=pltpu.CompilerParams(vmem_limit_bytes=48 * 1024 * 1024),
    )(held, twist, ahead, back)
    returned = lax.all_to_all(made, "ctx", split_axis=0, concat_axis=0, tiled=True)
    half = jax.ShapeDtypeStruct((channels, width), jnp.bfloat16)
    return pl.pallas_call(
        ungate_kernel,
        grid=(count,),
        in_specs=[packed, rows, rows, rows],
        out_specs=[rows] * 4,
        out_shape=[half, half, half, jax.ShapeDtypeStruct((channels, width), jnp.float32)],
    )(returned, values, keys, grad_out)


def solution(mesh):
    token = P(None, ("groups", "ctx"))
    return jax.shard_map(
        shards,
        mesh=mesh,
        in_specs=(token, token, token, token, P(None, "ctx")),
        out_specs=(token, token, token, token),
        check_vma=False,
    )
```

profile of v0, /device:TPU:13, one launch (start us, length us, event | category | flops | bytes accessed | tf_op | source)
XLA Modules:
  0.0 112.0 jit_solution(3629771674772843714)
XLA Ops:
  0.6 9.5 %shard_map.111 = bf16[16,3,128,128]{3,2,1,0:T(8,128)(2,1)} custom-call(bf16[2048,128]{1,0:T(8,128)(2,1)} %value_ref.3, bf16[2048,128]{1,0:T(8,128)(2,1)} %key_ref.3, bf16[2048,128]{1,0:T(8,128)(2,1)} %query_ref.1, bf16[2048,128]{1,0:T(8,128)(2,1)} %cot_ref.3, f32[2048,128]{1,0:T(8,128)} %filter_ref.1), custom_call_target="tpu_custom_call" | custom-call | tf_op jit(solution)/shard_map/pallas_call | solution.py:131
  10.2 0.0 copy-start
  10.2 0.0 copy-start.1
  10.2 0.0 copy-start.2
  10.2 43.3 %all_to_all.10.sig_ref = bf16[16,3,128,128]{3,2,1,0:T(8,128)(2,1)S(1)} all-to-all(bf16[16,3,128,128]{3,2,1,0:T(8,128)(2,1)} %shard_map.111), channel_id=1, replica_groups=mesh['groups'=2,'ctx'=16] {'ctx'}, dimensions={0} | all-to-all | bytes 3145728 | tf_op jit(solution)/shard_map/all_to_all | solution.py:138
  53.5 0.0 copy-done
  53.5 0.0 copy-done.1
  53.5 0.0 copy-done.2
  53.5 7.9 %shard_map.112 = bf16[16,3,128,128]{3,2,1,0:T(8,128)(2,1)S(1)} custom-call(bf16[16,3,128,128]{3,2,1,0:T(8,128)(2,1)S(1)} %all_to_all.10.sig_ref, f32[16,4,128]{2,1,0:T(4,128)S(1)} %copy-done.2, bf16[256,256]{1,0:T(8,128)(2,1)S(1)} %copy-done.1, bf16[256,256]{1,0:T(8,128)(2,1)S(1)} %copy-done), custom_call_target="tpu_custom_call" | custom-call | tf_op jit(solution)/shard_map/pallas_call | solution.py:141
  61.4 41.0 %all_to_all.11.part_ref = bf16[16,3,128,128]{3,2,1,0:T(8,128)(2,1)} all-to-all(bf16[16,3,128,128]{3,2,1,0:T(8,128)(2,1)S(1)} %shard_map.112), channel_id=1, replica_groups=mesh['groups'=2,'ctx'=16] {'ctx'}, dimensions={0} | all-to-all | bytes 3145728 | tf_op jit(solution)/shard_map/all_to_all | solution.py:155
  102.4 9.6 %shard_map.113 = (bf16[2048,128]{1,0:T(8,128)(2,1)}, bf16[2048,128]{1,0:T(8,128)(2,1)}, bf16[2048,128]{1,0:T(8,128)(2,1)}, f32[2048,128]{1,0:T(8,128)}) custom-call(bf16[16,3,128,128]{3,2,1,0:T(8,128)(2,1)} %all_to_all.11.part_ref, bf16[2048,128]{1,0:T(8,128)(2,1)} %value_ref.3, bf16[2048,128]{1,0:T(8,128)(2,1)} %key_ref.3, bf16[2048,128]{1,0:T(8,128)(2,1)} %cot_ref.3), custom_call_target="tpu_custom_call" | custom-call | tf_op jit(solution)/shard_map/pallas_call | solution.py:157
Async XLA Ops:
  10.2 43.4 %copy-start = (bf16[256,256]{1,0:T(8,128)(2,1)S(1)}, bf16[256,256]{1,0:T(8,128)(2,1)}, u32[]{:S(2)}) copy-start(bf16[256,256]{1,0:T(8,128)(2,1)} %constant.7.clone.back_ref) | copy-start | bytes 393220
  10.2 43.4 %copy-start.1 = (bf16[256,256]{1,0:T(8,128)(2,1)S(1)}, bf16[256,256]{1,0:T(8,128)(2,1)}, u32[]{:S(2)}) copy-start(bf16[256,256]{1,0:T(8,128)(2,1)} %constant.6.clone.ahead_ref) | copy-start | bytes 393220
  10.2 43.4 %copy-start.2 = (f32[16,4,128]{2,1,0:T(4,128)S(1)}, f32[16,4,128]{2,1,0:T(4,128)}, u32[]{:S(2)}) copy-start(f32[16,4,128]{2,1,0:T(4,128)} %constant.8.clone.twist_ref) | copy-start | bytes 98308
where the time goes:
time: 114 us; the launch traced here: 112 us
  blocking collectives  84.4 us (74%)
  Pallas kernels  27 us (24%)
    all_to_all x1, blocking collectives, shards(): held = lax.all_to_all(sent, 'ctx', split_axis=0, concat_axis=0, tiled=True)  43.3 us
    all_to_all x1, blocking collectives, shards(): lax.all_to_all(made, 'ctx', split_axis=0, concat_axis=0, tiled=True)  41 us
    pallas_call x1, Pallas kernels, shards(): pl.pallas_call(ungate_kernel, grid=(count,), in_specs=[packed, rows, rows...  9.63 us
    pallas_call x1, Pallas kernels, shards(): pl.pallas_call(gate_kernel, grid=(count,), in_specs=[rows] * 5, out_specs...  9.54 us
    pallas_call x1, Pallas kernels, shards(): pl.pallas_call(spectral_kernel, grid=(chunk // TILE,), in_specs=[lanes, w...  7.85 us

commit v1 on v0

--- a/solution.py
+++ b/solution.py
@@ -9,6 +9,7 @@
 from jax.sharding import PartitionSpec as P
 
 TILE = 16
+STEPS = 4
 
 
 def leaf_angles(count, theta=math.pi / 2):
@@ -72,16 +73,27 @@
 
 
 def gate_kernel(value_ref, key_ref, query_ref, cot_ref, filter_ref, out_ref):
-    out_ref[0, 0] = (
-        value_ref[...].astype(jnp.float32) * key_ref[...].astype(jnp.float32)
-    ).astype(jnp.bfloat16)
-    out_ref[0, 1] = (
-        cot_ref[...].astype(jnp.float32) * query_ref[...].astype(jnp.float32)
-    ).astype(jnp.bfloat16)
-    out_ref[0, 2] = filter_ref[...].astype(jnp.bfloat16)
+    blocks, _, chunk, width = out_ref.shape
+    shape = (blocks, chunk, width)
+    mixed = value_ref[...].astype(jnp.float32) * key_ref[...].astype(jnp.float32)
+    grad = cot_ref[...].astype(jnp.float32) * query_ref[...].astype(jnp.float32)
+    out_ref[:, 0] = mixed.astype(jnp.bfloat16).reshape(shape)
+    out_ref[:, 1] = grad.astype(jnp.bfloat16).reshape(shape)
+    out_ref[:, 2] = filter_ref[...].astype(jnp.bfloat16).reshape(shape)
 
 
 def spectral_kernel(sig_ref, twist_ref, ahead_ref, back_ref, out_ref, turned_ref):
+    shards, _, chunk, width = sig_ref.shape
+
+    @pl.loop(0, chunk // TILE)
+    def _(step):
+        lanes = pl.ds(pl.multiple_of(step * TILE, TILE), TILE)
+        spectral_tile(
+            sig_ref.at[:, :, lanes], twist_ref, ahead_ref, back_ref, out_ref.at[:, :, lanes], turned_ref
+        )
+
+
+def spectral_tile(sig_ref, twist_ref, ahead_ref, back_ref, out_ref, turned_ref):
     shards, _, tile, width = sig_ref.shape
     specs = []
     for which in range(3):
@@ -113,12 +125,18 @@
 
 
 def ungate_kernel(part_ref, value_ref, key_ref, cot_ref, gv_ref, gk_ref, gq_ref, gf_ref):
-    conv = part_ref[0, 0].astype(jnp.float32)
-    grad = part_ref[0, 1].astype(jnp.float32)
-    gv_ref[...] = (grad * key_ref[...].astype(jnp.float32)).astype(jnp.bfloat16)
-    gk_ref[...] = (grad * value_ref[...].astype(jnp.float32)).astype(jnp.bfloat16)
-    gq_ref[...] = (cot_ref[...].astype(jnp.float32) * conv).astype(jnp.bfloat16)
-    gf_ref[...] = part_ref[0, 2].astype(jnp.float32)
+    _, _, chunk, width = part_ref.shape
+    span = gv_ref.shape[0]
+    step = pl.program_id(0)
+    blocks = pl.ds(step * (span // chunk), span // chunk)
+    rows = pl.ds(pl.multiple_of(step * span, span), span)
+    conv, grad, filt = (
+        part_ref[blocks, which].astype(jnp.float32).reshape(span, width) for which in range(3)
+    )
+    gv_ref[...] = (grad * key_ref[rows].astype(jnp.float32)).astype(jnp.bfloat16)
+    gk_ref[...] = (grad * value_ref[rows].astype(jnp.float32)).astype(jnp.bfloat16)
+    gq_ref[...] = (cot_ref[rows].astype(jnp.float32) * conv).astype(jnp.bfloat16)
+    gf_ref[...] = filt
 
 
 def shards(values, keys, queries, grad_out, filters):
@@ -126,40 +144,36 @@
     channels, width = values.shape
     chunk = channels // count
     twist, ahead, back = make_tables(count, width)
-    rows = pl.BlockSpec((chunk, width), lambda i: (i, 0))
-    packed = pl.BlockSpec((1, 3, chunk, width), lambda i: (i, 0, 0, 0))
+    rows = pl.BlockSpec((channels // STEPS, width), lambda i: (i, 0))
+    packed = pl.BlockSpec((count // STEPS, 3, chunk, width), lambda i: (i, 0, 0, 0))
+    here = pl.BlockSpec(memory_space=pltpu.VMEM)
+    limit = pltpu.CompilerParams(vmem_limit_bytes=48 * 1024 * 1024)
     sent = pl.pallas_call(
         gate_kernel,
-        grid=(count,),
+        grid=(STEPS,),
         in_specs=[rows] * 5,
         out_specs=packed,
         out_shape=jax.ShapeDtypeStruct((count, 3, chunk, width), jnp.bfloat16),
+        compiler_params=limit,
     )(values, keys, queries, grad_out, filters)
     held = lax.all_to_all(sent, "ctx", split_axis=0, concat_axis=0, tiled=True)
-    whole = lambda *shape: pl.BlockSpec(shape, lambda i: (0,) * len(shape))
-    lanes = pl.BlockSpec((count, 3, TILE, width), lambda i: (0, 0, i, 0))
     made = pl.pallas_call(
         spectral_kernel,
-        grid=(chunk // TILE,),
-        in_specs=[
-            lanes,
-            whole(count, 4, width),
-            whole(2 * width, 2 * width),
-            whole(2 * width, 2 * width),
-        ],
-        out_specs=lanes,
+        in_specs=[here] * 4,
+        out_specs=here,
         out_shape=jax.ShapeDtypeStruct((count, 3, chunk, width), jnp.bfloat16),
         scratch_shapes=[pltpu.VMEM((3, count * TILE, 2 * width), jnp.bfloat16)],
-        compiler_params=pltpu.CompilerParams(vmem_limit_bytes=48 * 1024 * 1024),
+        compiler_params=limit,
     )(held, twist, ahead, back)
     returned = lax.all_to_all(made, "ctx", split_axis=0, concat_axis=0, tiled=True)
     half = jax.ShapeDtypeStruct((channels, width), jnp.bfloat16)
     return pl.pallas_call(
         ungate_kernel,
-        grid=(count,),
-        in_specs=[packed, rows, rows, rows],
+        grid=(STEPS,),
+        in_specs=[here] * 4,
         out_specs=[rows] * 4,
         out_shape=[half, half, half, jax.ShapeDtypeStruct((channels, width), jnp.float32)],
+        compiler_params=limit,
     )(returned, values, keys, grad_out)
 
 

time: 114 us -> 101 us (0.89)
  Pallas kernels: 27 us -> 9.79 us
  local copies, waits for them, and re-layouts: 0.01 us -> 5.42 us
    pallas_call x3, Pallas kernels: 27 us -> 9.79 us  [the longest x1 7.49 us: shards(): pl.pallas_call(spectral_kernel, in_specs=[here] * 4, out_specs=here, out_...]
    unnamed x6 -> x22, local copies, waits for them, and re-layouts: 0.01 us -> 5.42 us
where the time goes in v1:
time: 101 us; the launch traced here: 100 us
  blocking collectives  84.2 us (83%)
  Pallas kernels  9.79 us (10%)
  local copies, waits for them, and re-layouts  5.42 us (5%)
    all_to_all x1, blocking collectives, shards(): held = lax.all_to_all(sent, 'ctx', split_axis=0, concat_axis=0, tiled=True)  43.1 us
    all_to_all x1, blocking collectives, shards(): lax.all_to_all(made, 'ctx', split_axis=0, concat_axis=0, tiled=True)  41 us
    pallas_call x1, Pallas kernels, shards(): pl.pallas_call(spectral_kernel, in_specs=[here] * 4, out_specs=here, out_...  7.49 us
    unnamed x22, local copies, waits for them, and re-layouts  5.42 us

profile of v1, /device:TPU:13, one launch (start us, length us, event | category | flops | bytes accessed | tf_op | source)
XLA Modules:
  0.0 100.1 jit_solution(9246165210319496602)
XLA Ops:
  0.6 0.0 copy-start
  0.6 1.0 %copy-done = bf16[2048,128]{1,0:T(8,128)(2,1)S(1)} copy-done((bf16[2048,128]{1,0:T(8,128)(2,1)S(1)}, bf16[2048,128]{1,0:T(8,128)(2,1)}, u32[]{:S(2)}) %copy-start) | copy-done | bytes 524312
  1.7 0.0 copy-start.2
  1.7 1.0 %copy-done.2 = bf16[2048,128]{1,0:T(8,128)(2,1)S(1)} copy-done((bf16[2048,128]{1,0:T(8,128)(2,1)S(1)}, bf16[2048,128]{1,0:T(8,128)(2,1)}, u32[]{:S(2)}) %copy-start.2) | copy-done | bytes 524312
  2.7 0.0 copy-start.4
  2.7 1.0 %copy-done.4 = bf16[2048,128]{1,0:T(8,128)(2,1)S(1)} copy-done((bf16[2048,128]{1,0:T(8,128)(2,1)S(1)}, bf16[2048,128]{1,0:T(8,128)(2,1)}, u32[]{:S(2)}) %copy-start.4) | copy-done | bytes 524312
  3.8 0.0 copy-start.6
  3.8 1.2 %copy-done.6 = f32[2048,128]{1,0:T(8,128)S(1)} copy-done((f32[2048,128]{1,0:T(8,128)S(1)}, f32[2048,128]{1,0:T(8,128)}, u32[]{:S(2)}) %copy-start.6) | copy-done | bytes 1048600
  5.0 0.0 copy-start.7
  5.0 1.0 %copy-done.7 = bf16[2048,128]{1,0:T(8,128)(2,1)S(1)} copy-done((bf16[2048,128]{1,0:T(8,128)(2,1)S(1)}, bf16[2048,128]{1,0:T(8,128)(2,1)}, u32[]{:S(2)}) %copy-start.7) | copy-done | bytes 524312
  6.0 0.3 shard_map.111
  6.4 0.0 copy-start.8
  6.4 0.0 copy-start.9
  6.4 0.0 copy-start.10
  6.4 43.1 %all_to_all.10.sig_ref = bf16[16,3,128,128]{3,2,1,0:T(8,128)(2,1)S(1)} all-to-all(bf16[16,3,128,128]{3,2,1,0:T(8,128)(2,1)S(1)} %shard_map.111), channel_id=1, replica_groups=mesh['groups'=2,'ctx'=16] {'ctx'}, dimensions={0} | all-to-all | bytes 3145728 | tf_op jit(solution)/shard_map/all_to_all | solution.py:159
  49.5 0.0 copy-done.8
  49.5 0.0 copy-done.9
  49.5 0.0 copy-done.10
  49.5 7.5 %shard_map.112 = bf16[16,3,128,128]{3,2,1,0:T(8,128)(2,1)S(1)} custom-call(bf16[16,3,128,128]{3,2,1,0:T(8,128)(2,1)S(1)} %all_to_all.10.sig_ref, f32[16,4,128]{2,1,0:T(4,128)S(1)} %copy-done.10, bf16[256,256]{1,0:T(8,128)(2,1)S(1)} %copy-done.9, bf16[256,256]{1,0:T(8,128)(2,1)S(1)} %copy-done.8), custom_call_target="tpu_custom_call" | custom-call | tf_op jit(solution)/shard_map/pallas_call | solution.py:160
  57.0 0.0 copy-start.1
  57.1 0.0 copy-start.3
  57.1 0.0 copy-start.5
  57.1 41.0 %all_to_all.11.part_ref = bf16[16,3,128,128]{3,2,1,0:T(8,128)(2,1)S(1)} all-to-all(bf16[16,3,128,128]{3,2,1,0:T(8,128)(2,1)S(1)} %shard_map.112), channel_id=1, replica_groups=mesh['groups'=2,'ctx'=16] {'ctx'}, dimensions={0} | all-to-all | bytes 3145728 | tf_op jit(solution)/shard_map/all_to_all | solution.py:168
  98.1 0.0 copy-done.1
  98.1 0.0 copy-done.3
  98.1 0.0 copy-done.5
  98.1 2.0 %shard_map.113 = (bf16[2048,128]{1,0:T(8,128)(2,1)}, bf16[2048,128]{1,0:T(8,128)(2,1)}, bf16[2048,128]{1,0:T(8,128)(2,1)}, f32[2048,128]{1,0:T(8,128)}) custom-call(bf16[16,3,128,128]{3,2,1,0:T(8,128)(2,1)S(1)} %all_to_all.11.part_ref, bf16[2048,128]{1,0:T(8,128)(2,1)S(1)} %copy-done.1, bf16[2048,128]{1,0:T(8,128)(2,1)S(1)} %copy-done.3, ...), custom_call_target="tpu_custom_call" | custom-call | tf_op jit(solution)/shard_map/pallas_call | solution.py:170
Async XLA Ops:
  0.6 1.0 %copy-start = (bf16[2048,128]{1,0:T(8,128)(2,1)S(1)}, bf16[2048,128]{1,0:T(8,128)(2,1)}, u32[]{:S(2)}) copy-start(bf16[2048,128]{1,0:T(8,128)(2,1)} %value_ref.3) | copy-start | bytes 1572868
  1.7 1.0 %copy-start.2 = (bf16[2048,128]{1,0:T(8,128)(2,1)S(1)}, bf16[2048,128]{1,0:T(8,128)(2,1)}, u32[]{:S(2)}) copy-start(bf16[2048,128]{1,0:T(8,128)(2,1)} %key_ref.3) | copy-start | bytes 1572868
  2.7 1.0 %copy-start.4 = (bf16[2048,128]{1,0:T(8,128)(2,1)S(1)}, bf16[2048,128]{1,0:T(8,128)(2,1)}, u32[]{:S(2)}) copy-start(bf16[2048,128]{1,0:T(8,128)(2,1)} %cot_ref.3) | copy-start | bytes 1572868
  3.8 1.2 %copy-start.6 = (f32[2048,128]{1,0:T(8,128)S(1)}, f32[2048,128]{1,0:T(8,128)}, u32[]{:S(2)}) copy-start(f32[2048,128]{1,0:T(8,128)} %filter_ref.1) | copy-start | bytes 3145732
  5.0 1.0 %copy-start.7 = (bf16[2048,128]{1,0:T(8,128)(2,1)S(1)}, bf16[2048,128]{1,0:T(8,128)(2,1)}, u32[]{:S(2)}) copy-start(bf16[2048,128]{1,0:T(8,128)(2,1)} %query_ref.1) | copy-start | bytes 1572868
  6.4 43.2 %copy-start.8 = (bf16[256,256]{1,0:T(8,128)(2,1)S(1)}, bf16[256,256]{1,0:T(8,128)(2,1)}, u32[]{:S(2)}) copy-start(bf16[256,256]{1,0:T(8,128)(2,1)} %constant.7.clone.back_ref) | copy-start | bytes 393220
  6.4 43.2 %copy-start.9 = (bf16[256,256]{1,0:T(8,128)(2,1)S(1)}, bf16[256,256]{1,0:T(8,128)(2,1)}, u32[]{:S(2)}) copy-start(bf16[256,256]{1,0:T(8,128)(2,1)} %constant.6.clone.ahead_ref) | copy-start | bytes 393220
  6.4 43.2 %copy-start.10 = (f32[16,4,128]{2,1,0:T(4,128)S(1)}, f32[16,4,128]{2,1,0:T(4,128)}, u32[]{:S(2)}) copy-start(f32[16,4,128]{2,1,0:T(4,128)} %constant.8.clone.twist_ref) | copy-start | bytes 98308
  57.0 41.1 %copy-start.1 = (bf16[2048,128]{1,0:T(8,128)(2,1)S(1)}, bf16[2048,128]{1,0:T(8,128)(2,1)}, u32[]{:S(2)}) copy-start(bf16[2048,128]{1,0:T(8,128)(2,1)} %value_ref.3) | copy-start | bytes 1572868
  57.1 41.1 %copy-start.3 = (bf16[2048,128]{1,0:T(8,128)(2,1)S(1)}, bf16[2048,128]{1,0:T(8,128)(2,1)}, u32[]{:S(2)}) copy-start(bf16[2048,128]{1,0:T(8,128)(2,1)} %key_ref.3) | copy-start | bytes 1572868
  57.1 41.1 %copy-start.5 = (bf16[2048,128]{1,0:T(8,128)(2,1)S(1)}, bf16[2048,128]{1,0:T(8,128)(2,1)}, u32[]{:S(2)}) copy-start(bf16[2048,128]{1,0:T(8,128)(2,1)} %cot_ref.3) | copy-start | bytes 1572868

commit v2 on v1

--- a/solution.py
+++ b/solution.py
@@ -72,56 +72,89 @@
     return twist, jnp.asarray(ahead, jnp.bfloat16), jnp.asarray(ahead.T, jnp.bfloat16)
 
 
-def gate_kernel(value_ref, key_ref, query_ref, cot_ref, filter_ref, out_ref):
+def gate_kernel(value_ref, key_ref, query_ref, cot_ref, out_ref):
     blocks, _, chunk, width = out_ref.shape
     shape = (blocks, chunk, width)
     mixed = value_ref[...].astype(jnp.float32) * key_ref[...].astype(jnp.float32)
     grad = cot_ref[...].astype(jnp.float32) * query_ref[...].astype(jnp.float32)
     out_ref[:, 0] = mixed.astype(jnp.bfloat16).reshape(shape)
     out_ref[:, 1] = grad.astype(jnp.bfloat16).reshape(shape)
-    out_ref[:, 2] = filter_ref[...].astype(jnp.bfloat16).reshape(shape)
-
-
-def spectral_kernel(sig_ref, twist_ref, ahead_ref, back_ref, out_ref, turned_ref):
-    shards, _, chunk, width = sig_ref.shape
+
+
+def transform(points, twist_ref, ahead_ref, turned_ref):
+    tile, width = points[0].shape
+    points = [(point.astype(jnp.float32), None) for point in points]
+    for k, (re, im) in enumerate(evaluate(points, math.pi / 2)):
+        c, s = twist_ref[k, 0:1, :], twist_ref[k, 1:2, :]
+        rows = slice(k * tile, (k + 1) * tile)
+        turned_ref[rows, :width] = (re * c + im * s).astype(jnp.bfloat16)
+        turned_ref[rows, width:] = (im * c - re * s).astype(jnp.bfloat16)
+    return jnp.dot(turned_ref[...], ahead_ref[...], preferred_element_type=jnp.float32)
+
+
+def inverse(re, im, twist_ref, back_ref):
+    count, _, width = twist_ref.shape
+    tile = re.shape[0] // count
+    both = jnp.concatenate([re.astype(jnp.bfloat16), im.astype(jnp.bfloat16)], axis=1)
+    back = jnp.dot(both, back_ref[...], preferred_element_type=jnp.float32)
+    values = []
+    for k in range(count):
+        rows = slice(k * tile, (k + 1) * tile)
+        re, im = back[rows, :width], back[rows, width:]
+        c, s = twist_ref[k, 2:3, :], twist_ref[k, 3:4, :]
+        values.append((re * c - im * s, re * s + im * c))
+    return interpolate(values, math.pi / 2)
+
+
+def filter_kernel(mine_ref, other_ref, twist_ref, ahead_ref, spec_ref, turned_ref):
+    near, far, rows, _ = mine_ref.shape
+    me, side = lax.axis_index("ctx"), lax.axis_index("groups")
+
+    def piece(share_ref, b, lanes):
+        return share_ref[(me % near) ^ (b % near), (me // near) ^ (b // near), lanes]
+
+    def points(first, lanes):
+        return [
+            jnp.where(side == first, piece(mine_ref, b, lanes), piece(other_ref, b, lanes))
+            for b in range(near * far)
+        ]
+
+    if rows < TILE:
+        parts = zip(*[points(half, slice(None)) for half in range(2)])
+        joined = [jnp.concatenate([p.astype(jnp.float32) for p in pair]) for pair in parts]
+        spec_ref[0] = transform(joined, twist_ref, ahead_ref, turned_ref)
+    else:
+        for half in range(2):
+
+            @pl.loop(0, rows // TILE)
+            def _(step):
+                lanes = pl.ds(pl.multiple_of(step * TILE, TILE), TILE)
+                spec_ref[half * (rows // TILE) + step] = transform(
+                    points(half, lanes), twist_ref, ahead_ref, turned_ref
+                )
+
+
+def spectral_kernel(sig_ref, spec_ref, twist_ref, ahead_ref, back_ref, out_ref, turned_ref):
+    count, _, chunk, width = sig_ref.shape
 
     @pl.loop(0, chunk // TILE)
     def _(step):
         lanes = pl.ds(pl.multiple_of(step * TILE, TILE), TILE)
-        spectral_tile(
-            sig_ref.at[:, :, lanes], twist_ref, ahead_ref, back_ref, out_ref.at[:, :, lanes], turned_ref
+        specs = []
+        for which in range(2):
+            points = [sig_ref[b, which, lanes] for b in range(count)]
+            spec = transform(points, twist_ref, ahead_ref, turned_ref.at[which])
+            specs.append((spec[:, :width], spec[:, width:]))
+        (m_re, m_im), (g_re, g_im) = specs
+        f_re, f_im = spec_ref[step, :, :width], spec_ref[step, :, width:]
+        results = (
+            (f_re * m_re - f_im * m_im, f_re * m_im + f_im * m_re),
+            (f_re * g_re + f_im * g_im, f_re * g_im - f_im * g_re),
+            (g_re * m_re + g_im * m_im, g_im * m_re - g_re * m_im),
         )
-
-
-def spectral_tile(sig_ref, twist_ref, ahead_ref, back_ref, out_ref, turned_ref):
-    shards, _, tile, width = sig_ref.shape
-    specs = []
-    for which in range(3):
-        points = [(sig_ref[b, which].astype(jnp.float32), None) for b in range(shards)]
-        for k, (re, im) in enumerate(evaluate(points, math.pi / 2)):
-            c, s = twist_ref[k, 0:1, :], twist_ref[k, 1:2, :]
-            rows = slice(k * tile, (k + 1) * tile)
-            turned_ref[which, rows, :width] = (re * c + im * s).astype(jnp.bfloat16)
-            turned_ref[which, rows, width:] = (im * c - re * s).astype(jnp.bfloat16)
-        spec = jnp.dot(turned_ref[which], ahead_ref[...], preferred_element_type=jnp.float32)
-        specs.append((spec[:, :width], spec[:, width:]))
-    (m_re, m_im), (g_re, g_im), (f_re, f_im) = specs
-    results = (
-        (f_re * m_re - f_im * m_im, f_re * m_im + f_im * m_re),
-        (f_re * g_re + f_im * g_im, f_re * g_im - f_im * g_re),
-        (g_re * m_re + g_im * m_im, g_im * m_re - g_re * m_im),
-    )
-    for which, (re, im) in enumerate(results):
-        both = jnp.concatenate([re.astype(jnp.bfloat16), im.astype(jnp.bfloat16)], axis=1)
-        back = jnp.dot(both, back_ref[...], preferred_element_type=jnp.float32)
-        values = []
-        for k in range(shards):
-            rows = slice(k * tile, (k + 1) * tile)
-            re, im = back[rows, :width], back[rows, width:]
-            c, s = twist_ref[k, 2:3, :], twist_ref[k, 3:4, :]
-            values.append((re * c - im * s, re * s + im * c))
-        for b, part in enumerate(interpolate(values, math.pi / 2)):
-            out_ref[b, which] = part.astype(jnp.bfloat16)
+        for which, (re, im) in enumerate(results):
+            for b, part in enumerate(inverse(re, im, twist_ref, back_ref)):
+                out_ref[b, which, lanes] = part.astype(jnp.bfloat16)
 
 
 def ungate_kernel(part_ref, value_ref, key_ref, cot_ref, gv_ref, gk_ref, gq_ref, gf_ref):
@@ -139,33 +172,77 @@
     gf_ref[...] = filt
 
 
+def exchange(parts):
+    return lax.all_to_all(parts, "ctx", split_axis=0, concat_axis=0, tiled=True)
+
+
+def swap(block, axis, gap):
+    size = lax.axis_size(axis)
+    return lax.ppermute(block, axis, [(i, i ^ gap) for i in range(size)])
+
+
+def pick(blocks, where):
+    return lax.dynamic_index_in_dim(blocks, where, 0, keepdims=False)
+
+
+def far_filters(filters, far):
+    count, me, side = lax.axis_size("ctx"), lax.axis_index("ctx"), lax.axis_index("groups")
+    near = count // far
+    channels, width = filters.shape
+    share = filters.reshape(far, near, 2, channels // count // 2, width)
+    share = lax.dynamic_index_in_dim(share, side, 2, keepdims=False)
+    blocks = [pick(share, (me // near) ^ k).astype(jnp.bfloat16) for k in range(far)]
+    return blocks[:1] + [swap(blocks[k], "ctx", k * near) for k in range(1, far)]
+
+
+def near_filters(blocks):
+    me, near = lax.axis_index("ctx"), blocks[0].shape[0]
+    parts = [jnp.stack([pick(b, (me % near) ^ j) for b in blocks]) for j in range(near)]
+    mine = jnp.stack(parts[:1] + [swap(parts[j], "ctx", j) for j in range(1, near)])
+    return mine, swap(mine, "groups", 1)
+
+
 def shards(values, keys, queries, grad_out, filters):
     count = lax.axis_size("ctx")
     channels, width = values.shape
     chunk = channels // count
     twist, ahead, back = make_tables(count, width)
     rows = pl.BlockSpec((channels // STEPS, width), lambda i: (i, 0))
-    packed = pl.BlockSpec((count // STEPS, 3, chunk, width), lambda i: (i, 0, 0, 0))
     here = pl.BlockSpec(memory_space=pltpu.VMEM)
     limit = pltpu.CompilerParams(vmem_limit_bytes=48 * 1024 * 1024)
+    far = 1 << ((count.bit_length() - 1) // 2)
+    blocks = far_filters(filters, far)
     sent = pl.pallas_call(
         gate_kernel,
-        grid=(STEPS,),
-        in_specs=[rows] * 5,
-        out_specs=packed,
-        out_shape=jax.ShapeDtypeStruct((count, 3, chunk, width), jnp.bfloat16),
-        compiler_params=limit,
-    )(values, keys, queries, grad_out, filters)
-    held = lax.all_to_all(sent, "ctx", split_axis=0, concat_axis=0, tiled=True)
+        in_specs=[here] * 4,
+        out_specs=here,
+        out_shape=jax.ShapeDtypeStruct((count, 2, chunk, width), jnp.bfloat16),
+        compiler_params=limit,
+    )(values, keys, queries, grad_out)
+    blocks, sent = lax.optimization_barrier((blocks, sent))
+    held = exchange(sent)
+    mine, other = near_filters(blocks)
+    tall = count * TILE
+    spec = pl.pallas_call(
+        filter_kernel,
+        in_specs=[here] * 4,
+        out_specs=here,
+        out_shape=jax.ShapeDtypeStruct((chunk // TILE, tall, 2 * width), jnp.float32),
+        scratch_shapes=[pltpu.VMEM((tall, 2 * width), jnp.bfloat16)],
+        compiler_params=limit,
+        cost_estimate=pl.CostEstimate(
+            flops=8 * count * chunk * width * width, bytes_accessed=2**20, transcendentals=0
+        ),
+    )(mine, other, twist, ahead)
     made = pl.pallas_call(
         spectral_kernel,
-        in_specs=[here] * 4,
+        in_specs=[here] * 5,
         out_specs=here,
         out_shape=jax.ShapeDtypeStruct((count, 3, chunk, width), jnp.bfloat16),
-        scratch_shapes=[pltpu.VMEM((3, count * TILE, 2 * width), jnp.bfloat16)],
-        compiler_params=limit,
-    )(held, twist, ahead, back)
-    returned = lax.all_to_all(made, "ctx", split_axis=0, concat_axis=0, tiled=True)
+        scratch_shapes=[pltpu.VMEM((2, tall, 2 * width), jnp.bfloat16)],
+        compiler_params=limit,
+    )(held, spec, twist, ahead, back)
+    returned = exchange(made)
     half = jax.ShapeDtypeStruct((channels, width), jnp.bfloat16)
     return pl.pallas_call(
         ungate_kernel,

time: 101 us -> 93.9 us (0.930)
  blocking collectives: 84.2 us -> 41.6 us
  waiting for transfers between devices: 0 us -> 19.7 us
  starting transfers between devices: 0 us -> 13.8 us
  Pallas kernels: 9.79 us -> 11.5 us
    all_to_all x2 -> x1, blocking collectives: 84.2 us -> 41.6 us  [exchange(): return lax.all_to_all(parts, 'ctx', split_axis=0, concat_axis=0, tiled=True)]
    ppermute x0 -> x7, waiting for transfers between devices: none -> 15.7 us  [swap(): return lax.ppermute(block, axis, [(i, i ^ gap) for i in range(size)])]
    all_to_all x0 -> x1, starting transfers between devices: none -> 7.62 us  [exchange(): return lax.all_to_all(parts, 'ctx', split_axis=0, concat_axis=0, tiled=True)]
    ppermute x0 -> x7, starting transfers between devices: none -> 6.2 us  [swap(): return lax.ppermute(block, axis, [(i, i ^ gap) for i in range(size)])]
    all_to_all x0 -> x1, waiting for transfers between devices: none -> 4.05 us  [exchange(): return lax.all_to_all(parts, 'ctx', split_axis=0, concat_axis=0, tiled=True)]
    pallas_call x2 -> x3, Pallas kernels: 7.82 us -> 9.57 us  [the longest x1 6.03 us: shards(): pl.pallas_call(spectral_kernel, in_specs=[here] * 5, out_specs=here, out_...]
    unnamed x22 -> x20, local copies, waits for them, and re-layouts: 5.42 us -> 4.2 us
    convert_element_type x0 -> x1, local copies, waits for them, and re-layouts: none -> 1.15 us  [far_filters(): pick(share, me // near ^ k).astype(jnp.bfloat16)]
  transfers between devices with their start and end apart: 0 -> 8, of which waited for: 0 -> 4; matrix products, arithmetic and copies ran while one was open for 0% -> 0% of each run, Pallas kernels for 0% -> 4%
where the time goes in v2:
time: 93.9 us; the launch traced here: 92.9 us
  blocking collectives  41.6 us (44%)
  waiting for transfers between devices  19.7 us (21%)
  starting transfers between devices  13.8 us (15%)
  Pallas kernels  11.5 us (12%)
  local copies, waits for them, and re-layouts  5.39 us (6%)
    all_to_all x1, blocking collectives, exchange(): return lax.all_to_all(parts, 'ctx', split_axis=0, concat_axis=0, tiled=True)  41.6 us
    ppermute x7, waiting for transfers between devices, swap(): return lax.ppermute(block, axis, [(i, i ^ gap) for i in range(size)])  15.7 us
    all_to_all x1, starting transfers between devices, exchange(): return lax.all_to_all(parts, 'ctx', split_axis=0, concat_axis=0, tiled=True)  7.62 us
    ppermute x7, starting transfers between devices, swap(): return lax.ppermute(block, axis, [(i, i ^ gap) for i in range(size)])  6.2 us
    pallas_call x1, Pallas kernels, shards(): pl.pallas_call(spectral_kernel, in_specs=[here] * 5, out_specs=here, out_...  6.03 us
    unnamed x20, local copies, waits for them, and re-layouts  4.2 us
    all_to_all x1, waiting for transfers between devices, exchange(): return lax.all_to_all(parts, 'ctx', split_axis=0, concat_axis=0, tiled=True)  4.05 us
    pallas_call x1, Pallas kernels, shards(): pl.pallas_call(filter_kernel, in_specs=[here] * 4, out_specs=here, out_sh...  2.33 us
  transfers between devices with their start and end apart: 8, of which 4 were waited for; matrix products, arithmetic and copies ran while one was open for 0% of the time, Pallas kernels for 4%

profile of v2, /device:TPU:13, one launch (start us, length us, event | category | flops | bytes accessed | tf_op | source)
XLA Modules:
  0.0 92.9 jit_solution(890260500721158872)
XLA Ops:
  0.7 1.2 %fusion.3 = (bf16[4,64,128]{2,1,0:T(8,128)(2,1)S(1)}, bf16[4,64,128]{2,1,0:T(8,128)(2,1)S(1)}, bf16[4,64,128]{2,1,0:T(8,128)(2,1)S(1)}, bf16[4,64,128]{2,1,0:T(8,128)(2,1)S(1)}) fusion(f32[4,4,2,64,128]{4,3,2,1,0:T(8,128)} %bitcast.30, s32[]{:T(128)S(6)} %select_n.106, s32[]{:T(128)S(6)} %select_n.100, s32[]{:T(128)S(6)} %select_n.104, s32[]{:T(128)S(6)} %select_n.102, ...), kind=kLoop, calls=%fused_computation.8 | loop fusion | bytes 524308 | tf_op jit(solution)/shard_map/convert_element_type | solution.py:194
  1.8 1.4 %collective-permute-start.2 = (bf16[4,64,128]{2,1,0:T(8,128)(2,1)S(1)}, bf16[4,64,128]{2,1,0:T(8,128)(2,1)S(1)}, u32[]{:S(2)}, u32[]{:S(2)}) collective-permute-start(bf16[4,64,128]{2,1,0:T(8,128)(2,1)S(1)} %get-tuple-element.14), channel_id=1, source_target_pairs={{0,12},{1,13},{2,14},{3,15},{4,8},{5,9},{6,10},{7,11},{8,4},{9,5},... | collective-permute-start | bytes 196616 | tf_op jit(solution)/shard_map/ppermute | solution.py:181
  3.2 1.1 %collective-permute-start.1 = (bf16[4,64,128]{2,1,0:T(8,128)(2,1)S(1)}, bf16[4,64,128]{2,1,0:T(8,128)(2,1)S(1)}, u32[]{:S(2)}, u32[]{:S(2)}) collective-permute-start(bf16[4,64,128]{2,1,0:T(8,128)(2,1)S(1)} %get-tuple-element.15), channel_id=1, source_target_pairs={{0,8},{1,9},{2,10},{3,11},{4,12},{5,13},{6,14},{7,15},{8,0},{9,1},... | collective-permute-start | bytes 196616 | tf_op jit(solution)/shard_map/ppermute | solution.py:181
  4.3 1.1 %collective-permute-start = (bf16[4,64,128]{2,1,0:T(8,128)(2,1)S(1)}, bf16[4,64,128]{2,1,0:T(8,128)(2,1)S(1)}, u32[]{:S(2)}, u32[]{:S(2)}) collective-permute-start(bf16[4,64,128]{2,1,0:T(8,128)(2,1)S(1)} %get-tuple-element.16), channel_id=1, source_target_pairs={{0,4},{1,5},{2,6},{3,7},{4,0},{5,1},{6,2},{7,3},{8,12},{9,13},{10,... | collective-permute-start | bytes 196616 | tf_op jit(solution)/shard_map/ppermute | solution.py:181
  5.4 1.0 %copy-done = bf16[2048,128]{1,0:T(8,128)(2,1)S(1)} copy-done((bf16[2048,128]{1,0:T(8,128)(2,1)S(1)}, bf16[2048,128]{1,0:T(8,128)(2,1)}, u32[]{:S(2)}) %copy-start) | copy-done | bytes 524312
  6.4 1.0 %copy-done.2 = bf16[2048,128]{1,0:T(8,128)(2,1)S(1)} copy-done((bf16[2048,128]{1,0:T(8,128)(2,1)S(1)}, bf16[2048,128]{1,0:T(8,128)(2,1)}, u32[]{:S(2)}) %copy-start.2) | copy-done | bytes 524312
  7.5 1.0 %copy-done.4 = bf16[2048,128]{1,0:T(8,128)(2,1)S(1)} copy-done((bf16[2048,128]{1,0:T(8,128)(2,1)S(1)}, bf16[2048,128]{1,0:T(8,128)(2,1)}, u32[]{:S(2)}) %copy-start.4) | copy-done | bytes 524312
  8.5 1.0 %copy-done.7 = bf16[2048,128]{1,0:T(8,128)(2,1)S(1)} copy-done((bf16[2048,128]{1,0:T(8,128)(2,1)S(1)}, bf16[2048,128]{1,0:T(8,128)(2,1)}, u32[]{:S(2)}) %copy-start.7) | copy-done | bytes 524312
  9.6 1.2 %shard_map.111 = bf16[16,2,128,128]{3,2,1,0:T(8,128)(2,1)} custom-call(bf16[2048,128]{1,0:T(8,128)(2,1)S(1)} %copy-done, bf16[2048,128]{1,0:T(8,128)(2,1)S(1)} %copy-done.2, bf16[2048,128]{1,0:T(8,128)(2,1)S(1)} %copy-done.7, bf16[2048,128]{1,0:T(8,128)(2,1)S(1)} %copy-done.4), custom_call_target="tpu_custom_call" | custom-call | tf_op jit(solution)/shard_map/pallas_call | solution.py:215
  10.8 0.0 collective-permute-done.2
  10.8 0.0 collective-permute-done.1
  10.8 0.0 collective-permute-done
  10.8 0.0 copy-start.6
  10.8 0.0 copy-start.8
  10.8 7.6 %all-to-all-start = ((bf16[16,2,128,128]{3,2,1,0:T(8,128)(2,1)}), bf16[16,2,128,128]{3,2,1,0:T(8,128)(2,1)S(1)}, u32[]{:S(2)}, u32[]{:S(2)}) async-start(bf16[16,2,128,128]{3,2,1,0:T(8,128)(2,1)} %shard_map.111), calls=%async_computation | async-start | bytes 2097152 | tf_op jit(solution)/shard_map/all_to_all | solution.py:176
  18.5 0.4 collective-permute-start.3
  18.9 1.2 %collective-permute-start.4 = (bf16[4,64,128]{2,1,0:T(8,128)(2,1)S(1)}, bf16[4,64,128]{2,1,0:T(8,128)(2,1)S(1)}, u32[]{:S(2)}, u32[]{:S(2)}) collective-permute-start(bf16[4,64,128]{2,1,0:T(8,128)(2,1)S(1)} %pad_maximum_fusion.2), channel_id=1, source_target_pairs={{0,2},{1,3},{2,0},{3,1},{4,6},{5,7},{6,4},{7,5},{8,10},{9,11},{10,... | collective-permute-start | bytes 196616 | tf_op jit(solution)/shard_map/ppermute | solution.py:181
  20.2 0.7 collective-permute-start.5
  20.9 0.0 collective-permute-done.3
  20.9 5.2 %collective-permute-done.4 = bf16[4,64,128]{2,1,0:T(8,128)(2,1)S(1)} collective-permute-done((bf16[4,64,128]{2,1,0:T(8,128)(2,1)S(1)}, bf16[4,64,128]{2,1,0:T(8,128)(2,1)S(1)}, u32[]{:S(2)}, u32[]{:S(2)}) %collective-permute-start.4) | collective-permute-done | bytes 65568 | tf_op jit(solution)/shard_map/ppermute | solution.py:181
  26.1 2.4 %collective-permute-done.5 = bf16[4,64,128]{2,1,0:T(8,128)(2,1)S(1)} collective-permute-done((bf16[4,64,128]{2,1,0:T(8,128)(2,1)S(1)}, bf16[4,64,128]{2,1,0:T(8,128)(2,1)S(1)}, u32[]{:S(2)}, u32[]{:S(2)}) %collective-permute-start.5) | collective-permute-done | bytes 65568 | tf_op jit(solution)/shard_map/ppermute | solution.py:181
  28.6 0.3 collective-permute-start.6
  28.8 8.0 %collective-permute-done.6.other_ref = bf16[4,4,64,128]{3,2,1,0:T(8,128)(2,1)S(1)} collective-permute-done((bf16[4,4,64,128]{3,2,1,0:T(8,128)(2,1)S(1)}, bf16[4,4,64,128]{3,2,1,0:T(8,128)(2,1)S(1)}, u32[]{:S(2)}, u32[]{:S(2)}) %collective-permute-start.6) | collective-permute-done | bytes 262176 | tf_op jit(solution)/shard_map/ppermute | solution.py:181
  36.9 0.0 copy-done.8
  36.9 2.3 %shard_map.112.spec_ref = f32[8,256,256]{2,1,0:T(8,128)S(1)} custom-call(bf16[4,4,64,128]{3,2,1,0:T(8,128)(2,1)S(1)} %pad_maximum_fusion.mine_ref, bf16[4,4,64,128]{3,2,1,0:T(8,128)(2,1)S(1)} %collective-permute-done.6.other_ref, f32[16,4,128]{2,1,0:T(4,128)S(1)} %copy-done.8, bf16[256,256]{1,0:T(8,128)(2,1)S(1)} %copy-done.6), custom_call_target="tpu_custom_call" | custom-call | flops 268435456 | bytes 1048576 | tf_op jit(solution)/shard_map/pallas_call | solution.py:226
  39.2 4.0 %all-to-all-done.sig_ref = bf16[16,2,128,128]{3,2,1,0:T(8,128)(2,1)S(1)} async-done(((bf16[16,2,128,128]{3,2,1,0:T(8,128)(2,1)}), bf16[16,2,128,128]{3,2,1,0:T(8,128)(2,1)S(1)}, u32[]{:S(2)}, u32[]{:S(2)}) %all-to-all-start) | async-done | bytes 1048608 | tf_op jit(solution)/shard_map/all_to_all | solution.py:176
  43.3 6.0 %shard_map.113 = bf16[16,3,128,128]{3,2,1,0:T(8,128)(2,1)S(1)} custom-call(bf16[16,2,128,128]{3,2,1,0:T(8,128)(2,1)S(1)} %all-to-all-done.sig_ref, f32[8,256,256]{2,1,0:T(8,128)S(1)} %shard_map.112.spec_ref, f32[16,4,128]{2,1,0:T(4,128)S(1)} %copy-done.8, bf16[256,256]{1,0:T(8,128)(2,1)S(1)} %copy-done.6, bf16[256,256]{1,0:T(8,128)(2,1)S(1)} %copy-done.9), custom_call_target="tpu_custom_call" | custom-call | tf_op jit(solution)/shard_map/pallas_call | solution.py:237
  49.3 0.0 copy-start.1
  49.3 0.0 copy-start.3
  49.3 0.0 copy-start.5
  49.4 41.6 %all_to_all.10.part_ref = bf16[16,3,128,128]{3,2,1,0:T(8,128)(2,1)S(1)} all-to-all(bf16[16,3,128,128]{3,2,1,0:T(8,128)(2,1)S(1)} %shard_map.113), channel_id=1, replica_groups=mesh['groups'=2,'ctx'=16] {'ctx'}, dimensions={0} | all-to-all | bytes 3145728 | tf_op jit(solution)/shard_map/all_to_all | solution.py:176
  90.9 2.0 %shard_map.114 = (bf16[2048,128]{1,0:T(8,128)(2,1)}, bf16[2048,128]{1,0:T(8,128)(2,1)}, bf16[2048,128]{1,0:T(8,128)(2,1)}, f32[2048,128]{1,0:T(8,128)}) custom-call(bf16[16,3,128,128]{3,2,1,0:T(8,128)(2,1)S(1)} %all_to_all.10.part_ref, bf16[2048,128]{1,0:T(8,128)(2,1)S(1)} %copy-done.1, bf16[2048,128]{1,0:T(8,128)(2,1)S(1)} %copy-done.3, ...), custom_call_target="tpu_custom_call" | custom-call | tf_op jit(solution)/shard_map/pallas_call | solution.py:247
  (17 shorter events, 0.1 us)
Async XLA Ops:
  1.8 8.9 %collective-permute-start.2 = (bf16[4,64,128]{2,1,0:T(8,128)(2,1)S(1)}, bf16[4,64,128]{2,1,0:T(8,128)(2,1)S(1)}, u32[]{:S(2)}, u32[]{:S(2)}) collective-permute-start(bf16[4,64,128]{2,1,0:T(8,128)(2,1)S(1)} %get-tuple-element.14), channel_id=1, source_target_pairs={{0,12},{1,13},{2,14},{3,15},{4,8},{5,9},{6,10},{7,11},{8,4},{9,5},... | collective-permute-start | bytes 196616 | tf_op jit(solution)/shard_map/ppermute | solution.py:181
  3.2 7.6 %collective-permute-start.1 = (bf16[4,64,128]{2,1,0:T(8,128)(2,1)S(1)}, bf16[4,64,128]{2,1,0:T(8,128)(2,1)S(1)}, u32[]{:S(2)}, u32[]{:S(2)}) collective-permute-start(bf16[4,64,128]{2,1,0:T(8,128)(2,1)S(1)} %get-tuple-element.15), channel_id=1, source_target_pairs={{0,8},{1,9},{2,10},{3,11},{4,12},{5,13},{6,14},{7,15},{8,0},{9,1},... | collective-permute-start | bytes 196616 | tf_op jit(solution)/shard_map/ppermute | solution.py:181
  4.3 6.5 %collective-permute-start = (bf16[4,64,128]{2,1,0:T(8,128)(2,1)S(1)}, bf16[4,64,128]{2,1,0:T(8,128)(2,1)S(1)}, u32[]{:S(2)}, u32[]{:S(2)}) collective-permute-start(bf16[4,64,128]{2,1,0:T(8,128)(2,1)S(1)} %get-tuple-element.16), channel_id=1, source_target_pairs={{0,4},{1,5},{2,6},{3,7},{4,0},{5,1},{6,2},{7,3},{8,12},{9,13},{10,... | collective-permute-start | bytes 196616 | tf_op jit(solution)/shard_map/ppermute | solution.py:181
  5.4 1.0 %copy-start = (bf16[2048,128]{1,0:T(8,128)(2,1)S(1)}, bf16[2048,128]{1,0:T(8,128)(2,1)}, u32[]{:S(2)}) copy-start(bf16[2048,128]{1,0:T(8,128)(2,1)} %value_ref.3) | copy-start | bytes 1572868
  6.4 1.0 %copy-start.2 = (bf16[2048,128]{1,0:T(8,128)(2,1)S(1)}, bf16[2048,128]{1,0:T(8,128)(2,1)}, u32[]{:S(2)}) copy-start(bf16[2048,128]{1,0:T(8,128)(2,1)} %key_ref.3) | copy-start | bytes 1572868
  7.5 1.0 %copy-start.4 = (bf16[2048,128]{1,0:T(8,128)(2,1)S(1)}, bf16[2048,128]{1,0:T(8,128)(2,1)}, u32[]{:S(2)}) copy-start(bf16[2048,128]{1,0:T(8,128)(2,1)} %cot_ref.3) | copy-start | bytes 1572868
  8.5 1.0 %copy-start.7 = (bf16[2048,128]{1,0:T(8,128)(2,1)S(1)}, bf16[2048,128]{1,0:T(8,128)(2,1)}, u32[]{:S(2)}) copy-start(bf16[2048,128]{1,0:T(8,128)(2,1)} %query_ref.1) | copy-start | bytes 1572868
  10.8 26.1 %copy-start.6 = (bf16[256,256]{1,0:T(8,128)(2,1)S(1)}, bf16[256,256]{1,0:T(8,128)(2,1)}, u32[]{:S(2)}) copy-start(bf16[256,256]{1,0:T(8,128)(2,1)} %constant.224.clone.ahead_ref) | copy-start | bytes 393220
  10.8 26.1 %copy-start.8 = (f32[16,4,128]{2,1,0:T(4,128)S(1)}, f32[16,4,128]{2,1,0:T(4,128)}, u32[]{:S(2)}) copy-start(f32[16,4,128]{2,1,0:T(4,128)} %constant.226.clone.twist_ref) | copy-start | bytes 98308
  10.8 32.5 %all-to-all-start = ((bf16[16,2,128,128]{3,2,1,0:T(8,128)(2,1)}), bf16[16,2,128,128]{3,2,1,0:T(8,128)(2,1)S(1)}, u32[]{:S(2)}, u32[]{:S(2)}) async-start(bf16[16,2,128,128]{3,2,1,0:T(8,128)(2,1)} %shard_map.111), calls=%async_computation | async-start | bytes 2097152 | tf_op jit(solution)/shard_map/all_to_all | solution.py:176
  18.5 2.4 %collective-permute-start.3 = (bf16[4,64,128]{2,1,0:T(8,128)(2,1)S(1)}, bf16[4,64,128]{2,1,0:T(8,128)(2,1)S(1)}, u32[]{:S(2)}, u32[]{:S(2)}) collective-permute-start(bf16[4,64,128]{2,1,0:T(8,128)(2,1)S(1)} %pad_maximum_fusion.1), channel_id=1, source_target_pairs={{0,1},{1,0},{2,3},{3,2},{4,5},{5,4},{6,7},{7,6},{8,9},{9,8},{10,11... | collective-permute-start | bytes 196616 | tf_op jit(solution)/shard_map/ppermute | solution.py:181
  18.9 7.1 %collective-permute-start.4 = (bf16[4,64,128]{2,1,0:T(8,128)(2,1)S(1)}, bf16[4,64,128]{2,1,0:T(8,128)(2,1)S(1)}, u32[]{:S(2)}, u32[]{:S(2)}) collective-permute-start(bf16[4,64,128]{2,1,0:T(8,128)(2,1)S(1)} %pad_maximum_fusion.2), channel_id=1, source_target_pairs={{0,2},{1,3},{2,0},{3,1},{4,6},{5,7},{6,4},{7,5},{8,10},{9,11},{10,... | collective-permute-start | bytes 196616 | tf_op jit(solution)/shard_map/ppermute | solution.py:181
  20.2 8.3 %collective-permute-start.5 = (bf16[4,64,128]{2,1,0:T(8,128)(2,1)S(1)}, bf16[4,64,128]{2,1,0:T(8,128)(2,1)S(1)}, u32[]{:S(2)}, u32[]{:S(2)}) collective-permute-start(bf16[4,64,128]{2,1,0:T(8,128)(2,1)S(1)} %pad_maximum_fusion.3), channel_id=1, source_target_pairs={{0,3},{1,2},{2,1},{3,0},{4,7},{5,6},{6,5},{7,4},{8,11},{9,10},{10,... | collective-permute-start | bytes 196616 | tf_op jit(solution)/shard_map/ppermute | solution.py:181
  28.5 14.8 %copy-start.9 = (bf16[256,256]{1,0:T(8,128)(2,1)S(1)}, bf16[256,256]{1,0:T(8,128)(2,1)}, u32[]{:S(2)}) copy-start(bf16[256,256]{1,0:T(8,128)(2,1)} %constant.225.clone.back_ref) | copy-start | bytes 393220
  28.6 8.3 %collective-permute-start.6 = (bf16[4,4,64,128]{3,2,1,0:T(8,128)(2,1)S(1)}, bf16[4,4,64,128]{3,2,1,0:T(8,128)(2,1)S(1)}, u32[]{:S(2)}, u32[]{:S(2)}) collective-permute-start(bf16[4,4,64,128]{3,2,1,0:T(8,128)(2,1)S(1)} %pad_maximum_fusion.mine_ref), channel_id=1, source_target_pairs={{0,16},{16,0},{1,17},{17,1},{2,18},{18,2},{3,19},{19,3},{4,20},{20... | collective-permute-start | bytes 786440 | tf_op jit(solution)/shard_map/ppermute | solution.py:181
  49.3 41.6 %copy-start.1 = (bf16[2048,128]{1,0:T(8,128)(2,1)S(1)}, bf16[2048,128]{1,0:T(8,128)(2,1)}, u32[]{:S(2)}) copy-start(bf16[2048,128]{1,0:T(8,128)(2,1)} %value_ref.3) | copy-start | bytes 1572868
  49.3 41.6 %copy-start.3 = (bf16[2048,128]{1,0:T(8,128)(2,1)S(1)}, bf16[2048,128]{1,0:T(8,128)(2,1)}, u32[]{:S(2)}) copy-start(bf16[2048,128]{1,0:T(8,128)(2,1)} %key_ref.3) | copy-start | bytes 1572868
  49.3 41.6 %copy-start.5 = (bf16[2048,128]{1,0:T(8,128)(2,1)S(1)}, bf16[2048,128]{1,0:T(8,128)(2,1)}, u32[]{:S(2)}) copy-start(bf16[2048,128]{1,0:T(8,128)(2,1)} %cot_ref.3) | copy-start | bytes 1572868

commit v3 on v2

v3 whole, which is shorter than its diff:
```python
import math

import jax
import jax.numpy as jnp
import numpy as np
from jax import lax
from jax.experimental import pallas as pl
from jax.experimental.pallas import tpu as pltpu
from jax.sharding import PartitionSpec as P

TILE = 32
STEPS = 4


def evaluate(points, theta):
    count = len(points)
    if count == 1:
        return [(theta, *points[0])]
    half, phi = count // 2, theta / 2
    c, s = math.cos(phi), math.sin(phi)
    first, second = [], []
    for (low_re, low_im), (high_re, high_im) in zip(points[:half], points[half:]):
        if theta == math.pi / 2:
            turned_re, turned_im = (high_re + high_im) * c, (high_im - high_re) * c
        else:
            turned_re, turned_im = high_re * c + high_im * s, high_im * c - high_re * s
        first.append((low_re + turned_re, low_im + turned_im))
        second.append((low_re - turned_re, low_im - turned_im))
    return evaluate(first, phi) + evaluate(second, phi + math.pi)


def interpolate(values, theta):
    count = len(values)
    if count == 1:
        return values
    half, phi = count // 2, theta / 2
    c, s = math.cos(phi), math.sin(phi)
    first = interpolate(values[:half], phi)
    second = interpolate(values[half:], phi + math.pi)
    low, high = [], []
    for (a_re, a_im), (b_re, b_im) in zip(first, second):
        gap_re, gap_im = a_re - b_re, a_im - b_im
        low.append((a_re + b_re, a_im + b_im))
        if theta == math.pi / 2:
            high.append(((gap_re - gap_im) * c, (gap_re + gap_im) * c))
        else:
            high.append((gap_re * c - gap_im * s, gap_re * s + gap_im * c))
    return low + high


def odd_values(points):
    half = len(points) // 2
    return evaluate([(low, -high) for low, high in zip(points[:half], points[half:])], math.pi / 2)


def odd_points(values):
    turned = interpolate(values, math.pi / 2)
    return [re for re, _ in turned] + [-im for _, im in turned]


def even_values(points):
    if len(points) == 2:
        return [points[0] + points[1], points[0] - points[1]]
    half = len(points) // 2
    pairs = list(zip(points[:half], points[half:]))
    return even_values([a + b for a, b in pairs]) + odd_values([a - b for a, b in pairs])


def even_points(values, count):
    if count == 2:
        return [values[0] + values[1], values[0] - values[1]]
    split = count // 4 + 1
    even, odd = even_points(values[:split], count // 2), odd_points(values[split:])
    return [a + b for a, b in zip(even, odd)] + [a - b for a, b in zip(even, odd)]


def short_values(points):
    return even_values(points) + odd_values(points)


def short_points(values, count):
    split = count // 2 + 1
    even, odd = even_points(values[:split], count), odd_points(values[split:])
    return [a + b for a, b in zip(even, odd)]


def short_angles(count):
    zero = [(0.0, 0.0)] * count
    odd = lambda n: [angle for angle, *_ in evaluate(zero[: n // 2], math.pi / 2)]
    sizes, even = [count], count
    while even > 2:
        even //= 2
        sizes.append(even)
    return [0.0, math.pi] + sum((odd(n) for n in reversed(sizes)), [])


def make_tables(count, width):
    angles = np.array(short_angles(count))
    turn = np.outer(angles, np.arange(width)) / width
    scale = np.where(np.arange(len(angles)) < 2, 1.0, 2.0)[:, None] / (2 * count * width)
    twist = np.stack(
        [np.cos(turn), np.sin(turn), np.cos(turn) * scale, np.sin(turn) * scale], axis=1
    ).astype(np.float32)
    wave = np.outer(np.arange(width), np.arange(width)) % width * (2 * math.pi / width)
    c, s = np.cos(wave), np.sin(wave)
    ahead = np.block([[c, -s], [s, c]])
    return twist, jnp.asarray(np.stack([ahead, ahead.T]), jnp.bfloat16)


def gate_kernel(value_hbm, key_hbm, cot_hbm, query_hbm, out_hbm, *scratch):
    blocks, _, chunk, width = out_hbm.shape
    sources = (value_hbm, key_hbm, cot_hbm, query_hbm)
    *held, made, loads, stores = scratch
    span, some = blocks * chunk // STEPS, blocks // STEPS
    copies = []
    for step in range(STEPS):
        rows = pl.ds(step * span, span)
        copies.append(
            [
                pltpu.make_async_copy(source.at[rows], to.at[rows], loads.at[i, step])
                for i, (source, to) in enumerate(zip(sources, held))
            ]
        )
        for copy in copies[-1]:
            copy.start()
    sends = []
    for step in range(STEPS):
        for copy in copies[step]:
            copy.wait()
        rows, part = pl.ds(step * span, span), pl.ds(step * some, some)
        for which in range(2):
            left, right = held[2 * which][rows], held[2 * which + 1][rows]
            both = left.astype(jnp.float32) * right.astype(jnp.float32)
            made[part, which] = both.astype(jnp.bfloat16).reshape(some, chunk, width)
        sends.append(pltpu.make_async_copy(made.at[part], out_hbm.at[part], stores.at[step]))
        sends[-1].start()
    for send in sends:
        send.wait()


def transform(points, twist_ref, wave_ref, turned_ref):
    tile, width = points[0].shape
    points = [point.astype(jnp.float32) for point in points]
    for top in range(0, tile, 16):
        halves = []
        for start in (top, top + 8):
            done = []
            for k, value in enumerate(short_values([p[start : start + 8] for p in points])):
                c, s = twist_ref[k, 0:1, :], twist_ref[k, 1:2, :]
                if k == 0:
                    re, im = value, jnp.zeros_like(value)
                elif k == 1:
                    re, im = value * c, value * -s
                else:
                    _, re, im = value
                    re, im = re * c + im * s, im * c - re * s
                done.append((re, im))
            halves.append(done)
        for k, ((a_re, a_im), (b_re, b_im)) in enumerate(zip(*halves)):
            rows = slice(k * tile + top, k * tile + top + 16)
            turned_ref[rows, :width] = jnp.concatenate([a_re, b_re]).astype(jnp.bfloat16)
            turned_ref[rows, width:] = jnp.concatenate([a_im, b_im]).astype(jnp.bfloat16)
    return jnp.dot(turned_ref[...], wave_ref[0], preferred_element_type=jnp.float32)


def inverse(re, im, twist_ref, wave_ref):
    count, _, width = twist_ref.shape
    tile = re.shape[0] // count
    both = jnp.concatenate([re.astype(jnp.bfloat16), im.astype(jnp.bfloat16)], axis=1)
    back = jnp.dot(both, wave_ref[1], preferred_element_type=jnp.float32)
    parts = []
    for start in range(0, tile, 8):
        values = []
        for k in range(count):
            rows = slice(k * tile + start, k * tile + start + 8)
            re, im = back[rows, :width], back[rows, width:]
            c, s = twist_ref[k, 2:3, :], twist_ref[k, 3:4, :]
            if k == 0:
                values.append(re * c)
            elif k == 1:
                values.append(re * c - im * s)
            else:
                values.append((re * c - im * s, re * s + im * c))
        parts.append(short_points(values, count - 1))
    return [jnp.concatenate(part) for part in zip(*parts)]


def filter_kernel(mine_ref, other_ref, twist_ref, wave_ref, spec_ref, turned_ref):
    near, far, rows, _ = mine_ref.shape
    tile = spec_ref.shape[1] // twist_ref.shape[0]
    me, side = lax.axis_index("ctx"), lax.axis_index("groups")

    def piece(share_ref, b, lanes):
        return share_ref[(me % near) ^ (b % near), (me // near) ^ (b // near), lanes]

    def points(first, lanes):
        return [
            jnp.where(side == first, piece(mine_ref, b, lanes), piece(other_ref, b, lanes))
            for b in range(near * far)
        ]

    if rows < tile:
        parts = zip(*[points(half, slice(None)) for half in range(2)])
        joined = [jnp.concatenate([p.astype(jnp.float32) for p in pair]) for pair in parts]
        spec = transform(joined, twist_ref, wave_ref, turned_ref)
        spec_ref[0] = spec.astype(jnp.bfloat16)
    else:
        for half in range(2):

            @pl.loop(0, rows // tile)
            def _(step):
                lanes = pl.ds(pl.multiple_of(step * tile, tile), tile)
                spec = transform(points(half, lanes), twist_ref, wave_ref, turned_ref)
                spec_ref[half * (rows // tile) + step] = spec.astype(jnp.bfloat16)


def spectral_kernel(sig_ref, spec_ref, twist_ref, wave_ref, out_ref, turned_ref):
    count, _, chunk, width = sig_ref.shape
    tile = spec_ref.shape[1] // twist_ref.shape[0]

    @pl.loop(0, chunk // tile)
    def _(step):
        lanes = pl.ds(pl.multiple_of(step * tile, tile), tile)
        specs = []
        for which in range(2):
            points = [sig_ref[b, which, lanes] for b in range(count)]
            spec = transform(points, twist_ref, wave_ref, turned_ref.at[which])
            specs.append((spec[:, :width], spec[:, width:]))
        (m_re, m_im), (g_re, g_im) = specs
        spec = spec_ref[step].astype(jnp.float32)
        f_re, f_im = spec[:, :width], spec[:, width:]
        results = (
            (f_re * m_re - f_im * m_im, f_re * m_im + f_im * m_re),
            (f_re * g_re + f_im * g_im, f_re * g_im - f_im * g_re),
            (g_re * m_re + g_im * m_im, g_im * m_re - g_re * m_im),
        )
        for which, (re, im) in enumerate(results):
            for b, part in enumerate(inverse(re, im, twist_ref, wave_ref)):
                out_ref[b, which, lanes] = part.astype(jnp.bfloat16)


def ungate_kernel(part_ref, value_ref, key_ref, cot_ref, gv_hbm, gk_hbm, gq_hbm, gf_hbm, *scratch):
    blocks, _, chunk, width = part_ref.shape
    outs = (gv_hbm, gk_hbm, gq_hbm, gf_hbm)
    *made, sems = scratch
    span, some = blocks * chunk // STEPS, blocks // STEPS
    sends = []
    for step in range(STEPS):
        rows, part = pl.ds(step * span, span), pl.ds(step * some, some)
        conv, grad, filt = (
            part_ref[part, which].astype(jnp.float32).reshape(span, width) for which in range(3)
        )
        made[0][rows] = (grad * key_ref[rows].astype(jnp.float32)).astype(jnp.bfloat16)
        made[1][rows] = (grad * value_ref[rows].astype(jnp.float32)).astype(jnp.bfloat16)
        made[2][rows] = (cot_ref[rows].astype(jnp.float32) * conv).astype(jnp.bfloat16)
        made[3][rows] = filt
        for i, (source, to) in enumerate(zip(made, outs)):
            sends.append(pltpu.make_async_copy(source.at[rows], to.at[rows], sems.at[i, step]))
            sends[-1].start()
    for send in sends:
        send.wait()


def exchange(parts):
    return lax.all_to_all(parts, "ctx", split_axis=0, concat_axis=0, tiled=True)


def swap(block, axis, gap):
    size = lax.axis_size(axis)
    return lax.ppermute(block, axis, [(i, i ^ gap) for i in range(size)])


def pick(blocks, where):
    return lax.dynamic_index_in_dim(blocks, where, 0, keepdims=False)


def far_filters(filters, far):
    count, me, side = lax.axis_size("ctx"), lax.axis_index("ctx"), lax.axis_index("groups")
    near = count // far
    channels, width = filters.shape
    share = filters.reshape(far, near, 2, channels // count // 2, width)
    share = lax.dynamic_index_in_dim(share, side, 2, keepdims=False)
    blocks = [pick(share, (me // near) ^ k).astype(jnp.bfloat16) for k in range(far)]
    return blocks[:1] + [swap(blocks[k], "ctx", k * near) for k in range(1, far)]


def near_filters(blocks):
    me, near = lax.axis_index("ctx"), blocks[0].shape[0]
    parts = [jnp.stack([pick(b, (me % near) ^ j) for b in blocks]) for j in range(near)]
    mine = jnp.stack(parts[:1] + [swap(parts[j], "ctx", j) for j in range(1, near)])
    return mine, swap(mine, "groups", 1)


def shards(values, keys, queries, grad_out, filters):
    count = lax.axis_size("ctx")
    channels, width = values.shape
    chunk = channels // count
    twist, wave = make_tables(count, width)
    here = pl.BlockSpec(memory_space=pltpu.VMEM)
    limit = pltpu.CompilerParams(vmem_limit_bytes=24 * 1024 * 1024)
    far = 1 << ((count.bit_length() - 1) // 2)
    blocks = far_filters(filters, far)
    hbm = pl.BlockSpec(memory_space=pl.ANY)
    sent = pl.pallas_call(
        gate_kernel,
        in_specs=[hbm] * 4,
        out_specs=hbm,
        out_shape=jax.ShapeDtypeStruct((count, 2, chunk, width), jnp.bfloat16),
        scratch_shapes=[pltpu.VMEM((channels, width), jnp.bfloat16)] * 4
        + [
            pltpu.VMEM((count, 2, chunk, width), jnp.bfloat16),
            pltpu.SemaphoreType.DMA((4, STEPS)),
            pltpu.SemaphoreType.DMA((STEPS,)),
        ],
    )(values, keys, grad_out, queries)
    blocks, sent = lax.optimization_barrier((blocks, sent))
    held = exchange(sent)
    mine, other = near_filters(blocks)
    tile = min(TILE, chunk)
    tall = (count + 1) * tile
    spec = pl.pallas_call(
        filter_kernel,
        in_specs=[here] * 4,
        out_specs=here,
        out_shape=jax.ShapeDtypeStruct((chunk // tile, tall, 2 * width), jnp.bfloat16),
        scratch_shapes=[pltpu.VMEM((tall, 2 * width), jnp.bfloat16)],
        compiler_params=limit,
        cost_estimate=pl.CostEstimate(
            flops=8 * count * chunk * width * width, bytes_accessed=2**20, transcendentals=0
        ),
    )(mine, other, twist, wave)
    made = pl.pallas_call(
        spectral_kernel,
        in_specs=[here] * 4,
        out_specs=here,
        out_shape=jax.ShapeDtypeStruct((count, 3, chunk, width), jnp.bfloat16),
        scratch_shapes=[pltpu.VMEM((2, tall, 2 * width), jnp.bfloat16)],
        compiler_params=limit,
    )(held, spec, twist, wave)
    returned = exchange(made)
    half = jax.ShapeDtypeStruct((channels, width), jnp.bfloat16)
    wide = jax.ShapeDtypeStruct((channels, width), jnp.float32)
    return pl.pallas_call(
        ungate_kernel,
        in_specs=[here] * 4,
        out_specs=[hbm] * 4,
        out_shape=[half, half, half, wide],
        scratch_shapes=[pltpu.VMEM((channels, width), jnp.bfloat16)] * 3
        + [pltpu.VMEM((channels, width), jnp.float32), pltpu.SemaphoreType.DMA((4, STEPS))],
        compiler_params=limit,
    )(returned, values, keys, grad_out)


def solution(mesh):
    token = P(None, ("groups", "ctx"))
    return jax.shard_map(
        shards,
        mesh=mesh,
        in_specs=(token, token, token, token, P(None, "ctx")),
        out_specs=(token, token, token, token),
        check_vma=False,
    )
```

time: 93.9 us -> 90.9 us (0.968)
  local copies, waits for them, and re-layouts: 5.39 us -> 1.21 us
  waiting for transfers between devices: 19.7 us -> 22.2 us
    unnamed x20 -> x10, local copies, waits for them, and re-layouts: 4.2 us -> 0.03 us
    ppermute x7, waiting for transfers between devices: 15.7 us -> 17.2 us  [swap(): return lax.ppermute(block, axis, [(i, i ^ gap) for i in range(size)])]
  transfers between devices with their start and end apart: 8 -> 8, of which waited for: 4 -> 5; matrix products, arithmetic and copies ran while one was open for 0% -> 0% of each run, Pallas kernels for 4% -> 4%
where the time goes in v3:
time: 90.9 us; the launch traced here: 90 us
  blocking collectives  41.6 us (46%)
  waiting for transfers between devices  22.2 us (24%)
  starting transfers between devices  13.7 us (15%)
  Pallas kernels  10.6 us (12%)
  local copies, waits for them, and re-layouts  1.21 us (1%)
    all_to_all x1, blocking collectives, exchange(): return lax.all_to_all(parts, 'ctx', split_axis=0, concat_axis=0, tiled=True)  41.6 us
    ppermute x7, waiting for transfers between devices, swap(): return lax.ppermute(block, axis, [(i, i ^ gap) for i in range(size)])  17.2 us
    all_to_all x1, starting transfers between devices, exchange(): return lax.all_to_all(parts, 'ctx', split_axis=0, concat_axis=0, tiled=True)  7.46 us
    ppermute x7, starting transfers between devices, swap(): return lax.ppermute(block, axis, [(i, i ^ gap) for i in range(size)])  6.2 us
    pallas_call x1, Pallas kernels, shards(): pl.pallas_call(spectral_kernel, in_specs=[here] * 4, out_specs=here, out_...  5 us
    all_to_all x1, waiting for transfers between devices, exchange(): return lax.all_to_all(parts, 'ctx', split_axis=0, concat_axis=0, tiled=True)  4.96 us
    pallas_call x1, Pallas kernels, shards(): pl.pallas_call(gate_kernel, in_specs=[hbm] * 4, out_specs=hbm, out_shape=...  2.53 us
  transfers between devices with their start and end apart: 8, of which 5 were waited for; matrix products, arithmetic and copies ran while one was open for 0% of the time, Pallas kernels for 4%

profile of v3, /device:TPU:13, one launch (start us, length us, event | category | flops | bytes accessed | tf_op | source)
XLA Modules:
  0.0 90.0 jit_solution(8430509026189147924)
XLA Ops:
  0.7 1.1 %fusion.3 = (bf16[4,64,128]{2,1,0:T(8,128)(2,1)S(1)}, bf16[4,64,128]{2,1,0:T(8,128)(2,1)S(1)}, bf16[4,64,128]{2,1,0:T(8,128)(2,1)S(1)}, bf16[4,64,128]{2,1,0:T(8,128)(2,1)S(1)}) fusion(f32[4,4,2,64,128]{4,3,2,1,0:T(8,128)} %bitcast.30, s32[]{:T(128)S(6)} %select_n.106, s32[]{:T(128)S(6)} %select_n.100, s32[]{:T(128)S(6)} %select_n.104, s32[]{:T(128)S(6)} %select_n.102, ...), kind=kLoop, calls=%fused_computation.8 | loop fusion | bytes 524308 | tf_op jit(solution)/shard_map/convert_element_type | solution.py:283
  1.8 1.4 %collective-permute-start.2 = (bf16[4,64,128]{2,1,0:T(8,128)(2,1)S(1)}, bf16[4,64,128]{2,1,0:T(8,128)(2,1)S(1)}, u32[]{:S(2)}, u32[]{:S(2)}) collective-permute-start(bf16[4,64,128]{2,1,0:T(8,128)(2,1)S(1)} %get-tuple-element.14), channel_id=1, source_target_pairs={{0,12},{1,13},{2,14},{3,15},{4,8},{5,9},{6,10},{7,11},{8,4},{9,5},... | collective-permute-start | bytes 196616 | tf_op jit(solution)/shard_map/ppermute | solution.py:270
  3.2 1.1 %collective-permute-start.1 = (bf16[4,64,128]{2,1,0:T(8,128)(2,1)S(1)}, bf16[4,64,128]{2,1,0:T(8,128)(2,1)S(1)}, u32[]{:S(2)}, u32[]{:S(2)}) collective-permute-start(bf16[4,64,128]{2,1,0:T(8,128)(2,1)S(1)} %get-tuple-element.15), channel_id=1, source_target_pairs={{0,8},{1,9},{2,10},{3,11},{4,12},{5,13},{6,14},{7,15},{8,0},{9,1},... | collective-permute-start | bytes 196616 | tf_op jit(solution)/shard_map/ppermute | solution.py:270
  4.3 1.1 %collective-permute-start = (bf16[4,64,128]{2,1,0:T(8,128)(2,1)S(1)}, bf16[4,64,128]{2,1,0:T(8,128)(2,1)S(1)}, u32[]{:S(2)}, u32[]{:S(2)}) collective-permute-start(bf16[4,64,128]{2,1,0:T(8,128)(2,1)S(1)} %get-tuple-element.16), channel_id=1, source_target_pairs={{0,4},{1,5},{2,6},{3,7},{4,0},{5,1},{6,2},{7,3},{8,12},{9,13},{10,... | collective-permute-start | bytes 196616 | tf_op jit(solution)/shard_map/ppermute | solution.py:270
  5.4 2.5 %shard_map.102 = bf16[16,2,128,128]{3,2,1,0:T(8,128)(2,1)} custom-call(bf16[2048,128]{1,0:T(8,128)(2,1)} %value_ref.1, bf16[2048,128]{1,0:T(8,128)(2,1)} %key_ref.1, bf16[2048,128]{1,0:T(8,128)(2,1)} %cot_ref.1, bf16[2048,128]{1,0:T(8,128)(2,1)} %query_hbm.1), custom_call_target="tpu_custom_call" | custom-call | tf_op jit(solution)/shard_map/pallas_call | solution.py:304
  7.9 0.0 collective-permute-done.2
  7.9 0.0 collective-permute-done.1
  8.0 1.5 %collective-permute-done = bf16[4,64,128]{2,1,0:T(8,128)(2,1)S(1)} collective-permute-done((bf16[4,64,128]{2,1,0:T(8,128)(2,1)S(1)}, bf16[4,64,128]{2,1,0:T(8,128)(2,1)S(1)}, u32[]{:S(2)}, u32[]{:S(2)}) %collective-permute-start) | collective-permute-done | bytes 65568 | tf_op jit(solution)/shard_map/ppermute | solution.py:270
  9.5 0.0 copy-start.3
  9.5 0.0 copy-start.4
  9.5 7.5 %all-to-all-start = ((bf16[16,2,128,128]{3,2,1,0:T(8,128)(2,1)}), bf16[16,2,128,128]{3,2,1,0:T(8,128)(2,1)S(1)}, u32[]{:S(2)}, u32[]{:S(2)}) async-start(bf16[16,2,128,128]{3,2,1,0:T(8,128)(2,1)} %shard_map.102), calls=%async_computation | async-start | bytes 2097152 | tf_op jit(solution)/shard_map/all_to_all | solution.py:265
  17.0 0.4 collective-permute-start.3
  17.5 1.2 %collective-permute-start.4 = (bf16[4,64,128]{2,1,0:T(8,128)(2,1)S(1)}, bf16[4,64,128]{2,1,0:T(8,128)(2,1)S(1)}, u32[]{:S(2)}, u32[]{:S(2)}) collective-permute-start(bf16[4,64,128]{2,1,0:T(8,128)(2,1)S(1)} %pad_maximum_fusion.2), channel_id=1, source_target_pairs={{0,2},{1,3},{2,0},{3,1},{4,6},{5,7},{6,4},{7,5},{8,10},{9,11},{10,... | collective-permute-start | bytes 196616 | tf_op jit(solution)/shard_map/ppermute | solution.py:270
  18.7 0.7 collective-permute-start.5
  19.4 0.0 collective-permute-done.3
  19.4 5.2 %collective-permute-done.4 = bf16[4,64,128]{2,1,0:T(8,128)(2,1)S(1)} collective-permute-done((bf16[4,64,128]{2,1,0:T(8,128)(2,1)S(1)}, bf16[4,64,128]{2,1,0:T(8,128)(2,1)S(1)}, u32[]{:S(2)}, u32[]{:S(2)}) %collective-permute-start.4) | collective-permute-done | bytes 65568 | tf_op jit(solution)/shard_map/ppermute | solution.py:270
  24.6 2.4 %collective-permute-done.5 = bf16[4,64,128]{2,1,0:T(8,128)(2,1)S(1)} collective-permute-done((bf16[4,64,128]{2,1,0:T(8,128)(2,1)S(1)}, bf16[4,64,128]{2,1,0:T(8,128)(2,1)S(1)}, u32[]{:S(2)}, u32[]{:S(2)}) %collective-permute-start.5) | collective-permute-done | bytes 65568 | tf_op jit(solution)/shard_map/ppermute | solution.py:270
  27.1 0.3 collective-permute-start.6
  27.4 8.0 %collective-permute-done.6.other_ref = bf16[4,4,64,128]{3,2,1,0:T(8,128)(2,1)S(1)} collective-permute-done((bf16[4,4,64,128]{3,2,1,0:T(8,128)(2,1)S(1)}, bf16[4,4,64,128]{3,2,1,0:T(8,128)(2,1)S(1)}, u32[]{:S(2)}, u32[]{:S(2)}) %collective-permute-start.6) | collective-permute-done | bytes 262176 | tf_op jit(solution)/shard_map/ppermute | solution.py:270
  35.4 0.0 copy-done.3
  35.4 0.0 copy-done.4
  35.4 1.4 %shard_map.103.spec_ref = bf16[4,544,256]{2,1,0:T(8,128)(2,1)S(1)} custom-call(bf16[4,4,64,128]{3,2,1,0:T(8,128)(2,1)S(1)} %pad_maximum_fusion.mine_ref, bf16[4,4,64,128]{3,2,1,0:T(8,128)(2,1)S(1)} %collective-permute-done.6.other_ref, f32[17,4,128]{2,1,0:T(4,128)S(1)} %copy-done.4, bf16[2,256,256]{2,1,0:T(8,128)(2,1)S(1)} %copy-done.3), custom_call_target="tpu_custom_call" | custom-call | flops 268435456 | bytes 1048576 | tf_op jit(solution)/shard_map/pallas_call | solution.py:321
  36.8 5.0 %all-to-all-done.sig_ref = bf16[16,2,128,128]{3,2,1,0:T(8,128)(2,1)S(1)} async-done(((bf16[16,2,128,128]{3,2,1,0:T(8,128)(2,1)}), bf16[16,2,128,128]{3,2,1,0:T(8,128)(2,1)S(1)}, u32[]{:S(2)}, u32[]{:S(2)}) %all-to-all-start) | async-done | bytes 1048608 | tf_op jit(solution)/shard_map/all_to_all | solution.py:265
  41.8 5.0 %shard_map.104 = bf16[16,3,128,128]{3,2,1,0:T(8,128)(2,1)S(1)} custom-call(bf16[16,2,128,128]{3,2,1,0:T(8,128)(2,1)S(1)} %all-to-all-done.sig_ref, bf16[4,544,256]{2,1,0:T(8,128)(2,1)S(1)} %shard_map.103.spec_ref, f32[17,4,128]{2,1,0:T(4,128)S(1)} %copy-done.4, bf16[2,256,256]{2,1,0:T(8,128)(2,1)S(1)} %copy-done.3), custom_call_target="tpu_custom_call" | custom-call | tf_op jit(solution)/shard_map/pallas_call | solution.py:332
  46.8 0.0 copy-start
  46.8 0.0 copy-start.1
  46.8 0.0 copy-start.2
  46.8 41.6 %all_to_all.10.part_ref = bf16[16,3,128,128]{3,2,1,0:T(8,128)(2,1)S(1)} all-to-all(bf16[16,3,128,128]{3,2,1,0:T(8,128)(2,1)S(1)} %shard_map.104), channel_id=1, replica_groups=mesh['groups'=2,'ctx'=16] {'ctx'}, dimensions={0} | all-to-all | bytes 3145728 | tf_op jit(solution)/shard_map/all_to_all | solution.py:265
  88.4 0.0 copy-done
  88.4 0.0 copy-done.1
  88.4 0.0 copy-done.2
  88.4 1.6 %shard_map.105 = (bf16[2048,128]{1,0:T(8,128)(2,1)}, bf16[2048,128]{1,0:T(8,128)(2,1)}, bf16[2048,128]{1,0:T(8,128)(2,1)}, f32[2048,128]{1,0:T(8,128)}) custom-call(bf16[16,3,128,128]{3,2,1,0:T(8,128)(2,1)S(1)} %all_to_all.10.part_ref, bf16[2048,128]{1,0:T(8,128)(2,1)S(1)} %copy-done, bf16[2048,128]{1,0:T(8,128)(2,1)S(1)} %copy-done.1, ...), custom_call_target="tpu_custom_call" | custom-call | tf_op jit(solution)/shard_map/pallas_call | solution.py:343
  (7 shorter events, 0.1 us)
Async XLA Ops:
  1.8 6.1 %collective-permute-start.2 = (bf16[4,64,128]{2,1,0:T(8,128)(2,1)S(1)}, bf16[4,64,128]{2,1,0:T(8,128)(2,1)S(1)}, u32[]{:S(2)}, u32[]{:S(2)}) collective-permute-start(bf16[4,64,128]{2,1,0:T(8,128)(2,1)S(1)} %get-tuple-element.14), channel_id=1, source_target_pairs={{0,12},{1,13},{2,14},{3,15},{4,8},{5,9},{6,10},{7,11},{8,4},{9,5},... | collective-permute-start | bytes 196616 | tf_op jit(solution)/shard_map/ppermute | solution.py:270
  3.2 4.8 %collective-permute-start.1 = (bf16[4,64,128]{2,1,0:T(8,128)(2,1)S(1)}, bf16[4,64,128]{2,1,0:T(8,128)(2,1)S(1)}, u32[]{:S(2)}, u32[]{:S(2)}) collective-permute-start(bf16[4,64,128]{2,1,0:T(8,128)(2,1)S(1)} %get-tuple-element.15), channel_id=1, source_target_pairs={{0,8},{1,9},{2,10},{3,11},{4,12},{5,13},{6,14},{7,15},{8,0},{9,1},... | collective-permute-start | bytes 196616 | tf_op jit(solution)/shard_map/ppermute | solution.py:270
  4.3 5.2 %collective-permute-start = (bf16[4,64,128]{2,1,0:T(8,128)(2,1)S(1)}, bf16[4,64,128]{2,1,0:T(8,128)(2,1)S(1)}, u32[]{:S(2)}, u32[]{:S(2)}) collective-permute-start(bf16[4,64,128]{2,1,0:T(8,128)(2,1)S(1)} %get-tuple-element.16), channel_id=1, source_target_pairs={{0,4},{1,5},{2,6},{3,7},{4,0},{5,1},{6,2},{7,3},{8,12},{9,13},{10,... | collective-permute-start | bytes 196616 | tf_op jit(solution)/shard_map/ppermute | solution.py:270
  9.5 25.9 %copy-start.3 = (bf16[2,256,256]{2,1,0:T(8,128)(2,1)S(1)}, bf16[2,256,256]{2,1,0:T(8,128)(2,1)}, u32[]{:S(2)}) copy-start(bf16[2,256,256]{2,1,0:T(8,128)(2,1)} %constant.222.clone.wave_ref) | copy-start | bytes 786436
  9.5 25.9 %copy-start.4 = (f32[17,4,128]{2,1,0:T(4,128)S(1)}, f32[17,4,128]{2,1,0:T(4,128)}, u32[]{:S(2)}) copy-start(f32[17,4,128]{2,1,0:T(4,128)} %constant.223.clone.twist_ref) | copy-start | bytes 104452
  9.5 32.3 %all-to-all-start = ((bf16[16,2,128,128]{3,2,1,0:T(8,128)(2,1)}), bf16[16,2,128,128]{3,2,1,0:T(8,128)(2,1)S(1)}, u32[]{:S(2)}, u32[]{:S(2)}) async-start(bf16[16,2,128,128]{3,2,1,0:T(8,128)(2,1)} %shard_map.102), calls=%async_computation | async-start | bytes 2097152 | tf_op jit(solution)/shard_map/all_to_all | solution.py:265
  17.0 2.4 %collective-permute-start.3 = (bf16[4,64,128]{2,1,0:T(8,128)(2,1)S(1)}, bf16[4,64,128]{2,1,0:T(8,128)(2,1)S(1)}, u32[]{:S(2)}, u32[]{:S(2)}) collective-permute-start(bf16[4,64,128]{2,1,0:T(8,128)(2,1)S(1)} %pad_maximum_fusion.1), channel_id=1, source_target_pairs={{0,1},{1,0},{2,3},{3,2},{4,5},{5,4},{6,7},{7,6},{8,9},{9,8},{10,11... | collective-permute-start | bytes 196616 | tf_op jit(solution)/shard_map/ppermute | solution.py:270
  17.5 7.1 %collective-permute-start.4 = (bf16[4,64,128]{2,1,0:T(8,128)(2,1)S(1)}, bf16[4,64,128]{2,1,0:T(8,128)(2,1)S(1)}, u32[]{:S(2)}, u32[]{:S(2)}) collective-permute-start(bf16[4,64,128]{2,1,0:T(8,128)(2,1)S(1)} %pad_maximum_fusion.2), channel_id=1, source_target_pairs={{0,2},{1,3},{2,0},{3,1},{4,6},{5,7},{6,4},{7,5},{8,10},{9,11},{10,... | collective-permute-start | bytes 196616 | tf_op jit(solution)/shard_map/ppermute | solution.py:270
  18.7 8.3 %collective-permute-start.5 = (bf16[4,64,128]{2,1,0:T(8,128)(2,1)S(1)}, bf16[4,64,128]{2,1,0:T(8,128)(2,1)S(1)}, u32[]{:S(2)}, u32[]{:S(2)}) collective-permute-start(bf16[4,64,128]{2,1,0:T(8,128)(2,1)S(1)} %pad_maximum_fusion.3), channel_id=1, source_target_pairs={{0,3},{1,2},{2,1},{3,0},{4,7},{5,6},{6,5},{7,4},{8,11},{9,10},{10,... | collective-permute-start | bytes 196616 | tf_op jit(solution)/shard_map/ppermute | solution.py:270
  27.1 8.3 %collective-permute-start.6 = (bf16[4,4,64,128]{3,2,1,0:T(8,128)(2,1)S(1)}, bf16[4,4,64,128]{3,2,1,0:T(8,128)(2,1)S(1)}, u32[]{:S(2)}, u32[]{:S(2)}) collective-permute-start(bf16[4,4,64,128]{3,2,1,0:T(8,128)(2,1)S(1)} %pad_maximum_fusion.mine_ref), channel_id=1, source_target_pairs={{0,16},{16,0},{1,17},{17,1},{2,18},{18,2},{3,19},{19,3},{4,20},{20... | collective-permute-start | bytes 786440 | tf_op jit(solution)/shard_map/ppermute | solution.py:270
  46.8 41.6 %copy-start = (bf16[2048,128]{1,0:T(8,128)(2,1)S(1)}, bf16[2048,128]{1,0:T(8,128)(2,1)}, u32[]{:S(2)}) copy-start(bf16[2048,128]{1,0:T(8,128)(2,1)} %value_ref.1) | copy-start | bytes 1572868
  46.8 41.6 %copy-start.1 = (bf16[2048,128]{1,0:T(8,128)(2,1)S(1)}, bf16[2048,128]{1,0:T(8,128)(2,1)}, u32[]{:S(2)}) copy-start(bf16[2048,128]{1,0:T(8,128)(2,1)} %key_ref.1) | copy-start | bytes 1572868
  46.8 41.6 %copy-start.2 = (bf16[2048,128]{1,0:T(8,128)(2,1)S(1)}, bf16[2048,128]{1,0:T(8,128)(2,1)}, u32[]{:S(2)}) copy-start(bf16[2048,128]{1,0:T(8,128)(2,1)} %cot_ref.1) | copy-start | bytes 1572868

commit v4 on v3

--- a/solution.py
+++ b/solution.py
@@ -1,3 +1,4 @@
+import functools
 import math
 
 import jax
@@ -10,6 +11,7 @@
 
 TILE = 32
 STEPS = 4
+WINDOW = 6
 
 
 def evaluate(points, theta):
@@ -105,6 +107,10 @@
     c, s = np.cos(wave), np.sin(wave)
     ahead = np.block([[c, -s], [s, c]])
     return twist, jnp.asarray(np.stack([ahead, ahead.T]), jnp.bfloat16)
+
+
+def rows_of(block, chunk):
+    return pl.ds(pl.multiple_of(block * chunk, chunk), chunk)
 
 
 def gate_kernel(value_hbm, key_hbm, cot_hbm, query_hbm, out_hbm, *scratch):
@@ -214,13 +220,15 @@
                 spec_ref[half * (rows // tile) + step] = spec.astype(jnp.bfloat16)
 
 
-def spectral_kernel(sig_ref, spec_ref, twist_ref, wave_ref, out_ref, turned_ref):
+def spectral_kernel(sig_ref, spec_ref, twist_ref, wave_ref, *refs):
+    *out_refs, made_ref, turned_ref = refs
     count, _, chunk, width = sig_ref.shape
     tile = spec_ref.shape[1] // twist_ref.shape[0]
+    me = lax.axis_index("ctx")
 
     @pl.loop(0, chunk // tile)
     def _(step):
-        lanes = pl.ds(pl.multiple_of(step * tile, tile), tile)
+        lanes = rows_of(step, tile)
         specs = []
         for which in range(2):
             points = [sig_ref[b, which, lanes] for b in range(count)]
@@ -236,29 +244,56 @@
         )
         for which, (re, im) in enumerate(results):
             for b, part in enumerate(inverse(re, im, twist_ref, wave_ref)):
-                out_ref[b, which, lanes] = part.astype(jnp.bfloat16)
-
-
-def ungate_kernel(part_ref, value_ref, key_ref, cot_ref, gv_hbm, gk_hbm, gq_hbm, gf_hbm, *scratch):
-    blocks, _, chunk, width = part_ref.shape
-    outs = (gv_hbm, gk_hbm, gq_hbm, gf_hbm)
-    *made, sems = scratch
-    span, some = blocks * chunk // STEPS, blocks // STEPS
+                made_ref[b, which, lanes] = part.astype(jnp.bfloat16)
+
+    for k in range(count):
+        out_refs[k][...] = made_ref[me ^ k]
+
+
+def ungate_kernel(which_blocks, *refs):
+    *made, sems = refs[-5:]
+    outs = refs[-9:-5]
+    value_ref, key_ref, cot_ref = refs[:3]
+    me = lax.axis_index("ctx")
     sends = []
-    for step in range(STEPS):
-        rows, part = pl.ds(step * span, span), pl.ds(step * some, some)
-        conv, grad, filt = (
-            part_ref[part, which].astype(jnp.float32).reshape(span, width) for which in range(3)
-        )
+    for i, k in enumerate(which_blocks):
+        part_ref = refs[3 + i]
+        rows = rows_of(me ^ k, part_ref.shape[1])
+        conv, grad, filt = (part_ref[which].astype(jnp.float32) for which in range(3))
         made[0][rows] = (grad * key_ref[rows].astype(jnp.float32)).astype(jnp.bfloat16)
         made[1][rows] = (grad * value_ref[rows].astype(jnp.float32)).astype(jnp.bfloat16)
         made[2][rows] = (cot_ref[rows].astype(jnp.float32) * conv).astype(jnp.bfloat16)
         made[3][rows] = filt
-        for i, (source, to) in enumerate(zip(made, outs)):
-            sends.append(pltpu.make_async_copy(source.at[rows], to.at[rows], sems.at[i, step]))
+        for j, (source, to) in enumerate(zip(made, outs)):
+            sends.append(pltpu.make_async_copy(source.at[rows], to.at[rows], sems.at[j, i]))
             sends[-1].start()
     for send in sends:
         send.wait()
+
+
+def partners(count):
+    near, size = [], count // 4
+    while size:
+        near += range(size, 2 * size)
+        size //= 2
+    far = list(range(count // 2, count))
+    order = []
+    for i, k in enumerate(far):
+        order += [k] + near[i : i + 1]
+    return order
+
+
+def spread(blocks):
+    count = len(blocks)
+    got = list(blocks)
+    order = partners(count)
+    for i, k in enumerate(order):
+        block = blocks[k]
+        if i >= WINDOW:
+            before = order[i - WINDOW]
+            block, got[before] = lax.optimization_barrier((block, got[before]))
+        got[k] = lax.ppermute(block, "ctx", [(j, j ^ k) for j in range(count)])
+    return got
 
 
 def exchange(parts):
@@ -329,26 +364,39 @@
             flops=8 * count * chunk * width * width, bytes_accessed=2**20, transcendentals=0
         ),
     )(mine, other, twist, wave)
+    message = jax.ShapeDtypeStruct((3, chunk, width), jnp.bfloat16)
     made = pl.pallas_call(
         spectral_kernel,
         in_specs=[here] * 4,
-        out_specs=here,
-        out_shape=jax.ShapeDtypeStruct((count, 3, chunk, width), jnp.bfloat16),
-        scratch_shapes=[pltpu.VMEM((2, tall, 2 * width), jnp.bfloat16)],
+        out_specs=[here] * count,
+        out_shape=[message] * count,
+        scratch_shapes=[
+            pltpu.VMEM((count, 3, chunk, width), jnp.bfloat16),
+            pltpu.VMEM((2, tall, 2 * width), jnp.bfloat16),
+        ],
         compiler_params=limit,
     )(held, spec, twist, wave)
-    returned = exchange(made)
+    got = spread(made)
     half = jax.ShapeDtypeStruct((channels, width), jnp.bfloat16)
     wide = jax.ShapeDtypeStruct((channels, width), jnp.float32)
-    return pl.pallas_call(
-        ungate_kernel,
-        in_specs=[here] * 4,
-        out_specs=[hbm] * 4,
-        out_shape=[half, half, half, wide],
-        scratch_shapes=[pltpu.VMEM((channels, width), jnp.bfloat16)] * 3
-        + [pltpu.VMEM((channels, width), jnp.float32), pltpu.SemaphoreType.DMA((4, STEPS))],
-        compiler_params=limit,
-    )(returned, values, keys, grad_out)
+    order = [0] + partners(count)
+    early = max(count - WINDOW, 1)
+    outs = []
+    for blocks in (order[:early], order[early:]):
+        outs = pl.pallas_call(
+            functools.partial(ungate_kernel, blocks),
+            in_specs=[here] * (3 + len(blocks)) + [hbm] * len(outs),
+            out_specs=[hbm] * 4,
+            out_shape=[half, half, half, wide],
+            input_output_aliases={3 + len(blocks) + i: i for i in range(len(outs))},
+            scratch_shapes=[pltpu.VMEM((channels, width), jnp.bfloat16)] * 3
+            + [
+                pltpu.VMEM((channels, width), jnp.float32),
+                pltpu.SemaphoreType.DMA((4, len(blocks))),
+            ],
+            compiler_params=limit,
+        )(values, keys, grad_out, *[got[k] for k in blocks], *outs)
+    return outs
 
 
 def solution(mesh):

time: 90.9 us -> 86.1 us (0.947)
  blocking collectives: 41.6 us -> 0 us
  starting transfers between devices: 13.7 us -> 39.6 us
  waiting for transfers between devices: 22.2 us -> 30.8 us
  Pallas kernels: 10.6 us -> 13.2 us
    all_to_all x1 -> x0, blocking collectives: 41.6 us -> none  [exchange(): return lax.all_to_all(parts, 'ctx', split_axis=0, concat_axis=0, tiled=True)]
    ppermute x0 -> x15, starting transfers between devices: none -> 26.1 us  [spread(): got[k] = lax.ppermute(block, 'ctx', [(j, j ^ k) for j in range(count)])]
    ppermute x0 -> x15, waiting for transfers between devices: none -> 8.65 us  [spread(): got[k] = lax.ppermute(block, 'ctx', [(j, j ^ k) for j in range(count)])]
    pallas_call x2 -> x3, Pallas kernels: 6.65 us -> 9.24 us  [the longest x1 6.34 us: shards(): pl.pallas_call(spectral_kernel, in_specs=[here] * 4, out_specs=[here] * c...]
  transfers between devices with their start and end apart: 8 -> 23, of which waited for: 5 -> 12; matrix products, arithmetic and copies ran while one was open for 0% -> 0% of each run, Pallas kernels for 4% -> 7%
where the time goes in v4:
time: 86.1 us; the launch traced here: 85.8 us
  starting transfers between devices  39.6 us (46%)
  waiting for transfers between devices  30.8 us (36%)
  Pallas kernels  13.2 us (15%)
  local copies, waits for them, and re-layouts  1.22 us (1%)
  between operations  0.87 us (1%)
    ppermute x15, starting transfers between devices, spread(): got[k] = lax.ppermute(block, 'ctx', [(j, j ^ k) for j in range(count)])  26.1 us
    ppermute x7, waiting for transfers between devices, swap(): return lax.ppermute(block, axis, [(i, i ^ gap) for i in range(size)])  17.2 us
    ppermute x15, waiting for transfers between devices, spread(): got[k] = lax.ppermute(block, 'ctx', [(j, j ^ k) for j in range(count)])  8.65 us
    all_to_all x1, starting transfers between devices, exchange(): return lax.all_to_all(parts, 'ctx', split_axis=0, concat_axis=0, tiled=True)  7.32 us
    pallas_call x1, Pallas kernels, shards(): pl.pallas_call(spectral_kernel, in_specs=[here] * 4, out_specs=[here] * c...  6.34 us
    ppermute x7, starting transfers between devices, swap(): return lax.ppermute(block, axis, [(i, i ^ gap) for i in range(size)])  6.2 us
    all_to_all x1, waiting for transfers between devices, exchange(): return lax.all_to_all(parts, 'ctx', split_axis=0, concat_axis=0, tiled=True)  4.92 us
    pallas_call x2, Pallas kernels, shards(): pl.pallas_call(functools.partial(ungate_kernel, blocks), in_specs=[here]...  2.9 us
  transfers between devices with their start and end apart: 23, of which 12 were waited for; matrix products, arithmetic and copies ran while one was open for 0% of the time, Pallas kernels for 7%

profile of v4, /device:TPU:13, one launch (start us, length us, event | category | flops | bytes accessed | tf_op | source)
XLA Modules:
  0.0 85.8 jit_solution(10659264663843923245)
XLA Ops:
  0.7 1.1 %fusion.3 = (bf16[4,64,128]{2,1,0:T(8,128)(2,1)S(1)}, bf16[4,64,128]{2,1,0:T(8,128)(2,1)S(1)}, bf16[4,64,128]{2,1,0:T(8,128)(2,1)S(1)}, bf16[4,64,128]{2,1,0:T(8,128)(2,1)S(1)}) fusion(f32[4,4,2,64,128]{4,3,2,1,0:T(8,128)} %bitcast.30, s32[]{:T(128)S(6)} %select_n.106, s32[]{:T(128)S(6)} %select_n.100, s32[]{:T(128)S(6)} %select_n.104, s32[]{:T(128)S(6)} %select_n.102, ...), kind=kLoop, calls=%fused_computation.8 | loop fusion | bytes 524308 | tf_op jit(solution)/shard_map/convert_element_type | solution.py:318
  1.8 1.4 %collective-permute-start.2 = (bf16[4,64,128]{2,1,0:T(8,128)(2,1)S(1)}, bf16[4,64,128]{2,1,0:T(8,128)(2,1)S(1)}, u32[]{:S(2)}, u32[]{:S(2)}) collective-permute-start(bf16[4,64,128]{2,1,0:T(8,128)(2,1)S(1)} %get-tuple-element.90), channel_id=1, source_target_pairs={{0,12},{1,13},{2,14},{3,15},{4,8},{5,9},{6,10},{7,11},{8,4},{9,5},... | collective-permute-start | bytes 196616 | tf_op jit(solution)/shard_map/ppermute | solution.py:305
  3.2 1.1 %collective-permute-start.1 = (bf16[4,64,128]{2,1,0:T(8,128)(2,1)S(1)}, bf16[4,64,128]{2,1,0:T(8,128)(2,1)S(1)}, u32[]{:S(2)}, u32[]{:S(2)}) collective-permute-start(bf16[4,64,128]{2,1,0:T(8,128)(2,1)S(1)} %get-tuple-element.91), channel_id=1, source_target_pairs={{0,8},{1,9},{2,10},{3,11},{4,12},{5,13},{6,14},{7,15},{8,0},{9,1},... | collective-permute-start | bytes 196616 | tf_op jit(solution)/shard_map/ppermute | solution.py:305
  4.3 1.1 %collective-permute-start = (bf16[4,64,128]{2,1,0:T(8,128)(2,1)S(1)}, bf16[4,64,128]{2,1,0:T(8,128)(2,1)S(1)}, u32[]{:S(2)}, u32[]{:S(2)}) collective-permute-start(bf16[4,64,128]{2,1,0:T(8,128)(2,1)S(1)} %get-tuple-element.92), channel_id=1, source_target_pairs={{0,4},{1,5},{2,6},{3,7},{4,0},{5,1},{6,2},{7,3},{8,12},{9,13},{10,... | collective-permute-start | bytes 196616 | tf_op jit(solution)/shard_map/ppermute | solution.py:305
  5.4 2.5 %shard_map.102 = bf16[16,2,128,128]{3,2,1,0:T(8,128)(2,1)} custom-call(bf16[2048,128]{1,0:T(8,128)(2,1)} %refs_0_.3, bf16[2048,128]{1,0:T(8,128)(2,1)} %refs_1_.3, bf16[2048,128]{1,0:T(8,128)(2,1)} %refs_2_.3, bf16[2048,128]{1,0:T(8,128)(2,1)} %query_hbm.1), custom_call_target="tpu_custom_call" | custom-call | tf_op jit(solution)/shard_map/pallas_call | solution.py:339
  8.0 1.5 %collective-permute-done = bf16[4,64,128]{2,1,0:T(8,128)(2,1)S(1)} collective-permute-done((bf16[4,64,128]{2,1,0:T(8,128)(2,1)S(1)}, bf16[4,64,128]{2,1,0:T(8,128)(2,1)S(1)}, u32[]{:S(2)}, u32[]{:S(2)}) %collective-permute-start) | collective-permute-done | bytes 65568 | tf_op jit(solution)/shard_map/ppermute | solution.py:305
  9.5 7.3 %all-to-all-start = ((bf16[16,2,128,128]{3,2,1,0:T(8,128)(2,1)}), bf16[16,2,128,128]{3,2,1,0:T(8,128)(2,1)}, u32[]{:S(2)}, u32[]{:S(2)}) async-start(bf16[16,2,128,128]{3,2,1,0:T(8,128)(2,1)} %shard_map.102), calls=%async_computation | async-start | bytes 2097152 | tf_op jit(solution)/shard_map/all_to_all | solution.py:300
  17.4 1.2 %collective-permute-start.4 = (bf16[4,64,128]{2,1,0:T(8,128)(2,1)S(1)}, bf16[4,64,128]{2,1,0:T(8,128)(2,1)S(1)}, u32[]{:S(2)}, u32[]{:S(2)}) collective-permute-start(bf16[4,64,128]{2,1,0:T(8,128)(2,1)S(1)} %pad_maximum_fusion.2), channel_id=1, source_target_pairs={{0,2},{1,3},{2,0},{3,1},{4,6},{5,7},{6,4},{7,5},{8,10},{9,11},{10,... | collective-permute-start | bytes 196616 | tf_op jit(solution)/shard_map/ppermute | solution.py:305
  19.3 5.2 %collective-permute-done.4 = bf16[4,64,128]{2,1,0:T(8,128)(2,1)S(1)} collective-permute-done((bf16[4,64,128]{2,1,0:T(8,128)(2,1)S(1)}, bf16[4,64,128]{2,1,0:T(8,128)(2,1)S(1)}, u32[]{:S(2)}, u32[]{:S(2)}) %collective-permute-start.4) | collective-permute-done | bytes 65568 | tf_op jit(solution)/shard_map/ppermute | solution.py:305
  24.6 2.4 %collective-permute-done.5 = bf16[4,64,128]{2,1,0:T(8,128)(2,1)S(1)} collective-permute-done((bf16[4,64,128]{2,1,0:T(8,128)(2,1)S(1)}, bf16[4,64,128]{2,1,0:T(8,128)(2,1)S(1)}, u32[]{:S(2)}, u32[]{:S(2)}) %collective-permute-start.5) | collective-permute-done | bytes 65568 | tf_op jit(solution)/shard_map/ppermute | solution.py:305
  27.3 8.0 %collective-permute-done.6.other_ref = bf16[4,4,64,128]{3,2,1,0:T(8,128)(2,1)S(1)} collective-permute-done((bf16[4,4,64,128]{3,2,1,0:T(8,128)(2,1)S(1)}, bf16[4,4,64,128]{3,2,1,0:T(8,128)(2,1)S(1)}, u32[]{:S(2)}, u32[]{:S(2)}) %collective-permute-start.6) | collective-permute-done | bytes 262176 | tf_op jit(solution)/shard_map/ppermute | solution.py:305
  35.4 1.4 %shard_map.103.spec_ref = bf16[4,544,256]{2,1,0:T(8,128)(2,1)S(1)} custom-call(bf16[4,4,64,128]{3,2,1,0:T(8,128)(2,1)S(1)} %pad_maximum_fusion.mine_ref, bf16[4,4,64,128]{3,2,1,0:T(8,128)(2,1)S(1)} %collective-permute-done.6.other_ref, f32[17,4,128]{2,1,0:T(4,128)S(1)} %copy-done.4, bf16[2,256,256]{2,1,0:T(8,128)(2,1)S(1)} %copy-done.3), custom_call_target="tpu_custom_call" | custom-call | flops 268435456 | bytes 1048576 | tf_op jit(solution)/shard_map/pallas_call | solution.py:356
  36.8 4.9 %all-to-all-done.sig_ref = bf16[16,2,128,128]{3,2,1,0:T(8,128)(2,1)} async-done(((bf16[16,2,128,128]{3,2,1,0:T(8,128)(2,1)}), bf16[16,2,128,128]{3,2,1,0:T(8,128)(2,1)}, u32[]{:S(2)}, u32[]{:S(2)}) %all-to-all-start) | async-done | bytes 1048608 | tf_op jit(solution)/shard_map/all_to_all | solution.py:300
  41.8 6.3 %shard_map.104 = (bf16[3,128,128]{2,1,0:T(8,128)(2,1)S(1)}, bf16[3,128,128]{2,1,0:T(8,128)(2,1)S(1)}, bf16[3,128,128]{2,1,0:T(8,128)(2,1)S(1)}, bf16[3,128,128]{...) custom-call(bf16[16,2,128,128]{3,2,1,0:T(8,128)(2,1)} %all-to-all-do, ...), custom_call_target="tpu_custom_call" | custom-call | tf_op jit(solution)/shard_map/pallas_call | solution.py:368
  48.7 1.7 %collective-permute-start.16 = (bf16[3,128,128]{2,1,0:T(8,128)(2,1)S(1)}, bf16[3,128,128]{2,1,0:T(8,128)(2,1)S(1)}, u32[]{:S(2)}, u32[]{:S(2)}) collective-permute-start(bf16[3,128,128]{2,1,0:T(8,128)(2,1)S(1)} %get-tuple-element.68), channel_id=1, source_target_pairs={{0,4},{1,5},{2,6},{3,7},{4,0},{5,1},{6,2},{7,3},{8,12},{9,13},{10,... | collective-permute-start | bytes 294920 | tf_op jit(solution)/shard_map/ppermute | solution.py:295
  50.4 1.1 %collective-permute-start.19 = (bf16[3,128,128]{2,1,0:T(8,128)(2,1)S(1)}, bf16[3,128,128]{2,1,0:T(8,128)(2,1)S(1)}, u32[]{:S(2)}, u32[]{:S(2)}) collective-permute-start(bf16[3,128,128]{2,1,0:T(8,128)(2,1)S(1)} %get-tuple-element.73), channel_id=1, source_target_pairs={{0,9},{1,8},{2,11},{3,10},{4,13},{5,12},{6,15},{7,14},{8,1},{9,0},... | collective-permute-start | bytes 294920 | tf_op jit(solution)/shard_map/ppermute | solution.py:295
  51.5 0.8 collective-permute-start.7
  52.3 2.1 %collective-permute-start.9 = (bf16[3,128,128]{2,1,0:T(8,128)(2,1)S(1)}, bf16[3,128,128]{2,1,0:T(8,128)(2,1)S(1)}, u32[]{:S(2)}, u32[]{:S(2)}) collective-permute-start(bf16[3,128,128]{2,1,0:T(8,128)(2,1)S(1)} %get-tuple-element.56), channel_id=1, source_target_pairs={{0,10},{1,11},{2,8},{3,9},{4,14},{5,15},{6,12},{7,13},{8,2},{9,3},... | collective-permute-start | bytes 294920 | tf_op jit(solution)/shard_map/ppermute | solution.py:295
  54.4 1.0 %collective-permute-start.11 = (bf16[3,128,128]{2,1,0:T(8,128)(2,1)S(1)}, bf16[3,128,128]{2,1,0:T(8,128)(2,1)S(1)}, u32[]{:S(2)}, u32[]{:S(2)}) collective-permute-start(bf16[3,128,128]{2,1,0:T(8,128)(2,1)S(1)} %get-tuple-element.59), channel_id=1, source_target_pairs={{0,6},{1,7},{2,4},{3,5},{4,2},{5,3},{6,0},{7,1},{8,14},{9,15},{10,... | collective-permute-start | bytes 294920 | tf_op jit(solution)/shard_map/ppermute | solution.py:295
  55.4 4.4 %collective-permute-start.14 = (bf16[3,128,128]{2,1,0:T(8,128)(2,1)S(1)}, bf16[3,128,128]{2,1,0:T(8,128)(2,1)S(1)}, u32[]{:S(2)}, u32[]{:S(2)}) collective-permute-start(bf16[3,128,128]{2,1,0:T(8,128)(2,1)S(1)} %get-tuple-element.64), channel_id=1, source_target_pairs={{0,11},{1,10},{2,9},{3,8},{4,15},{5,14},{6,13},{7,12},{8,3},{9,2},... | collective-permute-start | bytes 294920 | tf_op jit(solution)/shard_map/ppermute | solution.py:295
  61.8 1.4 %collective-permute-done.9.refs_8_ = bf16[3,128,128]{2,1,0:T(8,128)(2,1)S(1)} collective-permute-done((bf16[3,128,128]{2,1,0:T(8,128)(2,1)S(1)}, bf16[3,128,128]{2,1,0:T(8,128)(2,1)S(1)}, u32[]{:S(2)}, u32[]{:S(2)}) %collective-permute-start.9) | collective-permute-done | bytes 98336 | tf_op jit(solution)/shard_map/ppermute | solution.py:295
  64.4 3.1 %collective-permute-start.10 = (bf16[3,128,128]{2,1,0:T(8,128)(2,1)S(1)}, bf16[3,128,128]{2,1,0:T(8,128)(2,1)S(1)}, u32[]{:S(2)}, u32[]{:S(2)}) collective-permute-start(bf16[3,128,128]{2,1,0:T(8,128)(2,1)S(1)} %get-tuple-element.57), channel_id=1, source_target_pairs={{0,13},{1,12},{2,15},{3,14},{4,9},{5,8},{6,11},{7,10},{8,5},{9,4},... | collective-permute-start | bytes 294920 | tf_op jit(solution)/shard_map/ppermute | solution.py:295
  67.5 1.1 %collective-permute-done.14.refs_10_ = bf16[3,128,128]{2,1,0:T(8,128)(2,1)S(1)} collective-permute-done((bf16[3,128,128]{2,1,0:T(8,128)(2,1)S(1)}, bf16[3,128,128]{2,1,0:T(8,128)(2,1)S(1)}, u32[]{:S(2)}, u32[]{:S(2)}) %collective-permute-start.14) | collective-permute-done | bytes 98336 | tf_op jit(solution)/shard_map/ppermute | solution.py:295
  68.6 1.0 %collective-permute-start.12 = (bf16[3,128,128]{2,1,0:T(8,128)(2,1)S(1)}, bf16[3,128,128]{2,1,0:T(8,128)(2,1)S(1)}, u32[]{:S(2)}, u32[]{:S(2)}) collective-permute-start(bf16[3,128,128]{2,1,0:T(8,128)(2,1)S(1)} %get-tuple-element.60), channel_id=1, source_target_pairs={{0,3},{1,2},{2,1},{3,0},{4,7},{5,6},{6,5},{7,4},{8,11},{9,10},{10,... | collective-permute-start | bytes 294920 | tf_op jit(solution)/shard_map/ppermute | solution.py:295
  69.7 1.1 %collective-permute-start.15 = (bf16[3,128,128]{2,1,0:T(8,128)(2,1)S(1)}, bf16[3,128,128]{2,1,0:T(8,128)(2,1)S(1)}, u32[]{:S(2)}, u32[]{:S(2)}) collective-permute-start(bf16[3,128,128]{2,1,0:T(8,128)(2,1)S(1)} %get-tuple-element.65), channel_id=1, source_target_pairs={{0,14},{1,15},{2,12},{3,13},{4,10},{5,11},{6,8},{7,9},{8,6},{9,7},... | collective-permute-start | bytes 294920 | tf_op jit(solution)/shard_map/ppermute | solution.py:295
  70.8 5.0 %collective-permute-start.18 = (bf16[3,128,128]{2,1,0:T(8,128)(2,1)S(1)}, bf16[3,128,128]{2,1,0:T(8,128)(2,1)S(1)}, u32[]{:S(2)}, u32[]{:S(2)}) collective-permute-start(bf16[3,128,128]{2,1,0:T(8,128)(2,1)S(1)} %get-tuple-element.70), channel_id=1, source_target_pairs={{0,1},{1,0},{2,3},{3,2},{4,5},{5,4},{6,7},{7,6},{8,9},{9,8},{10,11... | collective-permute-start | bytes 294920 | tf_op jit(solution)/shard_map/ppermute | solution.py:295
  75.8 2.1 %collective-permute-start.21 = (bf16[3,128,128]{2,1,0:T(8,128)(2,1)S(1)}, bf16[3,128,128]{2,1,0:T(8,128)(2,1)S(1)}, u32[]{:S(2)}, u32[]{:S(2)}) collective-permute-start(bf16[3,128,128]{2,1,0:T(8,128)(2,1)S(1)} %get-tuple-element.75), channel_id=1, source_target_pairs={{0,15},{1,14},{2,13},{3,12},{4,11},{5,10},{6,9},{7,8},{8,7},{9,6},... | collective-permute-start | bytes 294920 | tf_op jit(solution)/shard_map/ppermute | solution.py:295
  77.9 1.7 %shard_map.105 = (bf16[2048,128]{1,0:T(8,128)(2,1)}, bf16[2048,128]{1,0:T(8,128)(2,1)}, bf16[2048,128]{1,0:T(8,128)(2,1)}, f32[2048,128]{1,0:T(8,128)}) custom-call(bf16[2048,128]{1,0:T(8,128)(2,1)S(1)} %copy-done, bf16[2048,128]{1,0:T(8,128)(2,1)S(1)} %copy-done.1, bf16[2048,128]{1,0:T(8,128)(2,1)S(1)} %copy-done.2, ...), custom_call_target="tpu_custom_call" | custom-call | tf_op jit(solution)/shard_map/pallas_call | solution.py:386
  79.6 1.1 %collective-permute-done.10.refs_4_ = bf16[3,128,128]{2,1,0:T(8,128)(2,1)S(1)} collective-permute-done((bf16[3,128,128]{2,1,0:T(8,128)(2,1)S(1)}, bf16[3,128,128]{2,1,0:T(8,128)(2,1)S(1)}, u32[]{:S(2)}, u32[]{:S(2)}) %collective-permute-start.10) | collective-permute-done | bytes 98336 | tf_op jit(solution)/shard_map/ppermute | solution.py:295
  80.6 1.8 %collective-permute-done.15.refs_6_ = bf16[3,128,128]{2,1,0:T(8,128)(2,1)S(1)} collective-permute-done((bf16[3,128,128]{2,1,0:T(8,128)(2,1)S(1)}, bf16[3,128,128]{2,1,0:T(8,128)(2,1)S(1)}, u32[]{:S(2)}, u32[]{:S(2)}) %collective-permute-start.15) | collective-permute-done | bytes 98336 | tf_op jit(solution)/shard_map/ppermute | solution.py:295
  82.5 2.1 %collective-permute-done.21.refs_8_ = bf16[3,128,128]{2,1,0:T(8,128)(2,1)S(1)} collective-permute-done((bf16[3,128,128]{2,1,0:T(8,128)(2,1)S(1)}, bf16[3,128,128]{2,1,0:T(8,128)(2,1)S(1)}, u32[]{:S(2)}, u32[]{:S(2)}) %collective-permute-start.21) | collective-permute-done | bytes 98336 | tf_op jit(solution)/shard_map/ppermute | solution.py:295
  84.6 1.2 %shard_map.106 = (bf16[2048,128]{1,0:T(8,128)(2,1)}, bf16[2048,128]{1,0:T(8,128)(2,1)}, bf16[2048,128]{1,0:T(8,128)(2,1)}, f32[2048,128]{1,0:T(8,128)}) custom-call(bf16[2048,128]{1,0:T(8,128)(2,1)S(1)} %copy-done, bf16[2048,128]{1,0:T(8,128)(2,1)S(1)} %copy-done.1, ...), custom_call_target="tpu_custom_call", output_to_operand_aliasing={{0}: (9, {}), {1}: (10, {}), {2}: (11, {}), {3}: (12, {})} | custom-call | tf_op jit(solution)/shard_map/pallas_call | solution.py:386
  (37 shorter events, 5.4 us)
Async XLA Ops:
  1.8 6.1 %collective-permute-start.2 = (bf16[4,64,128]{2,1,0:T(8,128)(2,1)S(1)}, bf16[4,64,128]{2,1,0:T(8,128)(2,1)S(1)}, u32[]{:S(2)}, u32[]{:S(2)}) collective-permute-start(bf16[4,64,128]{2,1,0:T(8,128)(2,1)S(1)} %get-tuple-element.90), channel_id=1, source_target_pairs={{0,12},{1,13},{2,14},{3,15},{4,8},{5,9},{6,10},{7,11},{8,4},{9,5},... | collective-permute-start | bytes 196616 | tf_op jit(solution)/shard_map/ppermute | solution.py:305
  3.2 4.8 %collective-permute-start.1 = (bf16[4,64,128]{2,1,0:T(8,128)(2,1)S(1)}, bf16[4,64,128]{2,1,0:T(8,128)(2,1)S(1)}, u32[]{:S(2)}, u32[]{:S(2)}) collective-permute-start(bf16[4,64,128]{2,1,0:T(8,128)(2,1)S(1)} %get-tuple-element.91), channel_id=1, source_target_pairs={{0,8},{1,9},{2,10},{3,11},{4,12},{5,13},{6,14},{7,15},{8,0},{9,1},... | collective-permute-start | bytes 196616 | tf_op jit(solution)/shard_map/ppermute | solution.py:305
  4.3 5.2 %collective-permute-start = (bf16[4,64,128]{2,1,0:T(8,128)(2,1)S(1)}, bf16[4,64,128]{2,1,0:T(8,128)(2,1)S(1)}, u32[]{:S(2)}, u32[]{:S(2)}) collective-permute-start(bf16[4,64,128]{2,1,0:T(8,128)(2,1)S(1)} %get-tuple-element.92), channel_id=1, source_target_pairs={{0,4},{1,5},{2,6},{3,7},{4,0},{5,1},{6,2},{7,3},{8,12},{9,13},{10,... | collective-permute-start | bytes 196616 | tf_op jit(solution)/shard_map/ppermute | solution.py:305
  9.5 32.3 %all-to-all-start = ((bf16[16,2,128,128]{3,2,1,0:T(8,128)(2,1)}), bf16[16,2,128,128]{3,2,1,0:T(8,128)(2,1)}, u32[]{:S(2)}, u32[]{:S(2)}) async-start(bf16[16,2,128,128]{3,2,1,0:T(8,128)(2,1)} %shard_map.102), calls=%async_computation | async-start | bytes 2097152 | tf_op jit(solution)/shard_map/all_to_all | solution.py:300
  16.8 18.6 %copy-start.3 = (bf16[2,256,256]{2,1,0:T(8,128)(2,1)S(1)}, bf16[2,256,256]{2,1,0:T(8,128)(2,1)}, u32[]{:S(2)}) copy-start(bf16[2,256,256]{2,1,0:T(8,128)(2,1)} %constant.222.clone.wave_ref) | copy-start | bytes 786436
  16.8 18.6 %copy-start.4 = (f32[17,4,128]{2,1,0:T(4,128)S(1)}, f32[17,4,128]{2,1,0:T(4,128)}, u32[]{:S(2)}) copy-start(f32[17,4,128]{2,1,0:T(4,128)} %constant.223.clone.twist_ref) | copy-start | bytes 104452
  16.9 2.4 %collective-permute-start.3 = (bf16[4,64,128]{2,1,0:T(8,128)(2,1)S(1)}, bf16[4,64,128]{2,1,0:T(8,128)(2,1)S(1)}, u32[]{:S(2)}, u32[]{:S(2)}) collective-permute-start(bf16[4,64,128]{2,1,0:T(8,128)(2,1)S(1)} %pad_maximum_fusion.1), channel_id=1, source_target_pairs={{0,1},{1,0},{2,3},{3,2},{4,5},{5,4},{6,7},{7,6},{8,9},{9,8},{10,11... | collective-permute-start | bytes 196616 | tf_op jit(solution)/shard_map/ppermute | solution.py:305
  17.4 7.2 %collective-permute-start.4 = (bf16[4,64,128]{2,1,0:T(8,128)(2,1)S(1)}, bf16[4,64,128]{2,1,0:T(8,128)(2,1)S(1)}, u32[]{:S(2)}, u32[]{:S(2)}) collective-permute-start(bf16[4,64,128]{2,1,0:T(8,128)(2,1)S(1)} %pad_maximum_fusion.2), channel_id=1, source_target_pairs={{0,2},{1,3},{2,0},{3,1},{4,6},{5,7},{6,4},{7,5},{8,10},{9,11},{10,... | collective-permute-start | bytes 196616 | tf_op jit(solution)/shard_map/ppermute | solution.py:305
  18.6 8.3 %collective-permute-start.5 = (bf16[4,64,128]{2,1,0:T(8,128)(2,1)S(1)}, bf16[4,64,128]{2,1,0:T(8,128)(2,1)S(1)}, u32[]{:S(2)}, u32[]{:S(2)}) collective-permute-start(bf16[4,64,128]{2,1,0:T(8,128)(2,1)S(1)} %pad_maximum_fusion.3), channel_id=1, source_target_pairs={{0,3},{1,2},{2,1},{3,0},{4,7},{5,6},{6,5},{7,4},{8,11},{9,10},{10,... | collective-permute-start | bytes 196616 | tf_op jit(solution)/shard_map/ppermute | solution.py:305
  27.0 8.3 %collective-permute-start.6 = (bf16[4,4,64,128]{3,2,1,0:T(8,128)(2,1)S(1)}, bf16[4,4,64,128]{3,2,1,0:T(8,128)(2,1)S(1)}, u32[]{:S(2)}, u32[]{:S(2)}) collective-permute-start(bf16[4,4,64,128]{3,2,1,0:T(8,128)(2,1)S(1)} %pad_maximum_fusion.mine_ref), channel_id=1, source_target_pairs={{0,16},{16,0},{1,17},{17,1},{2,18},{18,2},{3,19},{19,3},{4,20},{20... | collective-permute-start | bytes 786440 | tf_op jit(solution)/shard_map/ppermute | solution.py:305
  36.8 41.1 %copy-start = (bf16[2048,128]{1,0:T(8,128)(2,1)S(1)}, bf16[2048,128]{1,0:T(8,128)(2,1)}, u32[]{:S(2)}) copy-start(bf16[2048,128]{1,0:T(8,128)(2,1)} %refs_0_.3) | copy-start | bytes 1572868
  36.8 41.1 %copy-start.1 = (bf16[2048,128]{1,0:T(8,128)(2,1)S(1)}, bf16[2048,128]{1,0:T(8,128)(2,1)}, u32[]{:S(2)}) copy-start(bf16[2048,128]{1,0:T(8,128)(2,1)} %refs_1_.3) | copy-start | bytes 1572868
  36.8 41.1 %copy-start.2 = (bf16[2048,128]{1,0:T(8,128)(2,1)S(1)}, bf16[2048,128]{1,0:T(8,128)(2,1)}, u32[]{:S(2)}) copy-start(bf16[2048,128]{1,0:T(8,128)(2,1)} %refs_2_.3) | copy-start | bytes 1572868
  48.1 6.3 %collective-permute-start.13 = (bf16[3,128,128]{2,1,0:T(8,128)(2,1)S(1)}, bf16[3,128,128]{2,1,0:T(8,128)(2,1)S(1)}, u32[]{:S(2)}, u32[]{:S(2)}) collective-permute-start(bf16[3,128,128]{2,1,0:T(8,128)(2,1)S(1)} %get-tuple-element.63), channel_id=1, source_target_pairs={{0,8},{1,9},{2,10},{3,11},{4,12},{5,13},{6,14},{7,15},{8,0},{9,1},... | collective-permute-start | bytes 294920 | tf_op jit(solution)/shard_map/ppermute | solution.py:295
  48.7 6.7 %collective-permute-start.16 = (bf16[3,128,128]{2,1,0:T(8,128)(2,1)S(1)}, bf16[3,128,128]{2,1,0:T(8,128)(2,1)S(1)}, u32[]{:S(2)}, u32[]{:S(2)}) collective-permute-start(bf16[3,128,128]{2,1,0:T(8,128)(2,1)S(1)} %get-tuple-element.68), channel_id=1, source_target_pairs={{0,4},{1,5},{2,6},{3,7},{4,0},{5,1},{6,2},{7,3},{8,12},{9,13},{10,... | collective-permute-start | bytes 294920 | tf_op jit(solution)/shard_map/ppermute | solution.py:295
  50.4 9.4 %collective-permute-start.19 = (bf16[3,128,128]{2,1,0:T(8,128)(2,1)S(1)}, bf16[3,128,128]{2,1,0:T(8,128)(2,1)S(1)}, u32[]{:S(2)}, u32[]{:S(2)}) collective-permute-start(bf16[3,128,128]{2,1,0:T(8,128)(2,1)S(1)} %get-tuple-element.73), channel_id=1, source_target_pairs={{0,9},{1,8},{2,11},{3,10},{4,13},{5,12},{6,15},{7,14},{8,1},{9,0},... | collective-permute-start | bytes 294920 | tf_op jit(solution)/shard_map/ppermute | solution.py:295
  51.5 9.6 %collective-permute-start.7 = (bf16[3,128,128]{2,1,0:T(8,128)(2,1)S(1)}, bf16[3,128,128]{2,1,0:T(8,128)(2,1)S(1)}, u32[]{:S(2)}, u32[]{:S(2)}) collective-permute-start(bf16[3,128,128]{2,1,0:T(8,128)(2,1)S(1)} %get-tuple-element.53), channel_id=1, source_target_pairs={{0,5},{1,4},{2,7},{3,6},{4,1},{5,0},{6,3},{7,2},{8,13},{9,12},{10,... | collective-permute-start | bytes 294920 | tf_op jit(solution)/shard_map/ppermute | solution.py:295
  52.3 10.9 %collective-permute-start.9 = (bf16[3,128,128]{2,1,0:T(8,128)(2,1)S(1)}, bf16[3,128,128]{2,1,0:T(8,128)(2,1)S(1)}, u32[]{:S(2)}, u32[]{:S(2)}) collective-permute-start(bf16[3,128,128]{2,1,0:T(8,128)(2,1)S(1)} %get-tuple-element.56), channel_id=1, source_target_pairs={{0,10},{1,11},{2,8},{3,9},{4,14},{5,15},{6,12},{7,13},{8,2},{9,3},... | collective-permute-start | bytes 294920 | tf_op jit(solution)/shard_map/ppermute | solution.py:295
  54.4 10.0 %collective-permute-start.11 = (bf16[3,128,128]{2,1,0:T(8,128)(2,1)S(1)}, bf16[3,128,128]{2,1,0:T(8,128)(2,1)S(1)}, u32[]{:S(2)}, u32[]{:S(2)}) collective-permute-start(bf16[3,128,128]{2,1,0:T(8,128)(2,1)S(1)} %get-tuple-element.59), channel_id=1, source_target_pairs={{0,6},{1,7},{2,4},{3,5},{4,2},{5,3},{6,0},{7,1},{8,14},{9,15},{10,... | collective-permute-start | bytes 294920 | tf_op jit(solution)/shard_map/ppermute | solution.py:295
  55.4 13.3 %collective-permute-start.14 = (bf16[3,128,128]{2,1,0:T(8,128)(2,1)S(1)}, bf16[3,128,128]{2,1,0:T(8,128)(2,1)S(1)}, u32[]{:S(2)}, u32[]{:S(2)}) collective-permute-start(bf16[3,128,128]{2,1,0:T(8,128)(2,1)S(1)} %get-tuple-element.64), channel_id=1, source_target_pairs={{0,11},{1,10},{2,9},{3,8},{4,15},{5,14},{6,13},{7,12},{8,3},{9,2},... | collective-permute-start | bytes 294920 | tf_op jit(solution)/shard_map/ppermute | solution.py:295
  59.7 9.9 %collective-permute-start.17 = (bf16[3,128,128]{2,1,0:T(8,128)(2,1)S(1)}, bf16[3,128,128]{2,1,0:T(8,128)(2,1)S(1)}, u32[]{:S(2)}, u32[]{:S(2)}) collective-permute-start(bf16[3,128,128]{2,1,0:T(8,128)(2,1)S(1)} %get-tuple-element.69), channel_id=1, source_target_pairs={{0,7},{1,6},{2,5},{3,4},{4,3},{5,2},{6,1},{7,0},{8,15},{9,14},{10,... | collective-permute-start | bytes 294920 | tf_op jit(solution)/shard_map/ppermute | solution.py:295
  61.1 9.7 %collective-permute-start.20 = (bf16[3,128,128]{2,1,0:T(8,128)(2,1)S(1)}, bf16[3,128,128]{2,1,0:T(8,128)(2,1)S(1)}, u32[]{:S(2)}, u32[]{:S(2)}) collective-permute-start(bf16[3,128,128]{2,1,0:T(8,128)(2,1)S(1)} %get-tuple-element.74), channel_id=1, source_target_pairs={{0,12},{1,13},{2,14},{3,15},{4,8},{5,9},{6,10},{7,11},{8,4},{9,5},... | collective-permute-start | bytes 294920 | tf_op jit(solution)/shard_map/ppermute | solution.py:295
  63.2 12.6 %collective-permute-start.8 = (bf16[3,128,128]{2,1,0:T(8,128)(2,1)S(1)}, bf16[3,128,128]{2,1,0:T(8,128)(2,1)S(1)}, u32[]{:S(2)}, u32[]{:S(2)}) collective-permute-start(bf16[3,128,128]{2,1,0:T(8,128)(2,1)S(1)} %get-tuple-element.54), channel_id=1, source_target_pairs={{0,2},{1,3},{2,0},{3,1},{4,6},{5,7},{6,4},{7,5},{8,10},{9,11},{10,... | collective-permute-start | bytes 294920 | tf_op jit(solution)/shard_map/ppermute | solution.py:295
  64.4 16.2 %collective-permute-start.10 = (bf16[3,128,128]{2,1,0:T(8,128)(2,1)S(1)}, bf16[3,128,128]{2,1,0:T(8,128)(2,1)S(1)}, u32[]{:S(2)}, u32[]{:S(2)}) collective-permute-start(bf16[3,128,128]{2,1,0:T(8,128)(2,1)S(1)} %get-tuple-element.57), channel_id=1, source_target_pairs={{0,13},{1,12},{2,15},{3,14},{4,9},{5,8},{6,11},{7,10},{8,5},{9,4},... | collective-permute-start | bytes 294920 | tf_op jit(solution)/shard_map/ppermute | solution.py:295
  68.6 12.0 %collective-permute-start.12 = (bf16[3,128,128]{2,1,0:T(8,128)(2,1)S(1)}, bf16[3,128,128]{2,1,0:T(8,128)(2,1)S(1)}, u32[]{:S(2)}, u32[]{:S(2)}) collective-permute-start(bf16[3,128,128]{2,1,0:T(8,128)(2,1)S(1)} %get-tuple-element.60), channel_id=1, source_target_pairs={{0,3},{1,2},{2,1},{3,0},{4,7},{5,6},{6,5},{7,4},{8,11},{9,10},{10,... | collective-permute-start | bytes 294920 | tf_op jit(solution)/shard_map/ppermute | solution.py:295
  69.7 12.8 %collective-permute-start.15 = (bf16[3,128,128]{2,1,0:T(8,128)(2,1)S(1)}, bf16[3,128,128]{2,1,0:T(8,128)(2,1)S(1)}, u32[]{:S(2)}, u32[]{:S(2)}) collective-permute-start(bf16[3,128,128]{2,1,0:T(8,128)(2,1)S(1)} %get-tuple-element.65), channel_id=1, source_target_pairs={{0,14},{1,15},{2,12},{3,13},{4,10},{5,11},{6,8},{7,9},{8,6},{9,7},... | collective-permute-start | bytes 294920 | tf_op jit(solution)/shard_map/ppermute | solution.py:295
  70.8 11.7 %collective-permute-start.18 = (bf16[3,128,128]{2,1,0:T(8,128)(2,1)S(1)}, bf16[3,128,128]{2,1,0:T(8,128)(2,1)S(1)}, u32[]{:S(2)}, u32[]{:S(2)}) collective-permute-start(bf16[3,128,128]{2,1,0:T(8,128)(2,1)S(1)} %get-tuple-element.70), channel_id=1, source_target_pairs={{0,1},{1,0},{2,3},{3,2},{4,5},{5,4},{6,7},{7,6},{8,9},{9,8},{10,11... | collective-permute-start | bytes 294920 | tf_op jit(solution)/shard_map/ppermute | solution.py:295
  75.8 8.8 %collective-permute-start.21 = (bf16[3,128,128]{2,1,0:T(8,128)(2,1)S(1)}, bf16[3,128,128]{2,1,0:T(8,128)(2,1)S(1)}, u32[]{:S(2)}, u32[]{:S(2)}) collective-permute-start(bf16[3,128,128]{2,1,0:T(8,128)(2,1)S(1)} %get-tuple-element.75), channel_id=1, source_target_pairs={{0,15},{1,14},{2,13},{3,12},{4,11},{5,10},{6,9},{7,8},{8,7},{9,6},... | collective-permute-start | bytes 294920 | tf_op jit(solution)/shard_map/ppermute | solution.py:295

commit v5 on v4

--- a/solution.py
+++ b/solution.py
@@ -12,6 +12,7 @@
 TILE = 32
 STEPS = 4
 WINDOW = 6
+LATE = 5
 
 
 def evaluate(points, theta):
@@ -224,10 +225,16 @@
     *out_refs, made_ref, turned_ref = refs
     count, _, chunk, width = sig_ref.shape
     tile = spec_ref.shape[1] // twist_ref.shape[0]
-    me = lax.axis_index("ctx")
-
-    @pl.loop(0, chunk // tile)
+    me, steps = lax.axis_index("ctx"), chunk // tile
+
+    def deliver(step):
+        lanes = rows_of(step, tile)
+        for k in range(count):
+            out_refs[k][:, lanes] = made_ref[k, :, lanes]
+
+    @pl.loop(0, steps)
     def _(step):
+        deliver(jnp.maximum(step - 1, 0))
         lanes = rows_of(step, tile)
         specs = []
         for which in range(2):
@@ -244,29 +251,67 @@
         )
         for which, (re, im) in enumerate(results):
             for b, part in enumerate(inverse(re, im, twist_ref, wave_ref)):
-                made_ref[b, which, lanes] = part.astype(jnp.bfloat16)
-
-    for k in range(count):
-        out_refs[k][...] = made_ref[me ^ k]
-
-
-def ungate_kernel(which_blocks, *refs):
-    *made, sems = refs[-5:]
-    outs = refs[-9:-5]
-    value_ref, key_ref, cot_ref = refs[:3]
+                made_ref[me ^ b, which, lanes] = part.astype(jnp.bfloat16)
+
+    deliver(steps - 1)
+
+
+def gates(operands, part_ref, made, rows):
+    value, key, cot = (operand.astype(jnp.float32) for operand in operands)
+    conv, grad, filt = (part_ref[which].astype(jnp.float32) for which in range(3))
+    made[0][rows] = (grad * key).astype(jnp.bfloat16)
+    made[1][rows] = (grad * value).astype(jnp.bfloat16)
+    made[2][rows] = (cot * conv).astype(jnp.bfloat16)
+    made[3][rows] = filt
+
+
+def send_rows(made, outs, rows, sems, i):
+    sends = [
+        pltpu.make_async_copy(source.at[rows], to.at[rows], sems.at[j, i])
+        for j, (source, to) in enumerate(zip(made, outs))
+    ]
+    for send in sends:
+        send.start()
+    return sends
+
+
+def first_gates(early, late, *refs):
+    operands, part_refs = refs[:3], refs[3 : 3 + len(early)]
+    *outs, late_ref = refs[3 + len(early) : 8 + len(early)]
+    held_ref, *made, loads, stores = refs[8 + len(early) :]
+    me = lax.axis_index("ctx")
+    copies = []
+    for i, k in enumerate(early + late):
+        rows = rows_of(me ^ k, part_refs[0].shape[1])
+        to = held_ref.at[i] if i < len(early) else late_ref.at[i - len(early)]
+        copies.append(
+            [
+                pltpu.make_async_copy(operand.at[rows], to.at[j], loads.at[j, i])
+                for j, operand in enumerate(operands)
+            ]
+        )
+        for copy in copies[-1]:
+            copy.start()
+    sends = []
+    for i, k in enumerate(early):
+        for copy in copies[i]:
+            copy.wait()
+        rows = rows_of(me ^ k, part_refs[0].shape[1])
+        gates([held_ref[i, j] for j in range(3)], part_refs[i], made, rows)
+        sends += send_rows(made, outs, rows, stores, i)
+    for copy in sum(copies[len(early) :], []) + sends:
+        copy.wait()
+
+
+def last_gates(late, held_ref, *refs):
+    part_refs, outs = refs[: len(late)], refs[len(late) + 4 : len(late) + 8]
+    *made, stores = refs[len(late) + 8 :]
     me = lax.axis_index("ctx")
     sends = []
-    for i, k in enumerate(which_blocks):
-        part_ref = refs[3 + i]
-        rows = rows_of(me ^ k, part_ref.shape[1])
-        conv, grad, filt = (part_ref[which].astype(jnp.float32) for which in range(3))
-        made[0][rows] = (grad * key_ref[rows].astype(jnp.float32)).astype(jnp.bfloat16)
-        made[1][rows] = (grad * value_ref[rows].astype(jnp.float32)).astype(jnp.bfloat16)
-        made[2][rows] = (cot_ref[rows].astype(jnp.float32) * conv).astype(jnp.bfloat16)
-        made[3][rows] = filt
-        for j, (source, to) in enumerate(zip(made, outs)):
-            sends.append(pltpu.make_async_copy(source.at[rows], to.at[rows], sems.at[j, i]))
-            sends[-1].start()
+    for i, k in enumerate(late):
+        rows = rows_of(me ^ k, part_refs[0].shape[1])
+        gates([held_ref[i, j] for j in range(3)], part_refs[i], made, rows)
+        sends += send_rows(made, outs, rows, stores, i)
     for send in sends:
         send.wait()
 
@@ -380,23 +425,33 @@
     half = jax.ShapeDtypeStruct((channels, width), jnp.bfloat16)
     wide = jax.ShapeDtypeStruct((channels, width), jnp.float32)
     order = [0] + partners(count)
-    early = max(count - WINDOW, 1)
-    outs = []
-    for blocks in (order[:early], order[early:]):
-        outs = pl.pallas_call(
-            functools.partial(ungate_kernel, blocks),
-            in_specs=[here] * (3 + len(blocks)) + [hbm] * len(outs),
-            out_specs=[hbm] * 4,
-            out_shape=[half, half, half, wide],
-            input_output_aliases={3 + len(blocks) + i: i for i in range(len(outs))},
-            scratch_shapes=[pltpu.VMEM((channels, width), jnp.bfloat16)] * 3
-            + [
-                pltpu.VMEM((channels, width), jnp.float32),
-                pltpu.SemaphoreType.DMA((4, len(blocks))),
-            ],
-            compiler_params=limit,
-        )(values, keys, grad_out, *[got[k] for k in blocks], *outs)
-    return outs
+    early, late = order[:-LATE], order[-LATE:]
+    made_scratch = [pltpu.VMEM((channels, width), jnp.bfloat16)] * 3 + [
+        pltpu.VMEM((channels, width), jnp.float32)
+    ]
+    *outs, operands = pl.pallas_call(
+        functools.partial(first_gates, early, late),
+        in_specs=[hbm] * 3 + [here] * len(early),
+        out_specs=[hbm] * 4 + [here],
+        out_shape=[half] * 3
+        + [wide, jax.ShapeDtypeStruct((len(late), 3, chunk, width), jnp.bfloat16)],
+        scratch_shapes=[
+            pltpu.VMEM((len(early), 3, chunk, width), jnp.bfloat16),
+            *made_scratch,
+            pltpu.SemaphoreType.DMA((3, count)),
+            pltpu.SemaphoreType.DMA((4, len(early))),
+        ],
+        compiler_params=pltpu.CompilerParams(vmem_limit_bytes=24 * 1024 * 1024),
+    )(values, keys, grad_out, *[got[k] for k in early])
+    return pl.pallas_call(
+        functools.partial(last_gates, late),
+        in_specs=[here] * (1 + len(late)) + [hbm] * 4,
+        out_specs=[hbm] * 4,
+        out_shape=[half] * 3 + [wide],
+        input_output_aliases={1 + len(late) + i: i for i in range(4)},
+        scratch_shapes=[*made_scratch, pltpu.SemaphoreType.DMA((4, len(late)))],
+        compiler_params=limit,
+    )(operands, *[got[k] for k in late], *outs)
 
 
 def solution(mesh):

time: 86.1 us -> 84.7 us (0.984)
  waiting for transfers between devices: 30.8 us -> 28 us
  Pallas kernels: 13.2 us -> 14.5 us
    ppermute x15, waiting for transfers between devices: 8.65 us -> 5.95 us  [spread(): got[k] = lax.ppermute(block, 'ctx', [(j, j ^ k) for j in range(count)])]
    pallas_call x2, Pallas kernels: 2.9 us -> 5.25 us  [the longest x1 4.19 us: shards(): pl.pallas_call(functools.partial(first_gates, early, late), in_specs=[hbm...]
    pallas_call x1, Pallas kernels: 6.34 us -> 5.31 us  [shards(): pl.pallas_call(spectral_kernel, in_specs=[here] * 4, out_specs=[here] * c...]
  transfers between devices with their start and end apart: 23 -> 23, of which waited for: 12 -> 11; matrix products, arithmetic and copies ran while one was open for 0% -> 0% of each run, Pallas kernels for 7% -> 10%
where the time goes in v5:
time: 84.7 us; the launch traced here: 84.5 us
  starting transfers between devices  39.8 us (47%)
  waiting for transfers between devices  28 us (33%)
  Pallas kernels  14.5 us (17%)
  local copies, waits for them, and re-layouts  1.22 us (1%)
  between operations  0.88 us (1%)
    ppermute x15, starting transfers between devices, spread(): got[k] = lax.ppermute(block, 'ctx', [(j, j ^ k) for j in range(count)])  26.3 us
    ppermute x7, waiting for transfers between devices, swap(): return lax.ppermute(block, axis, [(i, i ^ gap) for i in range(size)])  17.1 us
    all_to_all x1, starting transfers between devices, exchange(): return lax.all_to_all(parts, 'ctx', split_axis=0, concat_axis=0, tiled=True)  7.32 us
    ppermute x7, starting transfers between devices, swap(): return lax.ppermute(block, axis, [(i, i ^ gap) for i in range(size)])  6.2 us
    ppermute x15, waiting for transfers between devices, spread(): got[k] = lax.ppermute(block, 'ctx', [(j, j ^ k) for j in range(count)])  5.95 us
    pallas_call x1, Pallas kernels, shards(): pl.pallas_call(spectral_kernel, in_specs=[here] * 4, out_specs=[here] * c...  5.31 us
    all_to_all x1, waiting for transfers between devices, exchange(): return lax.all_to_all(parts, 'ctx', split_axis=0, concat_axis=0, tiled=True)  4.93 us
    pallas_call x1, Pallas kernels, shards(): pl.pallas_call(functools.partial(first_gates, early, late), in_specs=[hbm...  4.19 us
  transfers between devices with their start and end apart: 23, of which 11 were waited for; matrix products, arithmetic and copies ran while one was open for 0% of the time, Pallas kernels for 10%

profile of v5, /device:TPU:13, one launch (start us, length us, event | category | flops | bytes accessed | tf_op | source)
XLA Modules:
  0.0 84.5 jit_solution(8108343501838125813)
XLA Ops:
  0.7 1.1 %fusion.3 = (bf16[4,64,128]{2,1,0:T(8,128)(2,1)S(1)}, bf16[4,64,128]{2,1,0:T(8,128)(2,1)S(1)}, bf16[4,64,128]{2,1,0:T(8,128)(2,1)S(1)}, bf16[4,64,128]{2,1,0:T(8,128)(2,1)S(1)}) fusion(f32[4,4,2,64,128]{4,3,2,1,0:T(8,128)} %bitcast.30, s32[]{:T(128)S(6)} %select_n.106, s32[]{:T(128)S(6)} %select_n.100, s32[]{:T(128)S(6)} %select_n.104, s32[]{:T(128)S(6)} %select_n.102, ...), kind=kLoop, calls=%fused_computation.8 | loop fusion | bytes 524308 | tf_op jit(solution)/shard_map/convert_element_type | solution.py:363
  1.8 1.4 %collective-permute-start.2 = (bf16[4,64,128]{2,1,0:T(8,128)(2,1)S(1)}, bf16[4,64,128]{2,1,0:T(8,128)(2,1)S(1)}, u32[]{:S(2)}, u32[]{:S(2)}) collective-permute-start(bf16[4,64,128]{2,1,0:T(8,128)(2,1)S(1)} %get-tuple-element.92), channel_id=1, source_target_pairs={{0,12},{1,13},{2,14},{3,15},{4,8},{5,9},{6,10},{7,11},{8,4},{9,5},... | collective-permute-start | bytes 196616 | tf_op jit(solution)/shard_map/ppermute | solution.py:350
  3.2 1.1 %collective-permute-start.1 = (bf16[4,64,128]{2,1,0:T(8,128)(2,1)S(1)}, bf16[4,64,128]{2,1,0:T(8,128)(2,1)S(1)}, u32[]{:S(2)}, u32[]{:S(2)}) collective-permute-start(bf16[4,64,128]{2,1,0:T(8,128)(2,1)S(1)} %get-tuple-element.93), channel_id=1, source_target_pairs={{0,8},{1,9},{2,10},{3,11},{4,12},{5,13},{6,14},{7,15},{8,0},{9,1},... | collective-permute-start | bytes 196616 | tf_op jit(solution)/shard_map/ppermute | solution.py:350
  4.3 1.1 %collective-permute-start = (bf16[4,64,128]{2,1,0:T(8,128)(2,1)S(1)}, bf16[4,64,128]{2,1,0:T(8,128)(2,1)S(1)}, u32[]{:S(2)}, u32[]{:S(2)}) collective-permute-start(bf16[4,64,128]{2,1,0:T(8,128)(2,1)S(1)} %get-tuple-element.94), channel_id=1, source_target_pairs={{0,4},{1,5},{2,6},{3,7},{4,0},{5,1},{6,2},{7,3},{8,12},{9,13},{10,... | collective-permute-start | bytes 196616 | tf_op jit(solution)/shard_map/ppermute | solution.py:350
  5.4 2.5 %shard_map.102 = bf16[16,2,128,128]{3,2,1,0:T(8,128)(2,1)} custom-call(bf16[2048,128]{1,0:T(8,128)(2,1)} %refs_0_.1, bf16[2048,128]{1,0:T(8,128)(2,1)} %refs_1_.1, bf16[2048,128]{1,0:T(8,128)(2,1)} %refs_2_.1, bf16[2048,128]{1,0:T(8,128)(2,1)} %query_hbm.1), custom_call_target="tpu_custom_call" | custom-call | tf_op jit(solution)/shard_map/pallas_call | solution.py:384
  8.0 1.5 %collective-permute-done = bf16[4,64,128]{2,1,0:T(8,128)(2,1)S(1)} collective-permute-done((bf16[4,64,128]{2,1,0:T(8,128)(2,1)S(1)}, bf16[4,64,128]{2,1,0:T(8,128)(2,1)S(1)}, u32[]{:S(2)}, u32[]{:S(2)}) %collective-permute-start) | collective-permute-done | bytes 65568 | tf_op jit(solution)/shard_map/ppermute | solution.py:350
  9.5 7.3 %all-to-all-start = ((bf16[16,2,128,128]{3,2,1,0:T(8,128)(2,1)}), bf16[16,2,128,128]{3,2,1,0:T(8,128)(2,1)S(1)}, u32[]{:S(2)}, u32[]{:S(2)}) async-start(bf16[16,2,128,128]{3,2,1,0:T(8,128)(2,1)} %shard_map.102), calls=%async_computation | async-start | bytes 2097152 | tf_op jit(solution)/shard_map/all_to_all | solution.py:345
  17.4 1.2 %collective-permute-start.4 = (bf16[4,64,128]{2,1,0:T(8,128)(2,1)S(1)}, bf16[4,64,128]{2,1,0:T(8,128)(2,1)S(1)}, u32[]{:S(2)}, u32[]{:S(2)}) collective-permute-start(bf16[4,64,128]{2,1,0:T(8,128)(2,1)S(1)} %pad_maximum_fusion.2), channel_id=1, source_target_pairs={{0,2},{1,3},{2,0},{3,1},{4,6},{5,7},{6,4},{7,5},{8,10},{9,11},{10,... | collective-permute-start | bytes 196616 | tf_op jit(solution)/shard_map/ppermute | solution.py:350
  19.3 5.1 %collective-permute-done.4 = bf16[4,64,128]{2,1,0:T(8,128)(2,1)S(1)} collective-permute-done((bf16[4,64,128]{2,1,0:T(8,128)(2,1)S(1)}, bf16[4,64,128]{2,1,0:T(8,128)(2,1)S(1)}, u32[]{:S(2)}, u32[]{:S(2)}) %collective-permute-start.4) | collective-permute-done | bytes 65568 | tf_op jit(solution)/shard_map/ppermute | solution.py:350
  24.5 2.4 %collective-permute-done.5 = bf16[4,64,128]{2,1,0:T(8,128)(2,1)S(1)} collective-permute-done((bf16[4,64,128]{2,1,0:T(8,128)(2,1)S(1)}, bf16[4,64,128]{2,1,0:T(8,128)(2,1)S(1)}, u32[]{:S(2)}, u32[]{:S(2)}) %collective-permute-start.5) | collective-permute-done | bytes 65568 | tf_op jit(solution)/shard_map/ppermute | solution.py:350
  27.2 8.0 %collective-permute-done.6.other_ref = bf16[4,4,64,128]{3,2,1,0:T(8,128)(2,1)S(1)} collective-permute-done((bf16[4,4,64,128]{3,2,1,0:T(8,128)(2,1)S(1)}, bf16[4,4,64,128]{3,2,1,0:T(8,128)(2,1)S(1)}, u32[]{:S(2)}, u32[]{:S(2)}) %collective-permute-start.6) | collective-permute-done | bytes 262176 | tf_op jit(solution)/shard_map/ppermute | solution.py:350
  35.3 1.4 %shard_map.103.spec_ref = bf16[4,544,256]{2,1,0:T(8,128)(2,1)S(1)} custom-call(bf16[4,4,64,128]{3,2,1,0:T(8,128)(2,1)S(1)} %pad_maximum_fusion.mine_ref, bf16[4,4,64,128]{3,2,1,0:T(8,128)(2,1)S(1)} %collective-permute-done.6.other_ref, f32[17,4,128]{2,1,0:T(4,128)S(1)} %copy-done.4, bf16[2,256,256]{2,1,0:T(8,128)(2,1)S(1)} %copy-done.3), custom_call_target="tpu_custom_call" | custom-call | flops 268435456 | bytes 1048576 | tf_op jit(solution)/shard_map/pallas_call | solution.py:401
  36.7 4.9 %all-to-all-done.sig_ref = bf16[16,2,128,128]{3,2,1,0:T(8,128)(2,1)S(1)} async-done(((bf16[16,2,128,128]{3,2,1,0:T(8,128)(2,1)}), bf16[16,2,128,128]{3,2,1,0:T(8,128)(2,1)S(1)}, u32[]{:S(2)}, u32[]{:S(2)}) %all-to-all-start) | async-done | bytes 1048608 | tf_op jit(solution)/shard_map/all_to_all | solution.py:345
  41.7 5.3 %shard_map.104 = (bf16[3,128,128]{2,1,0:T(8,128)(2,1)S(1)}, bf16[3,128,128]{2,1,0:T(8,128)(2,1)S(1)}, bf16[3,128,128]{2,1,0:T(8,128)(2,1)S(1)}, bf16[3,128,128]{...) custom-call(bf16[16,2,128,128]{3,2,1,0:T(8,128)(2,1)S(1)} %all-to-al, ...), custom_call_target="tpu_custom_call" | custom-call | tf_op jit(solution)/shard_map/pallas_call | solution.py:413
  47.4 1.8 %collective-permute-start.8 = (bf16[3,128,128]{2,1,0:T(8,128)(2,1)S(1)}, bf16[3,128,128]{2,1,0:T(8,128)(2,1)S(1)}, u32[]{:S(2)}, u32[]{:S(2)}) collective-permute-start(bf16[3,128,128]{2,1,0:T(8,128)(2,1)S(1)} %get-tuple-element.58), channel_id=1, source_target_pairs={{0,4},{1,5},{2,6},{3,7},{4,0},{5,1},{6,2},{7,3},{8,12},{9,13},{10,... | collective-permute-start | bytes 294920 | tf_op jit(solution)/shard_map/ppermute | solution.py:340
  49.2 1.1 %collective-permute-start.9 = (bf16[3,128,128]{2,1,0:T(8,128)(2,1)S(1)}, bf16[3,128,128]{2,1,0:T(8,128)(2,1)S(1)}, u32[]{:S(2)}, u32[]{:S(2)}) collective-permute-start(bf16[3,128,128]{2,1,0:T(8,128)(2,1)S(1)} %get-tuple-element.61), channel_id=1, source_target_pairs={{0,9},{1,8},{2,11},{3,10},{4,13},{5,12},{6,15},{7,14},{8,1},{9,0},... | collective-permute-start | bytes 294920 | tf_op jit(solution)/shard_map/ppermute | solution.py:340
  50.3 0.8 collective-permute-start.10
  51.1 2.1 %collective-permute-start.11 = (bf16[3,128,128]{2,1,0:T(8,128)(2,1)S(1)}, bf16[3,128,128]{2,1,0:T(8,128)(2,1)S(1)}, u32[]{:S(2)}, u32[]{:S(2)}) collective-permute-start(bf16[3,128,128]{2,1,0:T(8,128)(2,1)S(1)} %get-tuple-element.67), channel_id=1, source_target_pairs={{0,10},{1,11},{2,8},{3,9},{4,14},{5,15},{6,12},{7,13},{8,2},{9,3},... | collective-permute-start | bytes 294920 | tf_op jit(solution)/shard_map/ppermute | solution.py:340
  53.3 1.0 %collective-permute-start.12 = (bf16[3,128,128]{2,1,0:T(8,128)(2,1)S(1)}, bf16[3,128,128]{2,1,0:T(8,128)(2,1)S(1)}, u32[]{:S(2)}, u32[]{:S(2)}) collective-permute-start(bf16[3,128,128]{2,1,0:T(8,128)(2,1)S(1)} %get-tuple-element.70), channel_id=1, source_target_pairs={{0,6},{1,7},{2,4},{3,5},{4,2},{5,3},{6,0},{7,1},{8,14},{9,15},{10,... | collective-permute-start | bytes 294920 | tf_op jit(solution)/shard_map/ppermute | solution.py:340
  54.2 4.3 %collective-permute-start.13 = (bf16[3,128,128]{2,1,0:T(8,128)(2,1)S(1)}, bf16[3,128,128]{2,1,0:T(8,128)(2,1)S(1)}, u32[]{:S(2)}, u32[]{:S(2)}) collective-permute-start(bf16[3,128,128]{2,1,0:T(8,128)(2,1)S(1)} %get-tuple-element.73), channel_id=1, source_target_pairs={{0,11},{1,10},{2,9},{3,8},{4,15},{5,14},{6,13},{7,12},{8,3},{9,2},... | collective-permute-start | bytes 294920 | tf_op jit(solution)/shard_map/ppermute | solution.py:340
  58.6 0.8 collective-permute-start.14
  60.5 1.5 %collective-permute-done.11.refs_8_ = bf16[3,128,128]{2,1,0:T(8,128)(2,1)S(1)} collective-permute-done((bf16[3,128,128]{2,1,0:T(8,128)(2,1)S(1)}, bf16[3,128,128]{2,1,0:T(8,128)(2,1)S(1)}, u32[]{:S(2)}, u32[]{:S(2)}) %collective-permute-start.11) | collective-permute-done | bytes 98336 | tf_op jit(solution)/shard_map/ppermute | solution.py:340
  62.0 0.8 collective-permute-start.16
  63.2 3.2 %collective-permute-start.17 = (bf16[3,128,128]{2,1,0:T(8,128)(2,1)S(1)}, bf16[3,128,128]{2,1,0:T(8,128)(2,1)S(1)}, u32[]{:S(2)}, u32[]{:S(2)}) collective-permute-start(bf16[3,128,128]{2,1,0:T(8,128)(2,1)S(1)} %get-tuple-element.83), channel_id=1, source_target_pairs={{0,13},{1,12},{2,15},{3,14},{4,9},{5,8},{6,11},{7,10},{8,5},{9,4},... | collective-permute-start | bytes 294920 | tf_op jit(solution)/shard_map/ppermute | solution.py:340
  66.3 1.1 %collective-permute-done.13.refs_10_ = bf16[3,128,128]{2,1,0:T(8,128)(2,1)S(1)} collective-permute-done((bf16[3,128,128]{2,1,0:T(8,128)(2,1)S(1)}, bf16[3,128,128]{2,1,0:T(8,128)(2,1)S(1)}, u32[]{:S(2)}, u32[]{:S(2)}) %collective-permute-start.13) | collective-permute-done | bytes 98336 | tf_op jit(solution)/shard_map/ppermute | solution.py:340
  67.5 1.0 %collective-permute-start.18 = (bf16[3,128,128]{2,1,0:T(8,128)(2,1)S(1)}, bf16[3,128,128]{2,1,0:T(8,128)(2,1)S(1)}, u32[]{:S(2)}, u32[]{:S(2)}) collective-permute-start(bf16[3,128,128]{2,1,0:T(8,128)(2,1)S(1)} %get-tuple-element.84), channel_id=1, source_target_pairs={{0,3},{1,2},{2,1},{3,0},{4,7},{5,6},{6,5},{7,4},{8,11},{9,10},{10,... | collective-permute-start | bytes 294920 | tf_op jit(solution)/shard_map/ppermute | solution.py:340
  68.5 1.1 %collective-permute-start.19 = (bf16[3,128,128]{2,1,0:T(8,128)(2,1)S(1)}, bf16[3,128,128]{2,1,0:T(8,128)(2,1)S(1)}, u32[]{:S(2)}, u32[]{:S(2)}) collective-permute-start(bf16[3,128,128]{2,1,0:T(8,128)(2,1)S(1)} %get-tuple-element.85), channel_id=1, source_target_pairs={{0,14},{1,15},{2,12},{3,13},{4,10},{5,11},{6,8},{7,9},{8,6},{9,7},... | collective-permute-start | bytes 294920 | tf_op jit(solution)/shard_map/ppermute | solution.py:340
  69.6 6.1 %collective-permute-start.20 = (bf16[3,128,128]{2,1,0:T(8,128)(2,1)S(1)}, bf16[3,128,128]{2,1,0:T(8,128)(2,1)S(1)}, u32[]{:S(2)}, u32[]{:S(2)}) collective-permute-start(bf16[3,128,128]{2,1,0:T(8,128)(2,1)S(1)} %get-tuple-element.86), channel_id=1, source_target_pairs={{0,1},{1,0},{2,3},{3,2},{4,5},{5,4},{6,7},{7,6},{8,9},{9,8},{10,11... | collective-permute-start | bytes 294920 | tf_op jit(solution)/shard_map/ppermute | solution.py:340
  75.7 1.1 %collective-permute-start.21 = (bf16[3,128,128]{2,1,0:T(8,128)(2,1)S(1)}, bf16[3,128,128]{2,1,0:T(8,128)(2,1)S(1)}, u32[]{:S(2)}, u32[]{:S(2)}) collective-permute-start(bf16[3,128,128]{2,1,0:T(8,128)(2,1)S(1)} %get-tuple-element.87), channel_id=1, source_target_pairs={{0,15},{1,14},{2,13},{3,12},{4,11},{5,10},{6,9},{7,8},{8,7},{9,6},... | collective-permute-start | bytes 294920 | tf_op jit(solution)/shard_map/ppermute | solution.py:340
  76.8 4.2 %shard_map.105 = (bf16[2048,128]{1,0:T(8,128)(2,1)}, bf16[2048,128]{1,0:T(8,128)(2,1)}, bf16[2048,128]{1,0:T(8,128)(2,1)}, f32[2048,128]{1,0:T(8,128)}, bf16[5,3,128,128]{3,2,1,0:T(8,128)(2,1)S(1)}) custom-call(bf16[2048,128]{1,0:T(8,128)(2,1)S(1)} %copy-done, bf16[2048,128]{1,0:T(8,128)(2,1)S(1)} %copy-done.1, bf16[2048,128]{1,0:T(8,128)(2,1)S(1)} %copy-done.2, ...), custom_call_target="tpu_custom_call" | custom-call | tf_op jit(solution)/shard_map/pallas_call | solution.py:432
  81.3 2.1 %collective-permute-done.21.refs_4_ = bf16[3,128,128]{2,1,0:T(8,128)(2,1)S(1)} collective-permute-done((bf16[3,128,128]{2,1,0:T(8,128)(2,1)S(1)}, bf16[3,128,128]{2,1,0:T(8,128)(2,1)S(1)}, u32[]{:S(2)}, u32[]{:S(2)}) %collective-permute-start.21) | collective-permute-done | bytes 98336 | tf_op jit(solution)/shard_map/ppermute | solution.py:340
  83.4 1.1 %shard_map.106 = (bf16[2048,128]{1,0:T(8,128)(2,1)}, bf16[2048,128]{1,0:T(8,128)(2,1)}, bf16[2048,128]{1,0:T(8,128)(2,1)}, f32[2048,128]{1,0:T(8,128)}) custom-call(bf16[5,3,128,128]{3,2,1,0:T(8,128)(2,1)S(1)} %get-tuple-element.82.held_ref, ...), custom_call_target="tpu_custom_call", output_to_operand_aliasing={{0}: (6, {}), {1}: (7, {}), {2}: (8, {}), {3}: (9, {})} | custom-call | tf_op jit(solution)/shard_map/pallas_call | solution.py:446
  (37 shorter events, 3.8 us)
Async XLA Ops:
  1.8 6.1 %collective-permute-start.2 = (bf16[4,64,128]{2,1,0:T(8,128)(2,1)S(1)}, bf16[4,64,128]{2,1,0:T(8,128)(2,1)S(1)}, u32[]{:S(2)}, u32[]{:S(2)}) collective-permute-start(bf16[4,64,128]{2,1,0:T(8,128)(2,1)S(1)} %get-tuple-element.92), channel_id=1, source_target_pairs={{0,12},{1,13},{2,14},{3,15},{4,8},{5,9},{6,10},{7,11},{8,4},{9,5},... | collective-permute-start | bytes 196616 | tf_op jit(solution)/shard_map/ppermute | solution.py:350
  3.2 4.8 %collective-permute-start.1 = (bf16[4,64,128]{2,1,0:T(8,128)(2,1)S(1)}, bf16[4,64,128]{2,1,0:T(8,128)(2,1)S(1)}, u32[]{:S(2)}, u32[]{:S(2)}) collective-permute-start(bf16[4,64,128]{2,1,0:T(8,128)(2,1)S(1)} %get-tuple-element.93), channel_id=1, source_target_pairs={{0,8},{1,9},{2,10},{3,11},{4,12},{5,13},{6,14},{7,15},{8,0},{9,1},... | collective-permute-start | bytes 196616 | tf_op jit(solution)/shard_map/ppermute | solution.py:350
  4.3 5.2 %collective-permute-start = (bf16[4,64,128]{2,1,0:T(8,128)(2,1)S(1)}, bf16[4,64,128]{2,1,0:T(8,128)(2,1)S(1)}, u32[]{:S(2)}, u32[]{:S(2)}) collective-permute-start(bf16[4,64,128]{2,1,0:T(8,128)(2,1)S(1)} %get-tuple-element.94), channel_id=1, source_target_pairs={{0,4},{1,5},{2,6},{3,7},{4,0},{5,1},{6,2},{7,3},{8,12},{9,13},{10,... | collective-permute-start | bytes 196616 | tf_op jit(solution)/shard_map/ppermute | solution.py:350
  9.5 32.2 %all-to-all-start = ((bf16[16,2,128,128]{3,2,1,0:T(8,128)(2,1)}), bf16[16,2,128,128]{3,2,1,0:T(8,128)(2,1)S(1)}, u32[]{:S(2)}, u32[]{:S(2)}) async-start(bf16[16,2,128,128]{3,2,1,0:T(8,128)(2,1)} %shard_map.102), calls=%async_computation | async-start | bytes 2097152 | tf_op jit(solution)/shard_map/all_to_all | solution.py:345
  16.8 18.5 %copy-start.3 = (bf16[2,256,256]{2,1,0:T(8,128)(2,1)S(1)}, bf16[2,256,256]{2,1,0:T(8,128)(2,1)}, u32[]{:S(2)}) copy-start(bf16[2,256,256]{2,1,0:T(8,128)(2,1)} %constant.222.clone.wave_ref) | copy-start | bytes 786436
  16.8 18.5 %copy-start.4 = (f32[17,4,128]{2,1,0:T(4,128)S(1)}, f32[17,4,128]{2,1,0:T(4,128)}, u32[]{:S(2)}) copy-start(f32[17,4,128]{2,1,0:T(4,128)} %constant.223.clone.twist_ref) | copy-start | bytes 104452
  16.9 2.4 %collective-permute-start.3 = (bf16[4,64,128]{2,1,0:T(8,128)(2,1)S(1)}, bf16[4,64,128]{2,1,0:T(8,128)(2,1)S(1)}, u32[]{:S(2)}, u32[]{:S(2)}) collective-permute-start(bf16[4,64,128]{2,1,0:T(8,128)(2,1)S(1)} %pad_maximum_fusion.1), channel_id=1, source_target_pairs={{0,1},{1,0},{2,3},{3,2},{4,5},{5,4},{6,7},{7,6},{8,9},{9,8},{10,11... | collective-permute-start | bytes 196616 | tf_op jit(solution)/shard_map/ppermute | solution.py:350
  17.4 7.1 %collective-permute-start.4 = (bf16[4,64,128]{2,1,0:T(8,128)(2,1)S(1)}, bf16[4,64,128]{2,1,0:T(8,128)(2,1)S(1)}, u32[]{:S(2)}, u32[]{:S(2)}) collective-permute-start(bf16[4,64,128]{2,1,0:T(8,128)(2,1)S(1)} %pad_maximum_fusion.2), channel_id=1, source_target_pairs={{0,2},{1,3},{2,0},{3,1},{4,6},{5,7},{6,4},{7,5},{8,10},{9,11},{10,... | collective-permute-start | bytes 196616 | tf_op jit(solution)/shard_map/ppermute | solution.py:350
  18.6 8.2 %collective-permute-start.5 = (bf16[4,64,128]{2,1,0:T(8,128)(2,1)S(1)}, bf16[4,64,128]{2,1,0:T(8,128)(2,1)S(1)}, u32[]{:S(2)}, u32[]{:S(2)}) collective-permute-start(bf16[4,64,128]{2,1,0:T(8,128)(2,1)S(1)} %pad_maximum_fusion.3), channel_id=1, source_target_pairs={{0,3},{1,2},{2,1},{3,0},{4,7},{5,6},{6,5},{7,4},{8,11},{9,10},{10,... | collective-permute-start | bytes 196616 | tf_op jit(solution)/shard_map/ppermute | solution.py:350
  26.9 8.3 %collective-permute-start.6 = (bf16[4,4,64,128]{3,2,1,0:T(8,128)(2,1)S(1)}, bf16[4,4,64,128]{3,2,1,0:T(8,128)(2,1)S(1)}, u32[]{:S(2)}, u32[]{:S(2)}) collective-permute-start(bf16[4,4,64,128]{3,2,1,0:T(8,128)(2,1)S(1)} %pad_maximum_fusion.mine_ref), channel_id=1, source_target_pairs={{0,16},{16,0},{1,17},{17,1},{2,18},{18,2},{3,19},{19,3},{4,20},{20... | collective-permute-start | bytes 786440 | tf_op jit(solution)/shard_map/ppermute | solution.py:350
  36.7 40.1 %copy-start = (bf16[2048,128]{1,0:T(8,128)(2,1)S(1)}, bf16[2048,128]{1,0:T(8,128)(2,1)}, u32[]{:S(2)}) copy-start(bf16[2048,128]{1,0:T(8,128)(2,1)} %refs_0_.1) | copy-start | bytes 1572868
  36.7 40.1 %copy-start.1 = (bf16[2048,128]{1,0:T(8,128)(2,1)S(1)}, bf16[2048,128]{1,0:T(8,128)(2,1)}, u32[]{:S(2)}) copy-start(bf16[2048,128]{1,0:T(8,128)(2,1)} %refs_1_.1) | copy-start | bytes 1572868
  41.7 35.2 %copy-start.2 = (bf16[2048,128]{1,0:T(8,128)(2,1)S(1)}, bf16[2048,128]{1,0:T(8,128)(2,1)}, u32[]{:S(2)}) copy-start(bf16[2048,128]{1,0:T(8,128)(2,1)} %refs_2_.1) | copy-start | bytes 1572868
  47.0 6.3 %collective-permute-start.7 = (bf16[3,128,128]{2,1,0:T(8,128)(2,1)S(1)}, bf16[3,128,128]{2,1,0:T(8,128)(2,1)S(1)}, u32[]{:S(2)}, u32[]{:S(2)}) collective-permute-start(bf16[3,128,128]{2,1,0:T(8,128)(2,1)S(1)} %get-tuple-element.55), channel_id=1, source_target_pairs={{0,8},{1,9},{2,10},{3,11},{4,12},{5,13},{6,14},{7,15},{8,0},{9,1},... | collective-permute-start | bytes 294920 | tf_op jit(solution)/shard_map/ppermute | solution.py:340
  47.4 6.8 %collective-permute-start.8 = (bf16[3,128,128]{2,1,0:T(8,128)(2,1)S(1)}, bf16[3,128,128]{2,1,0:T(8,128)(2,1)S(1)}, u32[]{:S(2)}, u32[]{:S(2)}) collective-permute-start(bf16[3,128,128]{2,1,0:T(8,128)(2,1)S(1)} %get-tuple-element.58), channel_id=1, source_target_pairs={{0,4},{1,5},{2,6},{3,7},{4,0},{5,1},{6,2},{7,3},{8,12},{9,13},{10,... | collective-permute-start | bytes 294920 | tf_op jit(solution)/shard_map/ppermute | solution.py:340
  49.2 9.3 %collective-permute-start.9 = (bf16[3,128,128]{2,1,0:T(8,128)(2,1)S(1)}, bf16[3,128,128]{2,1,0:T(8,128)(2,1)S(1)}, u32[]{:S(2)}, u32[]{:S(2)}) collective-permute-start(bf16[3,128,128]{2,1,0:T(8,128)(2,1)S(1)} %get-tuple-element.61), channel_id=1, source_target_pairs={{0,9},{1,8},{2,11},{3,10},{4,13},{5,12},{6,15},{7,14},{8,1},{9,0},... | collective-permute-start | bytes 294920 | tf_op jit(solution)/shard_map/ppermute | solution.py:340
  50.3 9.6 %collective-permute-start.10 = (bf16[3,128,128]{2,1,0:T(8,128)(2,1)S(1)}, bf16[3,128,128]{2,1,0:T(8,128)(2,1)S(1)}, u32[]{:S(2)}, u32[]{:S(2)}) collective-permute-start(bf16[3,128,128]{2,1,0:T(8,128)(2,1)S(1)} %get-tuple-element.64), channel_id=1, source_target_pairs={{0,5},{1,4},{2,7},{3,6},{4,1},{5,0},{6,3},{7,2},{8,13},{9,12},{10,... | collective-permute-start | bytes 294920 | tf_op jit(solution)/shard_map/ppermute | solution.py:340
  51.1 10.9 %collective-permute-start.11 = (bf16[3,128,128]{2,1,0:T(8,128)(2,1)S(1)}, bf16[3,128,128]{2,1,0:T(8,128)(2,1)S(1)}, u32[]{:S(2)}, u32[]{:S(2)}) collective-permute-start(bf16[3,128,128]{2,1,0:T(8,128)(2,1)S(1)} %get-tuple-element.67), channel_id=1, source_target_pairs={{0,10},{1,11},{2,8},{3,9},{4,14},{5,15},{6,12},{7,13},{8,2},{9,3},... | collective-permute-start | bytes 294920 | tf_op jit(solution)/shard_map/ppermute | solution.py:340
  53.3 9.9 %collective-permute-start.12 = (bf16[3,128,128]{2,1,0:T(8,128)(2,1)S(1)}, bf16[3,128,128]{2,1,0:T(8,128)(2,1)S(1)}, u32[]{:S(2)}, u32[]{:S(2)}) collective-permute-start(bf16[3,128,128]{2,1,0:T(8,128)(2,1)S(1)} %get-tuple-element.70), channel_id=1, source_target_pairs={{0,6},{1,7},{2,4},{3,5},{4,2},{5,3},{6,0},{7,1},{8,14},{9,15},{10,... | collective-permute-start | bytes 294920 | tf_op jit(solution)/shard_map/ppermute | solution.py:340
  54.2 13.2 %collective-permute-start.13 = (bf16[3,128,128]{2,1,0:T(8,128)(2,1)S(1)}, bf16[3,128,128]{2,1,0:T(8,128)(2,1)S(1)}, u32[]{:S(2)}, u32[]{:S(2)}) collective-permute-start(bf16[3,128,128]{2,1,0:T(8,128)(2,1)S(1)} %get-tuple-element.73), channel_id=1, source_target_pairs={{0,11},{1,10},{2,9},{3,8},{4,15},{5,14},{6,13},{7,12},{8,3},{9,2},... | collective-permute-start | bytes 294920 | tf_op jit(solution)/shard_map/ppermute | solution.py:340
  58.6 10.0 %collective-permute-start.14 = (bf16[3,128,128]{2,1,0:T(8,128)(2,1)S(1)}, bf16[3,128,128]{2,1,0:T(8,128)(2,1)S(1)}, u32[]{:S(2)}, u32[]{:S(2)}) collective-permute-start(bf16[3,128,128]{2,1,0:T(8,128)(2,1)S(1)} %get-tuple-element.76), channel_id=1, source_target_pairs={{0,7},{1,6},{2,5},{3,4},{4,3},{5,2},{6,1},{7,0},{8,15},{9,14},{10,... | collective-permute-start | bytes 294920 | tf_op jit(solution)/shard_map/ppermute | solution.py:340
  60.0 9.7 %collective-permute-start.15 = (bf16[3,128,128]{2,1,0:T(8,128)(2,1)S(1)}, bf16[3,128,128]{2,1,0:T(8,128)(2,1)S(1)}, u32[]{:S(2)}, u32[]{:S(2)}) collective-permute-start(bf16[3,128,128]{2,1,0:T(8,128)(2,1)S(1)} %get-tuple-element.79), channel_id=1, source_target_pairs={{0,12},{1,13},{2,14},{3,15},{4,8},{5,9},{6,10},{7,11},{8,4},{9,5},... | collective-permute-start | bytes 294920 | tf_op jit(solution)/shard_map/ppermute | solution.py:340
  62.0 13.7 %collective-permute-start.16 = (bf16[3,128,128]{2,1,0:T(8,128)(2,1)S(1)}, bf16[3,128,128]{2,1,0:T(8,128)(2,1)S(1)}, u32[]{:S(2)}, u32[]{:S(2)}) collective-permute-start(bf16[3,128,128]{2,1,0:T(8,128)(2,1)S(1)} %get-tuple-element.81), channel_id=1, source_target_pairs={{0,2},{1,3},{2,0},{3,1},{4,6},{5,7},{6,4},{7,5},{8,10},{9,11},{10,... | collective-permute-start | bytes 294920 | tf_op jit(solution)/shard_map/ppermute | solution.py:340
  63.2 17.9 %collective-permute-start.17 = (bf16[3,128,128]{2,1,0:T(8,128)(2,1)S(1)}, bf16[3,128,128]{2,1,0:T(8,128)(2,1)S(1)}, u32[]{:S(2)}, u32[]{:S(2)}) collective-permute-start(bf16[3,128,128]{2,1,0:T(8,128)(2,1)S(1)} %get-tuple-element.83), channel_id=1, source_target_pairs={{0,13},{1,12},{2,15},{3,14},{4,9},{5,8},{6,11},{7,10},{8,5},{9,4},... | collective-permute-start | bytes 294920 | tf_op jit(solution)/shard_map/ppermute | solution.py:340
  67.5 13.6 %collective-permute-start.18 = (bf16[3,128,128]{2,1,0:T(8,128)(2,1)S(1)}, bf16[3,128,128]{2,1,0:T(8,128)(2,1)S(1)}, u32[]{:S(2)}, u32[]{:S(2)}) collective-permute-start(bf16[3,128,128]{2,1,0:T(8,128)(2,1)S(1)} %get-tuple-element.84), channel_id=1, source_target_pairs={{0,3},{1,2},{2,1},{3,0},{4,7},{5,6},{6,5},{7,4},{8,11},{9,10},{10,... | collective-permute-start | bytes 294920 | tf_op jit(solution)/shard_map/ppermute | solution.py:340
  68.5 12.8 %collective-permute-start.19 = (bf16[3,128,128]{2,1,0:T(8,128)(2,1)S(1)}, bf16[3,128,128]{2,1,0:T(8,128)(2,1)S(1)}, u32[]{:S(2)}, u32[]{:S(2)}) collective-permute-start(bf16[3,128,128]{2,1,0:T(8,128)(2,1)S(1)} %get-tuple-element.85), channel_id=1, source_target_pairs={{0,14},{1,15},{2,12},{3,13},{4,10},{5,11},{6,8},{7,9},{8,6},{9,7},... | collective-permute-start | bytes 294920 | tf_op jit(solution)/shard_map/ppermute | solution.py:340
  69.6 11.7 %collective-permute-start.20 = (bf16[3,128,128]{2,1,0:T(8,128)(2,1)S(1)}, bf16[3,128,128]{2,1,0:T(8,128)(2,1)S(1)}, u32[]{:S(2)}, u32[]{:S(2)}) collective-permute-start(bf16[3,128,128]{2,1,0:T(8,128)(2,1)S(1)} %get-tuple-element.86), channel_id=1, source_target_pairs={{0,1},{1,0},{2,3},{3,2},{4,5},{5,4},{6,7},{7,6},{8,9},{9,8},{10,11... | collective-permute-start | bytes 294920 | tf_op jit(solution)/shard_map/ppermute | solution.py:340
  75.7 7.7 %collective-permute-start.21 = (bf16[3,128,128]{2,1,0:T(8,128)(2,1)S(1)}, bf16[3,128,128]{2,1,0:T(8,128)(2,1)S(1)}, u32[]{:S(2)}, u32[]{:S(2)}) collective-permute-start(bf16[3,128,128]{2,1,0:T(8,128)(2,1)S(1)} %get-tuple-element.87), channel_id=1, source_target_pairs={{0,15},{1,14},{2,13},{3,12},{4,11},{5,10},{6,9},{7,8},{8,7},{9,6},... | collective-permute-start | bytes 294920 | tf_op jit(solution)/shard_map/ppermute | solution.py:340

commit v6 on v5

--- a/solution.py
+++ b/solution.py
@@ -9,7 +9,8 @@
 from jax.experimental.pallas import tpu as pltpu
 from jax.sharding import PartitionSpec as P
 
-TILE = 32
+TILE = 16
+GROUP = 4
 STEPS = 4
 WINDOW = 6
 LATE = 5
@@ -97,7 +98,7 @@
     return [0.0, math.pi] + sum((odd(n) for n in reversed(sizes)), [])
 
 
-def make_tables(count, width):
+def make_tables(count, width, tile):
     angles = np.array(short_angles(count))
     turn = np.outer(angles, np.arange(width)) / width
     scale = np.where(np.arange(len(angles)) < 2, 1.0, 2.0)[:, None] / (2 * count * width)
@@ -107,7 +108,18 @@
     wave = np.outer(np.arange(width), np.arange(width)) % width * (2 * math.pi / width)
     c, s = np.cos(wave), np.sin(wave)
     ahead = np.block([[c, -s], [s, c]])
-    return twist, jnp.asarray(np.stack([ahead, ahead.T]), jnp.bfloat16)
+    short = np.zeros((2, 1, 1))
+    if on_matrix_unit(count, tile):
+        turn = np.outer(angles, np.arange(count))
+        parts = np.stack([np.cos(turn), -np.sin(turn)], axis=1)
+        parts = np.concatenate([parts[:2, 0], parts[2:].reshape(-1, count)])
+        short = np.kron(parts, np.eye(tile)).reshape(2, count * tile, count * tile)
+    waves = np.stack([ahead, ahead.T])
+    return twist, jnp.asarray(waves, jnp.bfloat16), jnp.asarray(short, jnp.bfloat16)
+
+
+def on_matrix_unit(count, tile):
+    return count * tile <= 256
 
 
 def rows_of(block, chunk):
@@ -145,29 +157,45 @@
         send.wait()
 
 
-def transform(points, twist_ref, wave_ref, turned_ref):
-    tile, width = points[0].shape
-    points = [point.astype(jnp.float32) for point in points]
-    for top in range(0, tile, 16):
-        halves = []
-        for start in (top, top + 8):
-            done = []
-            for k, value in enumerate(short_values([p[start : start + 8] for p in points])):
-                c, s = twist_ref[k, 0:1, :], twist_ref[k, 1:2, :]
-                if k == 0:
-                    re, im = value, jnp.zeros_like(value)
-                elif k == 1:
-                    re, im = value * c, value * -s
-                else:
-                    _, re, im = value
-                    re, im = re * c + im * s, im * c - re * s
-                done.append((re, im))
-            halves.append(done)
-        for k, ((a_re, a_im), (b_re, b_im)) in enumerate(zip(*halves)):
-            rows = slice(k * tile + top, k * tile + top + 16)
-            turned_ref[rows, :width] = jnp.concatenate([a_re, b_re]).astype(jnp.bfloat16)
-            turned_ref[rows, width:] = jnp.concatenate([a_im, b_im]).astype(jnp.bfloat16)
-    return jnp.dot(turned_ref[...], wave_ref[0], preferred_element_type=jnp.float32)
+def short_stage(blocks, short_ref):
+    count, (tile, width) = len(blocks[0]), blocks[0][0].shape
+    if not on_matrix_unit(count, tile):
+        blocks = [[b.astype(jnp.float32) for b in points] for points in blocks]
+        values = [short_values(points) for points in blocks]
+        return [v[:2] + [(re, im) for _, re, im in v[2:]] for v in values]
+    side = jnp.concatenate([jnp.concatenate(points) for points in blocks], axis=1)
+    parts = jnp.concatenate(
+        [jnp.dot(short_ref[i], side, preferred_element_type=jnp.float32) for i in range(2)]
+    )
+
+    def part(i, which):
+        return parts[i * tile : (i + 1) * tile, which * width : (which + 1) * width]
+
+    return [
+        [part(0, which), part(1, which)]
+        + [(part(2 * k - 2, which), part(2 * k - 1, which)) for k in range(2, count + 1)]
+        for which in range(len(blocks))
+    ]
+
+
+def transform(blocks, twist_ref, wave_ref, short_ref, turned_ref):
+    tile, width = blocks[0][0].shape
+    tall = (len(blocks[0]) + 1) * tile
+    for which, values in enumerate(short_stage(blocks, short_ref)):
+        for k, value in enumerate(values):
+            c, s = twist_ref[k, 0:1, :], twist_ref[k, 1:2, :]
+            if k == 0:
+                re, im = value, jnp.zeros_like(value)
+            elif k == 1:
+                re, im = value * c, value * -s
+            else:
+                re, im = value[0] * c + value[1] * s, value[1] * c - value[0] * s
+            rows = slice(which * tall + k * tile, which * tall + (k + 1) * tile)
+            turned_ref[rows, :width] = re.astype(jnp.bfloat16)
+            turned_ref[rows, width:] = im.astype(jnp.bfloat16)
+    turned = turned_ref[: len(blocks) * tall]
+    spec = jnp.dot(turned, wave_ref[0], preferred_element_type=jnp.float32)
+    return [spec[which * tall : (which + 1) * tall] for which in range(len(blocks))]
 
 
 def inverse(re, im, twist_ref, wave_ref):
@@ -192,10 +220,14 @@
     return [jnp.concatenate(part) for part in zip(*parts)]
 
 
-def filter_kernel(mine_ref, other_ref, twist_ref, wave_ref, spec_ref, turned_ref):
+def filter_kernel(mine_ref, other_ref, twist_ref, wave_ref, short_ref, spec_ref, turned_ref):
     near, far, rows, _ = mine_ref.shape
     tile = spec_ref.shape[1] // twist_ref.shape[0]
     me, side = lax.axis_index("ctx"), lax.axis_index("groups")
+    for first, table in ((4, wave_ref), (2, short_ref)):
+        for i in range(2):
+            _, high, wide = table.shape
+            spec_ref[spec_ref.shape[0] - first + i, :high, :wide] = table[i]
 
     def piece(share_ref, b, lanes):
         return share_ref[(me % near) ^ (b % near), (me // near) ^ (b // near), lanes]
@@ -209,49 +241,57 @@
     if rows < tile:
         parts = zip(*[points(half, slice(None)) for half in range(2)])
         joined = [jnp.concatenate([p.astype(jnp.float32) for p in pair]) for pair in parts]
-        spec = transform(joined, twist_ref, wave_ref, turned_ref)
+        (spec,) = transform([joined], twist_ref, wave_ref, short_ref, turned_ref)
         spec_ref[0] = spec.astype(jnp.bfloat16)
-    else:
-        for half in range(2):
-
-            @pl.loop(0, rows // tile)
-            def _(step):
-                lanes = pl.ds(pl.multiple_of(step * tile, tile), tile)
-                spec = transform(points(half, lanes), twist_ref, wave_ref, turned_ref)
-                spec_ref[half * (rows // tile) + step] = spec.astype(jnp.bfloat16)
-
-
-def spectral_kernel(sig_ref, spec_ref, twist_ref, wave_ref, *refs):
+        return
+    group = turned_ref.shape[0] // spec_ref.shape[1] // 2
+
+    @pl.loop(0, rows // tile // group)
+    def _(step):
+        tiles = [step * group + t for t in range(group)]
+        blocks = [points(half, rows_of(t, tile)) for half in range(2) for t in tiles]
+        specs = transform(blocks, twist_ref, wave_ref, short_ref, turned_ref)
+        for i, spec in enumerate(specs):
+            half, t = i // group, tiles[i % group]
+            spec_ref[half * (rows // tile) + t] = spec.astype(jnp.bfloat16)
+
+
+def spectral_kernel(sig_ref, spec_ref, twist_ref, *refs):
     *out_refs, made_ref, turned_ref = refs
     count, _, chunk, width = sig_ref.shape
     tile = spec_ref.shape[1] // twist_ref.shape[0]
-    me, steps = lax.axis_index("ctx"), chunk // tile
+    group = turned_ref.shape[0] // spec_ref.shape[1] // 2
+    me, steps = lax.axis_index("ctx"), chunk // tile // group
+    size = count * tile if on_matrix_unit(count, tile) else 1
+    wave_ref = spec_ref.at[chunk // tile : chunk // tile + 2, : 2 * width]
+    short_ref = spec_ref.at[chunk // tile + 2 :, :size, :size]
 
     def deliver(step):
-        lanes = rows_of(step, tile)
+        lanes = rows_of(step, tile * group)
         for k in range(count):
             out_refs[k][:, lanes] = made_ref[k, :, lanes]
 
     @pl.loop(0, steps)
     def _(step):
         deliver(jnp.maximum(step - 1, 0))
-        lanes = rows_of(step, tile)
-        specs = []
-        for which in range(2):
-            points = [sig_ref[b, which, lanes] for b in range(count)]
-            spec = transform(points, twist_ref, wave_ref, turned_ref.at[which])
-            specs.append((spec[:, :width], spec[:, width:]))
-        (m_re, m_im), (g_re, g_im) = specs
-        spec = spec_ref[step].astype(jnp.float32)
-        f_re, f_im = spec[:, :width], spec[:, width:]
-        results = (
-            (f_re * m_re - f_im * m_im, f_re * m_im + f_im * m_re),
-            (f_re * g_re + f_im * g_im, f_re * g_im - f_im * g_re),
-            (g_re * m_re + g_im * m_im, g_im * m_re - g_re * m_im),
-        )
-        for which, (re, im) in enumerate(results):
-            for b, part in enumerate(inverse(re, im, twist_ref, wave_ref)):
-                made_ref[me ^ b, which, lanes] = part.astype(jnp.bfloat16)
+        tiles = [step * group + t for t in range(group)]
+        blocks = [
+            [sig_ref[b, which, rows_of(t, tile)] for b in range(count)]
+            for t in tiles
+            for which in range(2)
+        ]
+        both = transform(blocks, twist_ref, wave_ref, short_ref, turned_ref)
+        for i, t in enumerate(tiles):
+            specs = [*both[2 * i : 2 * i + 2], spec_ref[t].astype(jnp.float32)]
+            (m_re, m_im), (g_re, g_im), (f_re, f_im) = ((s[:, :width], s[:, width:]) for s in specs)
+            results = (
+                (f_re * m_re - f_im * m_im, f_re * m_im + f_im * m_re),
+                (f_re * g_re + f_im * g_im, f_re * g_im - f_im * g_re),
+                (g_re * m_re + g_im * m_im, g_im * m_re - g_re * m_im),
+            )
+            for which, (re, im) in enumerate(results):
+                for b, part in enumerate(inverse(re, im, twist_ref, wave_ref)):
+                    made_ref[me ^ b, which, rows_of(t, tile)] = part.astype(jnp.bfloat16)
 
     deliver(steps - 1)
 
@@ -375,7 +415,8 @@
     count = lax.axis_size("ctx")
     channels, width = values.shape
     chunk = channels // count
-    twist, wave = make_tables(count, width)
+    tile = min(TILE, chunk)
+    twist, wave, short = make_tables(count, width, tile)
     here = pl.BlockSpec(memory_space=pltpu.VMEM)
     limit = pltpu.CompilerParams(vmem_limit_bytes=24 * 1024 * 1024)
     far = 1 << ((count.bit_length() - 1) // 2)
@@ -396,31 +437,31 @@
     blocks, sent = lax.optimization_barrier((blocks, sent))
     held = exchange(sent)
     mine, other = near_filters(blocks)
-    tile = min(TILE, chunk)
+    group = min(GROUP, chunk // tile)
     tall = (count + 1) * tile
     spec = pl.pallas_call(
         filter_kernel,
-        in_specs=[here] * 4,
+        in_specs=[here] * 5,
         out_specs=here,
-        out_shape=jax.ShapeDtypeStruct((chunk // tile, tall, 2 * width), jnp.bfloat16),
-        scratch_shapes=[pltpu.VMEM((tall, 2 * width), jnp.bfloat16)],
+        out_shape=jax.ShapeDtypeStruct((chunk // tile + 4, tall, 2 * width), jnp.bfloat16),
+        scratch_shapes=[pltpu.VMEM((2 * max(group // 2, 1) * tall, 2 * width), jnp.bfloat16)],
         compiler_params=limit,
         cost_estimate=pl.CostEstimate(
             flops=8 * count * chunk * width * width, bytes_accessed=2**20, transcendentals=0
         ),
-    )(mine, other, twist, wave)
+    )(mine, other, twist, wave, short)
     message = jax.ShapeDtypeStruct((3, chunk, width), jnp.bfloat16)
     made = pl.pallas_call(
         spectral_kernel,
-        in_specs=[here] * 4,
+        in_specs=[here] * 3,
         out_specs=[here] * count,
         out_shape=[message] * count,
         scratch_shapes=[
             pltpu.VMEM((count, 3, chunk, width), jnp.bfloat16),
-            pltpu.VMEM((2, tall, 2 * width), jnp.bfloat16),
+            pltpu.VMEM((2 * group * tall, 2 * width), jnp.bfloat16),
         ],
         compiler_params=limit,
-    )(held, spec, twist, wave)
+    )(held, spec, twist)
     got = spread(made)
     half = jax.ShapeDtypeStruct((channels, width), jnp.bfloat16)
     wide = jax.ShapeDtypeStruct((channels, width), jnp.float32)

time: 84.7 us -> 84.3 us (level)
  Pallas kernels: 14.5 us -> 13.5 us
    pallas_call x2, Pallas kernels: 6.71 us -> 5.72 us  [the longest x1 4.66 us: shards(): pl.pallas_call(spectral_kernel, in_specs=[here] * 3, out_specs=[here] * c...]
  transfers between devices with their start and end apart: 23 -> 23, of which waited for: 11 -> 11; matrix products, arithmetic and copies ran while one was open for 0% -> 0% of each run, Pallas kernels for 10% -> 9%
where the time goes in v6:
time: 84.3 us; the launch traced here: 84 us
  starting transfers between devices  40 us (47%)
  waiting for transfers between devices  28.4 us (34%)
  Pallas kernels  13.5 us (16%)
  local copies, waits for them, and re-layouts  1.21 us (1%)
    ppermute x15, starting transfers between devices, spread(): got[k] = lax.ppermute(block, 'ctx', [(j, j ^ k) for j in range(count)])  26.3 us
    ppermute x7, waiting for transfers between devices, swap(): return lax.ppermute(block, axis, [(i, i ^ gap) for i in range(size)])  17.2 us
    all_to_all x1, starting transfers between devices, exchange(): return lax.all_to_all(parts, 'ctx', split_axis=0, concat_axis=0, tiled=True)  7.47 us
    ppermute x7, starting transfers between devices, swap(): return lax.ppermute(block, axis, [(i, i ^ gap) for i in range(size)])  6.2 us
    ppermute x15, waiting for transfers between devices, spread(): got[k] = lax.ppermute(block, 'ctx', [(j, j ^ k) for j in range(count)])  5.88 us
    all_to_all x1, waiting for transfers between devices, exchange(): return lax.all_to_all(parts, 'ctx', split_axis=0, concat_axis=0, tiled=True)  5.29 us
    pallas_call x1, Pallas kernels, shards(): pl.pallas_call(spectral_kernel, in_specs=[here] * 3, out_specs=[here] * c...  4.66 us
    pallas_call x1, Pallas kernels, shards(): pl.pallas_call(functools.partial(first_gates, early, late), in_specs=[hbm...  4.19 us
  transfers between devices with their start and end apart: 23, of which 11 were waited for; matrix products, arithmetic and copies ran while one was open for 0% of the time, Pallas kernels for 9%

profile of v6, /device:TPU:13, one launch (start us, length us, event | category | flops | bytes accessed | tf_op | source)
XLA Modules:
  0.0 84.0 jit_solution(11858397662189208491)
XLA Ops:
  0.7 1.1 %fusion.3 = (bf16[4,64,128]{2,1,0:T(8,128)(2,1)S(1)}, bf16[4,64,128]{2,1,0:T(8,128)(2,1)S(1)}, bf16[4,64,128]{2,1,0:T(8,128)(2,1)S(1)}, bf16[4,64,128]{2,1,0:T(8,128)(2,1)S(1)}) fusion(f32[4,4,2,64,128]{4,3,2,1,0:T(8,128)} %bitcast.30, s32[]{:T(128)S(6)} %select_n.106, s32[]{:T(128)S(6)} %select_n.100, s32[]{:T(128)S(6)} %select_n.104, s32[]{:T(128)S(6)} %select_n.102, ...), kind=kLoop, calls=%fused_computation.8 | loop fusion | bytes 524308 | tf_op jit(solution)/shard_map/convert_element_type | solution.py:403
  1.8 1.4 %collective-permute-start.2 = (bf16[4,64,128]{2,1,0:T(8,128)(2,1)S(1)}, bf16[4,64,128]{2,1,0:T(8,128)(2,1)S(1)}, u32[]{:S(2)}, u32[]{:S(2)}) collective-permute-start(bf16[4,64,128]{2,1,0:T(8,128)(2,1)S(1)} %get-tuple-element.92), channel_id=1, source_target_pairs={{0,12},{1,13},{2,14},{3,15},{4,8},{5,9},{6,10},{7,11},{8,4},{9,5},... | collective-permute-start | bytes 196616 | tf_op jit(solution)/shard_map/ppermute | solution.py:390
  3.2 1.1 %collective-permute-start.1 = (bf16[4,64,128]{2,1,0:T(8,128)(2,1)S(1)}, bf16[4,64,128]{2,1,0:T(8,128)(2,1)S(1)}, u32[]{:S(2)}, u32[]{:S(2)}) collective-permute-start(bf16[4,64,128]{2,1,0:T(8,128)(2,1)S(1)} %get-tuple-element.93), channel_id=1, source_target_pairs={{0,8},{1,9},{2,10},{3,11},{4,12},{5,13},{6,14},{7,15},{8,0},{9,1},... | collective-permute-start | bytes 196616 | tf_op jit(solution)/shard_map/ppermute | solution.py:390
  4.3 1.1 %collective-permute-start = (bf16[4,64,128]{2,1,0:T(8,128)(2,1)S(1)}, bf16[4,64,128]{2,1,0:T(8,128)(2,1)S(1)}, u32[]{:S(2)}, u32[]{:S(2)}) collective-permute-start(bf16[4,64,128]{2,1,0:T(8,128)(2,1)S(1)} %get-tuple-element.94), channel_id=1, source_target_pairs={{0,4},{1,5},{2,6},{3,7},{4,0},{5,1},{6,2},{7,3},{8,12},{9,13},{10,... | collective-permute-start | bytes 196616 | tf_op jit(solution)/shard_map/ppermute | solution.py:390
  5.4 2.5 %shard_map.111 = bf16[16,2,128,128]{3,2,1,0:T(8,128)(2,1)} custom-call(bf16[2048,128]{1,0:T(8,128)(2,1)} %refs_0_.1, bf16[2048,128]{1,0:T(8,128)(2,1)} %refs_1_.1, bf16[2048,128]{1,0:T(8,128)(2,1)} %refs_2_.1, bf16[2048,128]{1,0:T(8,128)(2,1)} %query_hbm.1), custom_call_target="tpu_custom_call" | custom-call | tf_op jit(solution)/shard_map/pallas_call | solution.py:425
  8.0 1.5 %collective-permute-done = bf16[4,64,128]{2,1,0:T(8,128)(2,1)S(1)} collective-permute-done((bf16[4,64,128]{2,1,0:T(8,128)(2,1)S(1)}, bf16[4,64,128]{2,1,0:T(8,128)(2,1)S(1)}, u32[]{:S(2)}, u32[]{:S(2)}) %collective-permute-start) | collective-permute-done | bytes 65568 | tf_op jit(solution)/shard_map/ppermute | solution.py:390
  9.5 7.5 %all-to-all-start = ((bf16[16,2,128,128]{3,2,1,0:T(8,128)(2,1)}), bf16[16,2,128,128]{3,2,1,0:T(8,128)(2,1)S(1)}, u32[]{:S(2)}, u32[]{:S(2)}) async-start(bf16[16,2,128,128]{3,2,1,0:T(8,128)(2,1)} %shard_map.111), calls=%async_computation | async-start | bytes 2097152 | tf_op jit(solution)/shard_map/all_to_all | solution.py:385
  17.5 1.2 %collective-permute-start.4 = (bf16[4,64,128]{2,1,0:T(8,128)(2,1)S(1)}, bf16[4,64,128]{2,1,0:T(8,128)(2,1)S(1)}, u32[]{:S(2)}, u32[]{:S(2)}) collective-permute-start(bf16[4,64,128]{2,1,0:T(8,128)(2,1)S(1)} %pad_maximum_fusion.2), channel_id=1, source_target_pairs={{0,2},{1,3},{2,0},{3,1},{4,6},{5,7},{6,4},{7,5},{8,10},{9,11},{10,... | collective-permute-start | bytes 196616 | tf_op jit(solution)/shard_map/ppermute | solution.py:390
  19.4 5.2 %collective-permute-done.4 = bf16[4,64,128]{2,1,0:T(8,128)(2,1)S(1)} collective-permute-done((bf16[4,64,128]{2,1,0:T(8,128)(2,1)S(1)}, bf16[4,64,128]{2,1,0:T(8,128)(2,1)S(1)}, u32[]{:S(2)}, u32[]{:S(2)}) %collective-permute-start.4) | collective-permute-done | bytes 65568 | tf_op jit(solution)/shard_map/ppermute | solution.py:390
  24.6 2.4 %collective-permute-done.5 = bf16[4,64,128]{2,1,0:T(8,128)(2,1)S(1)} collective-permute-done((bf16[4,64,128]{2,1,0:T(8,128)(2,1)S(1)}, bf16[4,64,128]{2,1,0:T(8,128)(2,1)S(1)}, u32[]{:S(2)}, u32[]{:S(2)}) %collective-permute-start.5) | collective-permute-done | bytes 65568 | tf_op jit(solution)/shard_map/ppermute | solution.py:390
  27.4 8.0 %collective-permute-done.6.other_ref = bf16[4,4,64,128]{3,2,1,0:T(8,128)(2,1)S(1)} collective-permute-done((bf16[4,4,64,128]{3,2,1,0:T(8,128)(2,1)S(1)}, bf16[4,4,64,128]{3,2,1,0:T(8,128)(2,1)S(1)}, u32[]{:S(2)}, u32[]{:S(2)}) %collective-permute-start.6) | collective-permute-done | bytes 262176 | tf_op jit(solution)/shard_map/ppermute | solution.py:390
  35.4 1.1 %shard_map.112.spec_ref = bf16[12,272,256]{2,1,0:T(8,128)(2,1)S(1)} custom-call(bf16[4,4,64,128]{3,2,1,0:T(8,128)(2,1)S(1)} %pad_maximum_fusion.mine_ref, bf16[4,4,64,128]{3,2,1,0:T(8,128)(2,1)S(1)} %collective-permute-done.6.other_ref, f32[17,4,128]{2,1,0:T(4,128)S(1)} %copy-done.5, bf16[2,256,256]{2,1,0:T(8,128)(2,1)S(1)} %copy-done.4, ...), custom_call_target="tpu_custom_call" | custom-call | flops 268435456 | bytes 1048576 | tf_op jit(solution)/shard_map/pallas_call | solution.py:442
  36.5 5.3 %all-to-all-done.sig_ref = bf16[16,2,128,128]{3,2,1,0:T(8,128)(2,1)S(1)} async-done(((bf16[16,2,128,128]{3,2,1,0:T(8,128)(2,1)}), bf16[16,2,128,128]{3,2,1,0:T(8,128)(2,1)S(1)}, u32[]{:S(2)}, u32[]{:S(2)}) %all-to-all-start) | async-done | bytes 1048608 | tf_op jit(solution)/shard_map/all_to_all | solution.py:385
  41.8 4.7 %shard_map.113 = (bf16[3,128,128]{2,1,0:T(8,128)(2,1)S(1)}, bf16[3,128,128]{2,1,0:T(8,128)(2,1)S(1)}, bf16[3,128,128]{2,1,0:T(8,128)(2,1)S(1)}, bf16[3,128,128]{...) custom-call(bf16[16,2,128,128]{3,2,1,0:T(8,128)(2,1)S(1)} %all-to-al, ...), custom_call_target="tpu_custom_call" | custom-call | tf_op jit(solution)/shard_map/pallas_call | solution.py:454
  46.8 1.9 %collective-permute-start.8 = (bf16[3,128,128]{2,1,0:T(8,128)(2,1)S(1)}, bf16[3,128,128]{2,1,0:T(8,128)(2,1)S(1)}, u32[]{:S(2)}, u32[]{:S(2)}) collective-permute-start(bf16[3,128,128]{2,1,0:T(8,128)(2,1)S(1)} %get-tuple-element.58), channel_id=1, source_target_pairs={{0,4},{1,5},{2,6},{3,7},{4,0},{5,1},{6,2},{7,3},{8,12},{9,13},{10,... | collective-permute-start | bytes 294920 | tf_op jit(solution)/shard_map/ppermute | solution.py:380
  48.7 1.1 %collective-permute-start.9 = (bf16[3,128,128]{2,1,0:T(8,128)(2,1)S(1)}, bf16[3,128,128]{2,1,0:T(8,128)(2,1)S(1)}, u32[]{:S(2)}, u32[]{:S(2)}) collective-permute-start(bf16[3,128,128]{2,1,0:T(8,128)(2,1)S(1)} %get-tuple-element.61), channel_id=1, source_target_pairs={{0,9},{1,8},{2,11},{3,10},{4,13},{5,12},{6,15},{7,14},{8,1},{9,0},... | collective-permute-start | bytes 294920 | tf_op jit(solution)/shard_map/ppermute | solution.py:380
  49.9 0.8 collective-permute-start.10
  50.7 2.1 %collective-permute-start.11 = (bf16[3,128,128]{2,1,0:T(8,128)(2,1)S(1)}, bf16[3,128,128]{2,1,0:T(8,128)(2,1)S(1)}, u32[]{:S(2)}, u32[]{:S(2)}) collective-permute-start(bf16[3,128,128]{2,1,0:T(8,128)(2,1)S(1)} %get-tuple-element.67), channel_id=1, source_target_pairs={{0,10},{1,11},{2,8},{3,9},{4,14},{5,15},{6,12},{7,13},{8,2},{9,3},... | collective-permute-start | bytes 294920 | tf_op jit(solution)/shard_map/ppermute | solution.py:380
  52.8 1.0 %collective-permute-start.12 = (bf16[3,128,128]{2,1,0:T(8,128)(2,1)S(1)}, bf16[3,128,128]{2,1,0:T(8,128)(2,1)S(1)}, u32[]{:S(2)}, u32[]{:S(2)}) collective-permute-start(bf16[3,128,128]{2,1,0:T(8,128)(2,1)S(1)} %get-tuple-element.70), channel_id=1, source_target_pairs={{0,6},{1,7},{2,4},{3,5},{4,2},{5,3},{6,0},{7,1},{8,14},{9,15},{10,... | collective-permute-start | bytes 294920 | tf_op jit(solution)/shard_map/ppermute | solution.py:380
  53.8 4.4 %collective-permute-start.13 = (bf16[3,128,128]{2,1,0:T(8,128)(2,1)S(1)}, bf16[3,128,128]{2,1,0:T(8,128)(2,1)S(1)}, u32[]{:S(2)}, u32[]{:S(2)}) collective-permute-start(bf16[3,128,128]{2,1,0:T(8,128)(2,1)S(1)} %get-tuple-element.73), channel_id=1, source_target_pairs={{0,11},{1,10},{2,9},{3,8},{4,15},{5,14},{6,13},{7,12},{8,3},{9,2},... | collective-permute-start | bytes 294920 | tf_op jit(solution)/shard_map/ppermute | solution.py:380
  58.1 0.8 collective-permute-start.14
  60.0 1.4 %collective-permute-done.11.refs_8_ = bf16[3,128,128]{2,1,0:T(8,128)(2,1)S(1)} collective-permute-done((bf16[3,128,128]{2,1,0:T(8,128)(2,1)S(1)}, bf16[3,128,128]{2,1,0:T(8,128)(2,1)S(1)}, u32[]{:S(2)}, u32[]{:S(2)}) %collective-permute-start.11) | collective-permute-done | bytes 98336 | tf_op jit(solution)/shard_map/ppermute | solution.py:380
  61.5 0.8 collective-permute-start.16
  62.7 3.2 %collective-permute-start.17 = (bf16[3,128,128]{2,1,0:T(8,128)(2,1)S(1)}, bf16[3,128,128]{2,1,0:T(8,128)(2,1)S(1)}, u32[]{:S(2)}, u32[]{:S(2)}) collective-permute-start(bf16[3,128,128]{2,1,0:T(8,128)(2,1)S(1)} %get-tuple-element.83), channel_id=1, source_target_pairs={{0,13},{1,12},{2,15},{3,14},{4,9},{5,8},{6,11},{7,10},{8,5},{9,4},... | collective-permute-start | bytes 294920 | tf_op jit(solution)/shard_map/ppermute | solution.py:380
  65.9 1.1 %collective-permute-done.13.refs_10_ = bf16[3,128,128]{2,1,0:T(8,128)(2,1)S(1)} collective-permute-done((bf16[3,128,128]{2,1,0:T(8,128)(2,1)S(1)}, bf16[3,128,128]{2,1,0:T(8,128)(2,1)S(1)}, u32[]{:S(2)}, u32[]{:S(2)}) %collective-permute-start.13) | collective-permute-done | bytes 98336 | tf_op jit(solution)/shard_map/ppermute | solution.py:380
  67.0 1.1 %collective-permute-start.18 = (bf16[3,128,128]{2,1,0:T(8,128)(2,1)S(1)}, bf16[3,128,128]{2,1,0:T(8,128)(2,1)S(1)}, u32[]{:S(2)}, u32[]{:S(2)}) collective-permute-start(bf16[3,128,128]{2,1,0:T(8,128)(2,1)S(1)} %get-tuple-element.84), channel_id=1, source_target_pairs={{0,3},{1,2},{2,1},{3,0},{4,7},{5,6},{6,5},{7,4},{8,11},{9,10},{10,... | collective-permute-start | bytes 294920 | tf_op jit(solution)/shard_map/ppermute | solution.py:380
  68.0 1.1 %collective-permute-start.19 = (bf16[3,128,128]{2,1,0:T(8,128)(2,1)S(1)}, bf16[3,128,128]{2,1,0:T(8,128)(2,1)S(1)}, u32[]{:S(2)}, u32[]{:S(2)}) collective-permute-start(bf16[3,128,128]{2,1,0:T(8,128)(2,1)S(1)} %get-tuple-element.85), channel_id=1, source_target_pairs={{0,14},{1,15},{2,12},{3,13},{4,10},{5,11},{6,8},{7,9},{8,6},{9,7},... | collective-permute-start | bytes 294920 | tf_op jit(solution)/shard_map/ppermute | solution.py:380
  69.1 6.0 %collective-permute-start.20 = (bf16[3,128,128]{2,1,0:T(8,128)(2,1)S(1)}, bf16[3,128,128]{2,1,0:T(8,128)(2,1)S(1)}, u32[]{:S(2)}, u32[]{:S(2)}) collective-permute-start(bf16[3,128,128]{2,1,0:T(8,128)(2,1)S(1)} %get-tuple-element.86), channel_id=1, source_target_pairs={{0,1},{1,0},{2,3},{3,2},{4,5},{5,4},{6,7},{7,6},{8,9},{9,8},{10,11... | collective-permute-start | bytes 294920 | tf_op jit(solution)/shard_map/ppermute | solution.py:380
  75.2 1.1 %collective-permute-start.21 = (bf16[3,128,128]{2,1,0:T(8,128)(2,1)S(1)}, bf16[3,128,128]{2,1,0:T(8,128)(2,1)S(1)}, u32[]{:S(2)}, u32[]{:S(2)}) collective-permute-start(bf16[3,128,128]{2,1,0:T(8,128)(2,1)S(1)} %get-tuple-element.87), channel_id=1, source_target_pairs={{0,15},{1,14},{2,13},{3,12},{4,11},{5,10},{6,9},{7,8},{8,7},{9,6},... | collective-permute-start | bytes 294920 | tf_op jit(solution)/shard_map/ppermute | solution.py:380
  76.4 4.2 %shard_map.114 = (bf16[2048,128]{1,0:T(8,128)(2,1)}, bf16[2048,128]{1,0:T(8,128)(2,1)}, bf16[2048,128]{1,0:T(8,128)(2,1)}, f32[2048,128]{1,0:T(8,128)}, bf16[5,3,128,128]{3,2,1,0:T(8,128)(2,1)S(1)}) custom-call(bf16[2048,128]{1,0:T(8,128)(2,1)S(1)} %copy-done, bf16[2048,128]{1,0:T(8,128)(2,1)S(1)} %copy-done.1, bf16[2048,128]{1,0:T(8,128)(2,1)S(1)} %copy-done.2, ...), custom_call_target="tpu_custom_call" | custom-call | tf_op jit(solution)/shard_map/pallas_call | solution.py:473
  80.8 2.1 %collective-permute-done.21.refs_4_ = bf16[3,128,128]{2,1,0:T(8,128)(2,1)S(1)} collective-permute-done((bf16[3,128,128]{2,1,0:T(8,128)(2,1)S(1)}, bf16[3,128,128]{2,1,0:T(8,128)(2,1)S(1)}, u32[]{:S(2)}, u32[]{:S(2)}) %collective-permute-start.21) | collective-permute-done | bytes 98336 | tf_op jit(solution)/shard_map/ppermute | solution.py:380
  82.9 1.1 %shard_map.115 = (bf16[2048,128]{1,0:T(8,128)(2,1)}, bf16[2048,128]{1,0:T(8,128)(2,1)}, bf16[2048,128]{1,0:T(8,128)(2,1)}, f32[2048,128]{1,0:T(8,128)}) custom-call(bf16[5,3,128,128]{3,2,1,0:T(8,128)(2,1)S(1)} %get-tuple-element.82.held_ref, ...), custom_call_target="tpu_custom_call", output_to_operand_aliasing={{0}: (6, {}), {1}: (7, {}), {2}: (8, {}), {3}: (9, {})} | custom-call | tf_op jit(solution)/shard_map/pallas_call | solution.py:487
  (39 shorter events, 3.7 us)
Async XLA Ops:
  1.8 6.1 %collective-permute-start.2 = (bf16[4,64,128]{2,1,0:T(8,128)(2,1)S(1)}, bf16[4,64,128]{2,1,0:T(8,128)(2,1)S(1)}, u32[]{:S(2)}, u32[]{:S(2)}) collective-permute-start(bf16[4,64,128]{2,1,0:T(8,128)(2,1)S(1)} %get-tuple-element.92), channel_id=1, source_target_pairs={{0,12},{1,13},{2,14},{3,15},{4,8},{5,9},{6,10},{7,11},{8,4},{9,5},... | collective-permute-start | bytes 196616 | tf_op jit(solution)/shard_map/ppermute | solution.py:390
  3.2 4.8 %collective-permute-start.1 = (bf16[4,64,128]{2,1,0:T(8,128)(2,1)S(1)}, bf16[4,64,128]{2,1,0:T(8,128)(2,1)S(1)}, u32[]{:S(2)}, u32[]{:S(2)}) collective-permute-start(bf16[4,64,128]{2,1,0:T(8,128)(2,1)S(1)} %get-tuple-element.93), channel_id=1, source_target_pairs={{0,8},{1,9},{2,10},{3,11},{4,12},{5,13},{6,14},{7,15},{8,0},{9,1},... | collective-permute-start | bytes 196616 | tf_op jit(solution)/shard_map/ppermute | solution.py:390
  4.3 5.2 %collective-permute-start = (bf16[4,64,128]{2,1,0:T(8,128)(2,1)S(1)}, bf16[4,64,128]{2,1,0:T(8,128)(2,1)S(1)}, u32[]{:S(2)}, u32[]{:S(2)}) collective-permute-start(bf16[4,64,128]{2,1,0:T(8,128)(2,1)S(1)} %get-tuple-element.94), channel_id=1, source_target_pairs={{0,4},{1,5},{2,6},{3,7},{4,0},{5,1},{6,2},{7,3},{8,12},{9,13},{10,... | collective-permute-start | bytes 196616 | tf_op jit(solution)/shard_map/ppermute | solution.py:390
  9.5 25.9 %copy-start.3 = (bf16[2,256,256]{2,1,0:T(8,128)(2,1)S(1)}, bf16[2,256,256]{2,1,0:T(8,128)(2,1)}, u32[]{:S(2)}) copy-start(bf16[2,256,256]{2,1,0:T(8,128)(2,1)} %constant.225.clone.short_ref) | copy-start | bytes 786436
  9.5 25.9 %copy-start.4 = (bf16[2,256,256]{2,1,0:T(8,128)(2,1)S(1)}, bf16[2,256,256]{2,1,0:T(8,128)(2,1)}, u32[]{:S(2)}) copy-start(bf16[2,256,256]{2,1,0:T(8,128)(2,1)} %constant.224.clone.wave_ref) | copy-start | bytes 786436
  9.5 25.9 %copy-start.5 = (f32[17,4,128]{2,1,0:T(4,128)S(1)}, f32[17,4,128]{2,1,0:T(4,128)}, u32[]{:S(2)}) copy-start(f32[17,4,128]{2,1,0:T(4,128)} %constant.226.clone.twist_ref) | copy-start | bytes 104452
  9.5 32.3 %all-to-all-start = ((bf16[16,2,128,128]{3,2,1,0:T(8,128)(2,1)}), bf16[16,2,128,128]{3,2,1,0:T(8,128)(2,1)S(1)}, u32[]{:S(2)}, u32[]{:S(2)}) async-start(bf16[16,2,128,128]{3,2,1,0:T(8,128)(2,1)} %shard_map.111), calls=%async_computation | async-start | bytes 2097152 | tf_op jit(solution)/shard_map/all_to_all | solution.py:385
  17.0 2.4 %collective-permute-start.3 = (bf16[4,64,128]{2,1,0:T(8,128)(2,1)S(1)}, bf16[4,64,128]{2,1,0:T(8,128)(2,1)S(1)}, u32[]{:S(2)}, u32[]{:S(2)}) collective-permute-start(bf16[4,64,128]{2,1,0:T(8,128)(2,1)S(1)} %pad_maximum_fusion.1), channel_id=1, source_target_pairs={{0,1},{1,0},{2,3},{3,2},{4,5},{5,4},{6,7},{7,6},{8,9},{9,8},{10,11... | collective-permute-start | bytes 196616 | tf_op jit(solution)/shard_map/ppermute | solution.py:390
  17.5 7.1 %collective-permute-start.4 = (bf16[4,64,128]{2,1,0:T(8,128)(2,1)S(1)}, bf16[4,64,128]{2,1,0:T(8,128)(2,1)S(1)}, u32[]{:S(2)}, u32[]{:S(2)}) collective-permute-start(bf16[4,64,128]{2,1,0:T(8,128)(2,1)S(1)} %pad_maximum_fusion.2), channel_id=1, source_target_pairs={{0,2},{1,3},{2,0},{3,1},{4,6},{5,7},{6,4},{7,5},{8,10},{9,11},{10,... | collective-permute-start | bytes 196616 | tf_op jit(solution)/shard_map/ppermute | solution.py:390
  18.7 8.3 %collective-permute-start.5 = (bf16[4,64,128]{2,1,0:T(8,128)(2,1)S(1)}, bf16[4,64,128]{2,1,0:T(8,128)(2,1)S(1)}, u32[]{:S(2)}, u32[]{:S(2)}) collective-permute-start(bf16[4,64,128]{2,1,0:T(8,128)(2,1)S(1)} %pad_maximum_fusion.3), channel_id=1, source_target_pairs={{0,3},{1,2},{2,1},{3,0},{4,7},{5,6},{6,5},{7,4},{8,11},{9,10},{10,... | collective-permute-start | bytes 196616 | tf_op jit(solution)/shard_map/ppermute | solution.py:390
  27.1 8.3 %collective-permute-start.6 = (bf16[4,4,64,128]{3,2,1,0:T(8,128)(2,1)S(1)}, bf16[4,4,64,128]{3,2,1,0:T(8,128)(2,1)S(1)}, u32[]{:S(2)}, u32[]{:S(2)}) collective-permute-start(bf16[4,4,64,128]{3,2,1,0:T(8,128)(2,1)S(1)} %pad_maximum_fusion.mine_ref), channel_id=1, source_target_pairs={{0,16},{16,0},{1,17},{17,1},{2,18},{18,2},{3,19},{19,3},{4,20},{20... | collective-permute-start | bytes 786440 | tf_op jit(solution)/shard_map/ppermute | solution.py:390
  36.5 39.8 %copy-start = (bf16[2048,128]{1,0:T(8,128)(2,1)S(1)}, bf16[2048,128]{1,0:T(8,128)(2,1)}, u32[]{:S(2)}) copy-start(bf16[2048,128]{1,0:T(8,128)(2,1)} %refs_0_.1) | copy-start | bytes 1572868
  41.8 34.5 %copy-start.1 = (bf16[2048,128]{1,0:T(8,128)(2,1)S(1)}, bf16[2048,128]{1,0:T(8,128)(2,1)}, u32[]{:S(2)}) copy-start(bf16[2048,128]{1,0:T(8,128)(2,1)} %refs_1_.1) | copy-start | bytes 1572868
  41.8 34.5 %copy-start.2 = (bf16[2048,128]{1,0:T(8,128)(2,1)S(1)}, bf16[2048,128]{1,0:T(8,128)(2,1)}, u32[]{:S(2)}) copy-start(bf16[2048,128]{1,0:T(8,128)(2,1)} %refs_2_.1) | copy-start | bytes 1572868
  46.5 6.3 %collective-permute-start.7 = (bf16[3,128,128]{2,1,0:T(8,128)(2,1)S(1)}, bf16[3,128,128]{2,1,0:T(8,128)(2,1)S(1)}, u32[]{:S(2)}, u32[]{:S(2)}) collective-permute-start(bf16[3,128,128]{2,1,0:T(8,128)(2,1)S(1)} %get-tuple-element.55), channel_id=1, source_target_pairs={{0,8},{1,9},{2,10},{3,11},{4,12},{5,13},{6,14},{7,15},{8,0},{9,1},... | collective-permute-start | bytes 294920 | tf_op jit(solution)/shard_map/ppermute | solution.py:380
  46.8 6.9 %collective-permute-start.8 = (bf16[3,128,128]{2,1,0:T(8,128)(2,1)S(1)}, bf16[3,128,128]{2,1,0:T(8,128)(2,1)S(1)}, u32[]{:S(2)}, u32[]{:S(2)}) collective-permute-start(bf16[3,128,128]{2,1,0:T(8,128)(2,1)S(1)} %get-tuple-element.58), channel_id=1, source_target_pairs={{0,4},{1,5},{2,6},{3,7},{4,0},{5,1},{6,2},{7,3},{8,12},{9,13},{10,... | collective-permute-start | bytes 294920 | tf_op jit(solution)/shard_map/ppermute | solution.py:380
  48.7 9.4 %collective-permute-start.9 = (bf16[3,128,128]{2,1,0:T(8,128)(2,1)S(1)}, bf16[3,128,128]{2,1,0:T(8,128)(2,1)S(1)}, u32[]{:S(2)}, u32[]{:S(2)}) collective-permute-start(bf16[3,128,128]{2,1,0:T(8,128)(2,1)S(1)} %get-tuple-element.61), channel_id=1, source_target_pairs={{0,9},{1,8},{2,11},{3,10},{4,13},{5,12},{6,15},{7,14},{8,1},{9,0},... | collective-permute-start | bytes 294920 | tf_op jit(solution)/shard_map/ppermute | solution.py:380
  49.9 9.6 %collective-permute-start.10 = (bf16[3,128,128]{2,1,0:T(8,128)(2,1)S(1)}, bf16[3,128,128]{2,1,0:T(8,128)(2,1)S(1)}, u32[]{:S(2)}, u32[]{:S(2)}) collective-permute-start(bf16[3,128,128]{2,1,0:T(8,128)(2,1)S(1)} %get-tuple-element.64), channel_id=1, source_target_pairs={{0,5},{1,4},{2,7},{3,6},{4,1},{5,0},{6,3},{7,2},{8,13},{9,12},{10,... | collective-permute-start | bytes 294920 | tf_op jit(solution)/shard_map/ppermute | solution.py:380
  50.7 10.8 %collective-permute-start.11 = (bf16[3,128,128]{2,1,0:T(8,128)(2,1)S(1)}, bf16[3,128,128]{2,1,0:T(8,128)(2,1)S(1)}, u32[]{:S(2)}, u32[]{:S(2)}) collective-permute-start(bf16[3,128,128]{2,1,0:T(8,128)(2,1)S(1)} %get-tuple-element.67), channel_id=1, source_target_pairs={{0,10},{1,11},{2,8},{3,9},{4,14},{5,15},{6,12},{7,13},{8,2},{9,3},... | collective-permute-start | bytes 294920 | tf_op jit(solution)/shard_map/ppermute | solution.py:380
  52.8 9.9 %collective-permute-start.12 = (bf16[3,128,128]{2,1,0:T(8,128)(2,1)S(1)}, bf16[3,128,128]{2,1,0:T(8,128)(2,1)S(1)}, u32[]{:S(2)}, u32[]{:S(2)}) collective-permute-start(bf16[3,128,128]{2,1,0:T(8,128)(2,1)S(1)} %get-tuple-element.70), channel_id=1, source_target_pairs={{0,6},{1,7},{2,4},{3,5},{4,2},{5,3},{6,0},{7,1},{8,14},{9,15},{10,... | collective-permute-start | bytes 294920 | tf_op jit(solution)/shard_map/ppermute | solution.py:380
  53.8 13.2 %collective-permute-start.13 = (bf16[3,128,128]{2,1,0:T(8,128)(2,1)S(1)}, bf16[3,128,128]{2,1,0:T(8,128)(2,1)S(1)}, u32[]{:S(2)}, u32[]{:S(2)}) collective-permute-start(bf16[3,128,128]{2,1,0:T(8,128)(2,1)S(1)} %get-tuple-element.73), channel_id=1, source_target_pairs={{0,11},{1,10},{2,9},{3,8},{4,15},{5,14},{6,13},{7,12},{8,3},{9,2},... | collective-permute-start | bytes 294920 | tf_op jit(solution)/shard_map/ppermute | solution.py:380
  58.1 9.9 %collective-permute-start.14 = (bf16[3,128,128]{2,1,0:T(8,128)(2,1)S(1)}, bf16[3,128,128]{2,1,0:T(8,128)(2,1)S(1)}, u32[]{:S(2)}, u32[]{:S(2)}) collective-permute-start(bf16[3,128,128]{2,1,0:T(8,128)(2,1)S(1)} %get-tuple-element.76), channel_id=1, source_target_pairs={{0,7},{1,6},{2,5},{3,4},{4,3},{5,2},{6,1},{7,0},{8,15},{9,14},{10,... | collective-permute-start | bytes 294920 | tf_op jit(solution)/shard_map/ppermute | solution.py:380
  59.5 9.7 %collective-permute-start.15 = (bf16[3,128,128]{2,1,0:T(8,128)(2,1)S(1)}, bf16[3,128,128]{2,1,0:T(8,128)(2,1)S(1)}, u32[]{:S(2)}, u32[]{:S(2)}) collective-permute-start(bf16[3,128,128]{2,1,0:T(8,128)(2,1)S(1)} %get-tuple-element.79), channel_id=1, source_target_pairs={{0,12},{1,13},{2,14},{3,15},{4,8},{5,9},{6,10},{7,11},{8,4},{9,5},... | collective-permute-start | bytes 294920 | tf_op jit(solution)/shard_map/ppermute | solution.py:380
  61.5 13.7 %collective-permute-start.16 = (bf16[3,128,128]{2,1,0:T(8,128)(2,1)S(1)}, bf16[3,128,128]{2,1,0:T(8,128)(2,1)S(1)}, u32[]{:S(2)}, u32[]{:S(2)}) collective-permute-start(bf16[3,128,128]{2,1,0:T(8,128)(2,1)S(1)} %get-tuple-element.81), channel_id=1, source_target_pairs={{0,2},{1,3},{2,0},{3,1},{4,6},{5,7},{6,4},{7,5},{8,10},{9,11},{10,... | collective-permute-start | bytes 294920 | tf_op jit(solution)/shard_map/ppermute | solution.py:380
  62.7 17.9 %collective-permute-start.17 = (bf16[3,128,128]{2,1,0:T(8,128)(2,1)S(1)}, bf16[3,128,128]{2,1,0:T(8,128)(2,1)S(1)}, u32[]{:S(2)}, u32[]{:S(2)}) collective-permute-start(bf16[3,128,128]{2,1,0:T(8,128)(2,1)S(1)} %get-tuple-element.83), channel_id=1, source_target_pairs={{0,13},{1,12},{2,15},{3,14},{4,9},{5,8},{6,11},{7,10},{8,5},{9,4},... | collective-permute-start | bytes 294920 | tf_op jit(solution)/shard_map/ppermute | solution.py:380
  67.0 13.6 %collective-permute-start.18 = (bf16[3,128,128]{2,1,0:T(8,128)(2,1)S(1)}, bf16[3,128,128]{2,1,0:T(8,128)(2,1)S(1)}, u32[]{:S(2)}, u32[]{:S(2)}) collective-permute-start(bf16[3,128,128]{2,1,0:T(8,128)(2,1)S(1)} %get-tuple-element.84), channel_id=1, source_target_pairs={{0,3},{1,2},{2,1},{3,0},{4,7},{5,6},{6,5},{7,4},{8,11},{9,10},{10,... | collective-permute-start | bytes 294920 | tf_op jit(solution)/shard_map/ppermute | solution.py:380
  68.0 12.8 %collective-permute-start.19 = (bf16[3,128,128]{2,1,0:T(8,128)(2,1)S(1)}, bf16[3,128,128]{2,1,0:T(8,128)(2,1)S(1)}, u32[]{:S(2)}, u32[]{:S(2)}) collective-permute-start(bf16[3,128,128]{2,1,0:T(8,128)(2,1)S(1)} %get-tuple-element.85), channel_id=1, source_target_pairs={{0,14},{1,15},{2,12},{3,13},{4,10},{5,11},{6,8},{7,9},{8,6},{9,7},... | collective-permute-start | bytes 294920 | tf_op jit(solution)/shard_map/ppermute | solution.py:380
  69.1 11.7 %collective-permute-start.20 = (bf16[3,128,128]{2,1,0:T(8,128)(2,1)S(1)}, bf16[3,128,128]{2,1,0:T(8,128)(2,1)S(1)}, u32[]{:S(2)}, u32[]{:S(2)}) collective-permute-start(bf16[3,128,128]{2,1,0:T(8,128)(2,1)S(1)} %get-tuple-element.86), channel_id=1, source_target_pairs={{0,1},{1,0},{2,3},{3,2},{4,5},{5,4},{6,7},{7,6},{8,9},{9,8},{10,11... | collective-permute-start | bytes 294920 | tf_op jit(solution)/shard_map/ppermute | solution.py:380
  75.2 7.7 %collective-permute-start.21 = (bf16[3,128,128]{2,1,0:T(8,128)(2,1)S(1)}, bf16[3,128,128]{2,1,0:T(8,128)(2,1)S(1)}, u32[]{:S(2)}, u32[]{:S(2)}) collective-permute-start(bf16[3,128,128]{2,1,0:T(8,128)(2,1)S(1)} %get-tuple-element.87), channel_id=1, source_target_pairs={{0,15},{1,14},{2,13},{3,12},{4,11},{5,10},{6,9},{7,8},{8,7},{9,6},... | collective-permute-start | bytes 294920 | tf_op jit(solution)/shard_map/ppermute | solution.py:380

commit v7 on v6

--- a/solution.py
+++ b/solution.py
@@ -11,6 +11,7 @@
 
 TILE = 16
 GROUP = 4
+ON_UNIT = 2
 STEPS = 4
 WINDOW = 6
 LATE = 5
@@ -108,14 +109,17 @@
     wave = np.outer(np.arange(width), np.arange(width)) % width * (2 * math.pi / width)
     c, s = np.cos(wave), np.sin(wave)
     ahead = np.block([[c, -s], [s, c]])
-    short = np.zeros((2, 1, 1))
+    short = back = np.zeros((2, 1, 1))
     if on_matrix_unit(count, tile):
         turn = np.outer(angles, np.arange(count))
         parts = np.stack([np.cos(turn), -np.sin(turn)], axis=1)
         parts = np.concatenate([parts[:2, 0], parts[2:].reshape(-1, count)])
-        short = np.kron(parts, np.eye(tile)).reshape(2, count * tile, count * tile)
+        size = count * tile
+        short = np.kron(parts, np.eye(tile)).reshape(2, size, size)
+        scale = np.where(np.arange(2 * count) < 2, 1.0, 2.0)[:, None] / (2 * size // tile * width)
+        back = np.kron((parts * scale).T, np.eye(tile)).reshape(size, 2, size).swapaxes(0, 1)
     waves = np.stack([ahead, ahead.T])
-    return twist, jnp.asarray(waves, jnp.bfloat16), jnp.asarray(short, jnp.bfloat16)
+    return (twist, *(jnp.asarray(table, jnp.bfloat16) for table in (waves, short, back)))
 
 
 def on_matrix_unit(count, tile):
@@ -220,12 +224,28 @@
     return [jnp.concatenate(part) for part in zip(*parts)]
 
 
+def held_inverse(re, im, twist_ref, wave_ref, held_ref):
+    count, _, width = twist_ref.shape
+    tile = re.shape[0] // count
+    both = jnp.concatenate([re.astype(jnp.bfloat16), im.astype(jnp.bfloat16)], axis=1)
+    back = jnp.dot(both, wave_ref[1], preferred_element_type=jnp.float32)
+    for k in range(count):
+        rows = slice(k * tile, (k + 1) * tile)
+        re, im = back[rows, :width], back[rows, width:]
+        c, s = twist_ref[k, 0:1, :], twist_ref[k, 1:2, :]
+        first = k if k < 2 else 2 * k - 2
+        held_ref[first * tile : (first + 1) * tile] = (re * c - im * s).astype(jnp.bfloat16)
+        if k > 1:
+            rows = slice((first + 1) * tile, (first + 2) * tile)
+            held_ref[rows] = (re * s + im * c).astype(jnp.bfloat16)
+
+
 def filter_kernel(mine_ref, other_ref, twist_ref, wave_ref, short_ref, spec_ref, turned_ref):
     near, far, rows, _ = mine_ref.shape
     tile = spec_ref.shape[1] // twist_ref.shape[0]
     me, side = lax.axis_index("ctx"), lax.axis_index("groups")
     for first, table in ((4, wave_ref), (2, short_ref)):
-        for i in range(2):
+        for i in range(table.shape[0]):
             _, high, wide = table.shape
             spec_ref[spec_ref.shape[0] - first + i, :high, :wide] = table[i]
 
@@ -256,8 +276,8 @@
             spec_ref[half * (rows // tile) + t] = spec.astype(jnp.bfloat16)
 
 
-def spectral_kernel(sig_ref, spec_ref, twist_ref, *refs):
-    *out_refs, made_ref, turned_ref = refs
+def spectral_kernel(sig_ref, spec_ref, twist_ref, back_hbm, *refs):
+    *out_refs, made_ref, turned_ref, held_ref, back_ref, back_sem = refs
     count, _, chunk, width = sig_ref.shape
     tile = spec_ref.shape[1] // twist_ref.shape[0]
     group = turned_ref.shape[0] // spec_ref.shape[1] // 2
@@ -266,14 +286,18 @@
     wave_ref = spec_ref.at[chunk // tile : chunk // tile + 2, : 2 * width]
     short_ref = spec_ref.at[chunk // tile + 2 :, :size, :size]
 
+    on_unit = ON_UNIT if on_matrix_unit(count, tile) else 0
+    fetch = pltpu.make_async_copy(back_hbm, back_ref, back_sem)
+    fetch.start()
+
     def deliver(step):
         lanes = rows_of(step, tile * group)
         for k in range(count):
             out_refs[k][:, lanes] = made_ref[k, :, lanes]
 
-    @pl.loop(0, steps)
-    def _(step):
-        deliver(jnp.maximum(step - 1, 0))
+    for step in range(steps):
+        if step:
+            deliver(step - 1)
         tiles = [step * group + t for t in range(group)]
         blocks = [
             [sig_ref[b, which, rows_of(t, tile)] for b in range(count)]
@@ -290,8 +314,27 @@
                 (g_re * m_re + g_im * m_im, g_im * m_re - g_re * m_im),
             )
             for which, (re, im) in enumerate(results):
+                if which >= 3 - on_unit:
+                    lanes = slice(i * width, (i + 1) * width)
+                    held_inverse(re, im, twist_ref, wave_ref, held_ref.at[which + on_unit - 3, :, lanes])
+                    continue
                 for b, part in enumerate(inverse(re, im, twist_ref, wave_ref)):
                     made_ref[me ^ b, which, rows_of(t, tile)] = part.astype(jnp.bfloat16)
+        if step == 0:
+            fetch.wait()
+        for n in range(on_unit):
+            points = sum(
+                jnp.dot(
+                    back_ref[h],
+                    held_ref[n, h * size : (h + 1) * size],
+                    preferred_element_type=jnp.float32,
+                )
+                for h in range(2)
+            ).astype(jnp.bfloat16)
+            for i, t in enumerate(tiles):
+                for b in range(count):
+                    part = points[b * tile : (b + 1) * tile, i * width : (i + 1) * width]
+                    made_ref[me ^ b, 3 - on_unit + n, rows_of(t, tile)] = part
 
     deliver(steps - 1)
 
@@ -416,7 +459,7 @@
     channels, width = values.shape
     chunk = channels // count
     tile = min(TILE, chunk)
-    twist, wave, short = make_tables(count, width, tile)
+    twist, wave, short, back = make_tables(count, width, tile)
     here = pl.BlockSpec(memory_space=pltpu.VMEM)
     limit = pltpu.CompilerParams(vmem_limit_bytes=24 * 1024 * 1024)
     far = 1 << ((count.bit_length() - 1) // 2)
@@ -453,15 +496,18 @@
     message = jax.ShapeDtypeStruct((3, chunk, width), jnp.bfloat16)
     made = pl.pallas_call(
         spectral_kernel,
-        in_specs=[here] * 3,
+        in_specs=[here] * 3 + [hbm],
         out_specs=[here] * count,
         out_shape=[message] * count,
         scratch_shapes=[
             pltpu.VMEM((count, 3, chunk, width), jnp.bfloat16),
             pltpu.VMEM((2 * group * tall, 2 * width), jnp.bfloat16),
+            pltpu.VMEM((ON_UNIT, 2 * count * tile, group * width), jnp.bfloat16),
+            pltpu.VMEM(back.shape, jnp.bfloat16),
+            pltpu.SemaphoreType.DMA,
         ],
         compiler_params=limit,
-    )(held, spec, twist)
+    )(held, spec, twist, back)
     got = spread(made)
     half = jax.ShapeDtypeStruct((channels, width), jnp.bfloat16)
     wide = jax.ShapeDtypeStruct((channels, width), jnp.float32)

time: 84.3 us -> 83.9 us (level)
  no operation moved by 1% of the time
where the time goes in v7:
time: 83.9 us; the launch traced here: 83.7 us
  starting transfers between devices  40 us (48%)
  waiting for transfers between devices  28.4 us (34%)
  Pallas kernels  13.2 us (16%)
  local copies, waits for them, and re-layouts  1.21 us (1%)
    ppermute x15, starting transfers between devices, spread(): got[k] = lax.ppermute(block, 'ctx', [(j, j ^ k) for j in range(count)])  26.3 us
    ppermute x7, waiting for transfers between devices, swap(): return lax.ppermute(block, axis, [(i, i ^ gap) for i in range(size)])  17.2 us
    all_to_all x1, starting transfers between devices, exchange(): return lax.all_to_all(parts, 'ctx', split_axis=0, concat_axis=0, tiled=True)  7.47 us
    ppermute x7, starting transfers between devices, swap(): return lax.ppermute(block, axis, [(i, i ^ gap) for i in range(size)])  6.2 us
    ppermute x15, waiting for transfers between devices, spread(): got[k] = lax.ppermute(block, 'ctx', [(j, j ^ k) for j in range(count)])  5.91 us
    all_to_all x1, waiting for transfers between devices, exchange(): return lax.all_to_all(parts, 'ctx', split_axis=0, concat_axis=0, tiled=True)  5.29 us
    pallas_call x1, Pallas kernels, shards(): pl.pallas_call(spectral_kernel, in_specs=[here] * 3 + [hbm], out_specs=[h...  4.32 us
    pallas_call x1, Pallas kernels, shards(): pl.pallas_call(functools.partial(first_gates, early, late), in_specs=[hbm...  4.19 us
  transfers between devices with their start and end apart: 23, of which 11 were waited for; matrix products, arithmetic and copies ran while one was open for 0% of the time, Pallas kernels for 9%

profile of v7, /device:TPU:13, one launch (start us, length us, event | category | flops | bytes accessed | tf_op | source)
XLA Modules:
  0.0 83.7 jit_solution(8824124933783487365)
XLA Ops:
  0.7 1.1 %fusion.3 = (bf16[4,64,128]{2,1,0:T(8,128)(2,1)S(1)}, bf16[4,64,128]{2,1,0:T(8,128)(2,1)S(1)}, bf16[4,64,128]{2,1,0:T(8,128)(2,1)S(1)}, bf16[4,64,128]{2,1,0:T(8,128)(2,1)S(1)}) fusion(f32[4,4,2,64,128]{4,3,2,1,0:T(8,128)} %bitcast.30, s32[]{:T(128)S(6)} %select_n.106, s32[]{:T(128)S(6)} %select_n.100, s32[]{:T(128)S(6)} %select_n.104, s32[]{:T(128)S(6)} %select_n.102, ...), kind=kLoop, calls=%fused_computation.8 | loop fusion | bytes 524308 | tf_op jit(solution)/shard_map/convert_element_type | solution.py:446
  1.8 1.4 %collective-permute-start.2 = (bf16[4,64,128]{2,1,0:T(8,128)(2,1)S(1)}, bf16[4,64,128]{2,1,0:T(8,128)(2,1)S(1)}, u32[]{:S(2)}, u32[]{:S(2)}) collective-permute-start(bf16[4,64,128]{2,1,0:T(8,128)(2,1)S(1)} %get-tuple-element.92), channel_id=1, source_target_pairs={{0,12},{1,13},{2,14},{3,15},{4,8},{5,9},{6,10},{7,11},{8,4},{9,5},... | collective-permute-start | bytes 196616 | tf_op jit(solution)/shard_map/ppermute | solution.py:433
  3.2 1.1 %collective-permute-start.1 = (bf16[4,64,128]{2,1,0:T(8,128)(2,1)S(1)}, bf16[4,64,128]{2,1,0:T(8,128)(2,1)S(1)}, u32[]{:S(2)}, u32[]{:S(2)}) collective-permute-start(bf16[4,64,128]{2,1,0:T(8,128)(2,1)S(1)} %get-tuple-element.93), channel_id=1, source_target_pairs={{0,8},{1,9},{2,10},{3,11},{4,12},{5,13},{6,14},{7,15},{8,0},{9,1},... | collective-permute-start | bytes 196616 | tf_op jit(solution)/shard_map/ppermute | solution.py:433
  4.3 1.1 %collective-permute-start = (bf16[4,64,128]{2,1,0:T(8,128)(2,1)S(1)}, bf16[4,64,128]{2,1,0:T(8,128)(2,1)S(1)}, u32[]{:S(2)}, u32[]{:S(2)}) collective-permute-start(bf16[4,64,128]{2,1,0:T(8,128)(2,1)S(1)} %get-tuple-element.94), channel_id=1, source_target_pairs={{0,4},{1,5},{2,6},{3,7},{4,0},{5,1},{6,2},{7,3},{8,12},{9,13},{10,... | collective-permute-start | bytes 196616 | tf_op jit(solution)/shard_map/ppermute | solution.py:433
  5.4 2.5 %shard_map.120 = bf16[16,2,128,128]{3,2,1,0:T(8,128)(2,1)} custom-call(bf16[2048,128]{1,0:T(8,128)(2,1)} %refs_0_.1, bf16[2048,128]{1,0:T(8,128)(2,1)} %refs_1_.1, bf16[2048,128]{1,0:T(8,128)(2,1)} %refs_2_.1, bf16[2048,128]{1,0:T(8,128)(2,1)} %query_hbm.1), custom_call_target="tpu_custom_call" | custom-call | tf_op jit(solution)/shard_map/pallas_call | solution.py:468
  8.0 1.5 %collective-permute-done = bf16[4,64,128]{2,1,0:T(8,128)(2,1)S(1)} collective-permute-done((bf16[4,64,128]{2,1,0:T(8,128)(2,1)S(1)}, bf16[4,64,128]{2,1,0:T(8,128)(2,1)S(1)}, u32[]{:S(2)}, u32[]{:S(2)}) %collective-permute-start) | collective-permute-done | bytes 65568 | tf_op jit(solution)/shard_map/ppermute | solution.py:433
  9.5 7.5 %all-to-all-start = ((bf16[16,2,128,128]{3,2,1,0:T(8,128)(2,1)}), bf16[16,2,128,128]{3,2,1,0:T(8,128)(2,1)S(1)}, u32[]{:S(2)}, u32[]{:S(2)}) async-start(bf16[16,2,128,128]{3,2,1,0:T(8,128)(2,1)} %shard_map.120), calls=%async_computation | async-start | bytes 2097152 | tf_op jit(solution)/shard_map/all_to_all | solution.py:428
  17.5 1.2 %collective-permute-start.4 = (bf16[4,64,128]{2,1,0:T(8,128)(2,1)S(1)}, bf16[4,64,128]{2,1,0:T(8,128)(2,1)S(1)}, u32[]{:S(2)}, u32[]{:S(2)}) collective-permute-start(bf16[4,64,128]{2,1,0:T(8,128)(2,1)S(1)} %pad_maximum_fusion.2), channel_id=1, source_target_pairs={{0,2},{1,3},{2,0},{3,1},{4,6},{5,7},{6,4},{7,5},{8,10},{9,11},{10,... | collective-permute-start | bytes 196616 | tf_op jit(solution)/shard_map/ppermute | solution.py:433
  19.4 5.2 %collective-permute-done.4 = bf16[4,64,128]{2,1,0:T(8,128)(2,1)S(1)} collective-permute-done((bf16[4,64,128]{2,1,0:T(8,128)(2,1)S(1)}, bf16[4,64,128]{2,1,0:T(8,128)(2,1)S(1)}, u32[]{:S(2)}, u32[]{:S(2)}) %collective-permute-start.4) | collective-permute-done | bytes 65568 | tf_op jit(solution)/shard_map/ppermute | solution.py:433
  24.6 2.4 %collective-permute-done.5 = bf16[4,64,128]{2,1,0:T(8,128)(2,1)S(1)} collective-permute-done((bf16[4,64,128]{2,1,0:T(8,128)(2,1)S(1)}, bf16[4,64,128]{2,1,0:T(8,128)(2,1)S(1)}, u32[]{:S(2)}, u32[]{:S(2)}) %collective-permute-start.5) | collective-permute-done | bytes 65568 | tf_op jit(solution)/shard_map/ppermute | solution.py:433
  27.4 8.0 %collective-permute-done.6.other_ref = bf16[4,4,64,128]{3,2,1,0:T(8,128)(2,1)S(1)} collective-permute-done((bf16[4,4,64,128]{3,2,1,0:T(8,128)(2,1)S(1)}, bf16[4,4,64,128]{3,2,1,0:T(8,128)(2,1)S(1)}, u32[]{:S(2)}, u32[]{:S(2)}) %collective-permute-start.6) | collective-permute-done | bytes 262176 | tf_op jit(solution)/shard_map/ppermute | solution.py:433
  35.4 1.1 %shard_map.121.spec_ref = bf16[12,272,256]{2,1,0:T(8,128)(2,1)S(1)} custom-call(bf16[4,4,64,128]{3,2,1,0:T(8,128)(2,1)S(1)} %pad_maximum_fusion.mine_ref, bf16[4,4,64,128]{3,2,1,0:T(8,128)(2,1)S(1)} %collective-permute-done.6.other_ref, f32[17,4,128]{2,1,0:T(4,128)S(1)} %copy-done.6, bf16[2,256,256]{2,1,0:T(8,128)(2,1)S(1)} %copy-done.5, ...), custom_call_target="tpu_custom_call" | custom-call | flops 268435456 | bytes 1048576 | tf_op jit(solution)/shard_map/pallas_call | solution.py:485
  36.5 5.3 %all-to-all-done.sig_ref = bf16[16,2,128,128]{3,2,1,0:T(8,128)(2,1)S(1)} async-done(((bf16[16,2,128,128]{3,2,1,0:T(8,128)(2,1)}), bf16[16,2,128,128]{3,2,1,0:T(8,128)(2,1)S(1)}, u32[]{:S(2)}, u32[]{:S(2)}) %all-to-all-start) | async-done | bytes 1048608 | tf_op jit(solution)/shard_map/all_to_all | solution.py:428
  41.8 4.3 %shard_map.122 = (bf16[3,128,128]{2,1,0:T(8,128)(2,1)S(1)}, bf16[3,128,128]{2,1,0:T(8,128)(2,1)S(1)}, bf16[3,128,128]{2,1,0:T(8,128)(2,1)S(1)}, bf16[3,128,128]{...) custom-call(bf16[16,2,128,128]{3,2,1,0:T(8,128)(2,1)S(1)} %all-to-al, ...), custom_call_target="tpu_custom_call" | custom-call | tf_op jit(solution)/shard_map/pallas_call | solution.py:497
  46.5 1.9 %collective-permute-start.8 = (bf16[3,128,128]{2,1,0:T(8,128)(2,1)S(1)}, bf16[3,128,128]{2,1,0:T(8,128)(2,1)S(1)}, u32[]{:S(2)}, u32[]{:S(2)}) collective-permute-start(bf16[3,128,128]{2,1,0:T(8,128)(2,1)S(1)} %get-tuple-element.58), channel_id=1, source_target_pairs={{0,4},{1,5},{2,6},{3,7},{4,0},{5,1},{6,2},{7,3},{8,12},{9,13},{10,... | collective-permute-start | bytes 294920 | tf_op jit(solution)/shard_map/ppermute | solution.py:423
  48.4 1.1 %collective-permute-start.9 = (bf16[3,128,128]{2,1,0:T(8,128)(2,1)S(1)}, bf16[3,128,128]{2,1,0:T(8,128)(2,1)S(1)}, u32[]{:S(2)}, u32[]{:S(2)}) collective-permute-start(bf16[3,128,128]{2,1,0:T(8,128)(2,1)S(1)} %get-tuple-element.61), channel_id=1, source_target_pairs={{0,9},{1,8},{2,11},{3,10},{4,13},{5,12},{6,15},{7,14},{8,1},{9,0},... | collective-permute-start | bytes 294920 | tf_op jit(solution)/shard_map/ppermute | solution.py:423
  49.5 0.8 collective-permute-start.10
  50.3 2.1 %collective-permute-start.11 = (bf16[3,128,128]{2,1,0:T(8,128)(2,1)S(1)}, bf16[3,128,128]{2,1,0:T(8,128)(2,1)S(1)}, u32[]{:S(2)}, u32[]{:S(2)}) collective-permute-start(bf16[3,128,128]{2,1,0:T(8,128)(2,1)S(1)} %get-tuple-element.67), channel_id=1, source_target_pairs={{0,10},{1,11},{2,8},{3,9},{4,14},{5,15},{6,12},{7,13},{8,2},{9,3},... | collective-permute-start | bytes 294920 | tf_op jit(solution)/shard_map/ppermute | solution.py:423
  52.5 1.0 %collective-permute-start.12 = (bf16[3,128,128]{2,1,0:T(8,128)(2,1)S(1)}, bf16[3,128,128]{2,1,0:T(8,128)(2,1)S(1)}, u32[]{:S(2)}, u32[]{:S(2)}) collective-permute-start(bf16[3,128,128]{2,1,0:T(8,128)(2,1)S(1)} %get-tuple-element.70), channel_id=1, source_target_pairs={{0,6},{1,7},{2,4},{3,5},{4,2},{5,3},{6,0},{7,1},{8,14},{9,15},{10,... | collective-permute-start | bytes 294920 | tf_op jit(solution)/shard_map/ppermute | solution.py:423
  53.4 4.4 %collective-permute-start.13 = (bf16[3,128,128]{2,1,0:T(8,128)(2,1)S(1)}, bf16[3,128,128]{2,1,0:T(8,128)(2,1)S(1)}, u32[]{:S(2)}, u32[]{:S(2)}) collective-permute-start(bf16[3,128,128]{2,1,0:T(8,128)(2,1)S(1)} %get-tuple-element.73), channel_id=1, source_target_pairs={{0,11},{1,10},{2,9},{3,8},{4,15},{5,14},{6,13},{7,12},{8,3},{9,2},... | collective-permute-start | bytes 294920 | tf_op jit(solution)/shard_map/ppermute | solution.py:423
  57.8 0.8 collective-permute-start.14
  59.7 1.4 %collective-permute-done.11.refs_8_ = bf16[3,128,128]{2,1,0:T(8,128)(2,1)S(1)} collective-permute-done((bf16[3,128,128]{2,1,0:T(8,128)(2,1)S(1)}, bf16[3,128,128]{2,1,0:T(8,128)(2,1)S(1)}, u32[]{:S(2)}, u32[]{:S(2)}) %collective-permute-start.11) | collective-permute-done | bytes 98336 | tf_op jit(solution)/shard_map/ppermute | solution.py:423
  61.2 0.8 collective-permute-start.16
  62.3 3.2 %collective-permute-start.17 = (bf16[3,128,128]{2,1,0:T(8,128)(2,1)S(1)}, bf16[3,128,128]{2,1,0:T(8,128)(2,1)S(1)}, u32[]{:S(2)}, u32[]{:S(2)}) collective-permute-start(bf16[3,128,128]{2,1,0:T(8,128)(2,1)S(1)} %get-tuple-element.83), channel_id=1, source_target_pairs={{0,13},{1,12},{2,15},{3,14},{4,9},{5,8},{6,11},{7,10},{8,5},{9,4},... | collective-permute-start | bytes 294920 | tf_op jit(solution)/shard_map/ppermute | solution.py:423
  65.5 1.1 %collective-permute-done.13.refs_10_ = bf16[3,128,128]{2,1,0:T(8,128)(2,1)S(1)} collective-permute-done((bf16[3,128,128]{2,1,0:T(8,128)(2,1)S(1)}, bf16[3,128,128]{2,1,0:T(8,128)(2,1)S(1)}, u32[]{:S(2)}, u32[]{:S(2)}) %collective-permute-start.13) | collective-permute-done | bytes 98336 | tf_op jit(solution)/shard_map/ppermute | solution.py:423
  66.7 1.0 %collective-permute-start.18 = (bf16[3,128,128]{2,1,0:T(8,128)(2,1)S(1)}, bf16[3,128,128]{2,1,0:T(8,128)(2,1)S(1)}, u32[]{:S(2)}, u32[]{:S(2)}) collective-permute-start(bf16[3,128,128]{2,1,0:T(8,128)(2,1)S(1)} %get-tuple-element.84), channel_id=1, source_target_pairs={{0,3},{1,2},{2,1},{3,0},{4,7},{5,6},{6,5},{7,4},{8,11},{9,10},{10,... | collective-permute-start | bytes 294920 | tf_op jit(solution)/shard_map/ppermute | solution.py:423
  67.7 1.1 %collective-permute-start.19 = (bf16[3,128,128]{2,1,0:T(8,128)(2,1)S(1)}, bf16[3,128,128]{2,1,0:T(8,128)(2,1)S(1)}, u32[]{:S(2)}, u32[]{:S(2)}) collective-permute-start(bf16[3,128,128]{2,1,0:T(8,128)(2,1)S(1)} %get-tuple-element.85), channel_id=1, source_target_pairs={{0,14},{1,15},{2,12},{3,13},{4,10},{5,11},{6,8},{7,9},{8,6},{9,7},... | collective-permute-start | bytes 294920 | tf_op jit(solution)/shard_map/ppermute | solution.py:423
  68.8 6.1 %collective-permute-start.20 = (bf16[3,128,128]{2,1,0:T(8,128)(2,1)S(1)}, bf16[3,128,128]{2,1,0:T(8,128)(2,1)S(1)}, u32[]{:S(2)}, u32[]{:S(2)}) collective-permute-start(bf16[3,128,128]{2,1,0:T(8,128)(2,1)S(1)} %get-tuple-element.86), channel_id=1, source_target_pairs={{0,1},{1,0},{2,3},{3,2},{4,5},{5,4},{6,7},{7,6},{8,9},{9,8},{10,11... | collective-permute-start | bytes 294920 | tf_op jit(solution)/shard_map/ppermute | solution.py:423
  74.9 1.1 %collective-permute-start.21 = (bf16[3,128,128]{2,1,0:T(8,128)(2,1)S(1)}, bf16[3,128,128]{2,1,0:T(8,128)(2,1)S(1)}, u32[]{:S(2)}, u32[]{:S(2)}) collective-permute-start(bf16[3,128,128]{2,1,0:T(8,128)(2,1)S(1)} %get-tuple-element.87), channel_id=1, source_target_pairs={{0,15},{1,14},{2,13},{3,12},{4,11},{5,10},{6,9},{7,8},{8,7},{9,6},... | collective-permute-start | bytes 294920 | tf_op jit(solution)/shard_map/ppermute | solution.py:423
  76.0 4.2 %shard_map.123 = (bf16[2048,128]{1,0:T(8,128)(2,1)}, bf16[2048,128]{1,0:T(8,128)(2,1)}, bf16[2048,128]{1,0:T(8,128)(2,1)}, f32[2048,128]{1,0:T(8,128)}, bf16[5,3,128,128]{3,2,1,0:T(8,128)(2,1)S(1)}) custom-call(bf16[2048,128]{1,0:T(8,128)(2,1)S(1)} %copy-done, bf16[2048,128]{1,0:T(8,128)(2,1)S(1)} %copy-done.1, bf16[2048,128]{1,0:T(8,128)(2,1)S(1)} %copy-done.2, ...), custom_call_target="tpu_custom_call" | custom-call | tf_op jit(solution)/shard_map/pallas_call | solution.py:519
  80.5 2.1 %collective-permute-done.21.refs_4_ = bf16[3,128,128]{2,1,0:T(8,128)(2,1)S(1)} collective-permute-done((bf16[3,128,128]{2,1,0:T(8,128)(2,1)S(1)}, bf16[3,128,128]{2,1,0:T(8,128)(2,1)S(1)}, u32[]{:S(2)}, u32[]{:S(2)}) %collective-permute-start.21) | collective-permute-done | bytes 98336 | tf_op jit(solution)/shard_map/ppermute | solution.py:423
  82.6 1.1 %shard_map.124 = (bf16[2048,128]{1,0:T(8,128)(2,1)}, bf16[2048,128]{1,0:T(8,128)(2,1)}, bf16[2048,128]{1,0:T(8,128)(2,1)}, f32[2048,128]{1,0:T(8,128)}) custom-call(bf16[5,3,128,128]{3,2,1,0:T(8,128)(2,1)S(1)} %get-tuple-element.82.held_ref, ...), custom_call_target="tpu_custom_call", output_to_operand_aliasing={{0}: (6, {}), {1}: (7, {}), {2}: (8, {}), {3}: (9, {})} | custom-call | tf_op jit(solution)/shard_map/pallas_call | solution.py:533
  (41 shorter events, 3.7 us)
Async XLA Ops:
  1.8 6.1 %collective-permute-start.2 = (bf16[4,64,128]{2,1,0:T(8,128)(2,1)S(1)}, bf16[4,64,128]{2,1,0:T(8,128)(2,1)S(1)}, u32[]{:S(2)}, u32[]{:S(2)}) collective-permute-start(bf16[4,64,128]{2,1,0:T(8,128)(2,1)S(1)} %get-tuple-element.92), channel_id=1, source_target_pairs={{0,12},{1,13},{2,14},{3,15},{4,8},{5,9},{6,10},{7,11},{8,4},{9,5},... | collective-permute-start | bytes 196616 | tf_op jit(solution)/shard_map/ppermute | solution.py:433
  3.2 4.8 %collective-permute-start.1 = (bf16[4,64,128]{2,1,0:T(8,128)(2,1)S(1)}, bf16[4,64,128]{2,1,0:T(8,128)(2,1)S(1)}, u32[]{:S(2)}, u32[]{:S(2)}) collective-permute-start(bf16[4,64,128]{2,1,0:T(8,128)(2,1)S(1)} %get-tuple-element.93), channel_id=1, source_target_pairs={{0,8},{1,9},{2,10},{3,11},{4,12},{5,13},{6,14},{7,15},{8,0},{9,1},... | collective-permute-start | bytes 196616 | tf_op jit(solution)/shard_map/ppermute | solution.py:433
  4.3 5.2 %collective-permute-start = (bf16[4,64,128]{2,1,0:T(8,128)(2,1)S(1)}, bf16[4,64,128]{2,1,0:T(8,128)(2,1)S(1)}, u32[]{:S(2)}, u32[]{:S(2)}) collective-permute-start(bf16[4,64,128]{2,1,0:T(8,128)(2,1)S(1)} %get-tuple-element.94), channel_id=1, source_target_pairs={{0,4},{1,5},{2,6},{3,7},{4,0},{5,1},{6,2},{7,3},{8,12},{9,13},{10,... | collective-permute-start | bytes 196616 | tf_op jit(solution)/shard_map/ppermute | solution.py:433
  9.5 25.9 %copy-start.4 = (bf16[2,256,256]{2,1,0:T(8,128)(2,1)S(1)}, bf16[2,256,256]{2,1,0:T(8,128)(2,1)}, u32[]{:S(2)}) copy-start(bf16[2,256,256]{2,1,0:T(8,128)(2,1)} %constant.227.clone.short_ref) | copy-start | bytes 786436
  9.5 25.9 %copy-start.5 = (bf16[2,256,256]{2,1,0:T(8,128)(2,1)S(1)}, bf16[2,256,256]{2,1,0:T(8,128)(2,1)}, u32[]{:S(2)}) copy-start(bf16[2,256,256]{2,1,0:T(8,128)(2,1)} %constant.226.clone.wave_ref) | copy-start | bytes 786436
  9.5 25.9 %copy-start.6 = (f32[17,4,128]{2,1,0:T(4,128)S(1)}, f32[17,4,128]{2,1,0:T(4,128)}, u32[]{:S(2)}) copy-start(f32[17,4,128]{2,1,0:T(4,128)} %constant.229.clone.twist_ref) | copy-start | bytes 104452
  9.5 32.3 %all-to-all-start = ((bf16[16,2,128,128]{3,2,1,0:T(8,128)(2,1)}), bf16[16,2,128,128]{3,2,1,0:T(8,128)(2,1)S(1)}, u32[]{:S(2)}, u32[]{:S(2)}) async-start(bf16[16,2,128,128]{3,2,1,0:T(8,128)(2,1)} %shard_map.120), calls=%async_computation | async-start | bytes 2097152 | tf_op jit(solution)/shard_map/all_to_all | solution.py:428
  17.0 2.4 %collective-permute-start.3 = (bf16[4,64,128]{2,1,0:T(8,128)(2,1)S(1)}, bf16[4,64,128]{2,1,0:T(8,128)(2,1)S(1)}, u32[]{:S(2)}, u32[]{:S(2)}) collective-permute-start(bf16[4,64,128]{2,1,0:T(8,128)(2,1)S(1)} %pad_maximum_fusion.1), channel_id=1, source_target_pairs={{0,1},{1,0},{2,3},{3,2},{4,5},{5,4},{6,7},{7,6},{8,9},{9,8},{10,11... | collective-permute-start | bytes 196616 | tf_op jit(solution)/shard_map/ppermute | solution.py:433
  17.5 7.1 %collective-permute-start.4 = (bf16[4,64,128]{2,1,0:T(8,128)(2,1)S(1)}, bf16[4,64,128]{2,1,0:T(8,128)(2,1)S(1)}, u32[]{:S(2)}, u32[]{:S(2)}) collective-permute-start(bf16[4,64,128]{2,1,0:T(8,128)(2,1)S(1)} %pad_maximum_fusion.2), channel_id=1, source_target_pairs={{0,2},{1,3},{2,0},{3,1},{4,6},{5,7},{6,4},{7,5},{8,10},{9,11},{10,... | collective-permute-start | bytes 196616 | tf_op jit(solution)/shard_map/ppermute | solution.py:433
  18.7 8.3 %collective-permute-start.5 = (bf16[4,64,128]{2,1,0:T(8,128)(2,1)S(1)}, bf16[4,64,128]{2,1,0:T(8,128)(2,1)S(1)}, u32[]{:S(2)}, u32[]{:S(2)}) collective-permute-start(bf16[4,64,128]{2,1,0:T(8,128)(2,1)S(1)} %pad_maximum_fusion.3), channel_id=1, source_target_pairs={{0,3},{1,2},{2,1},{3,0},{4,7},{5,6},{6,5},{7,4},{8,11},{9,10},{10,... | collective-permute-start | bytes 196616 | tf_op jit(solution)/shard_map/ppermute | solution.py:433
  19.4 22.4 %copy-start.3 = (bf16[2,256,256]{2,1,0:T(8,128)(2,1)S(1)}, bf16[2,256,256]{2,1,0:T(8,128)(2,1)}, u32[]{:S(2)}) copy-start(bf16[2,256,256]{2,1,0:T(8,128)(2,1)} %constant.228.clone.back_hbm) | copy-start | bytes 786436
  27.1 8.3 %collective-permute-start.6 = (bf16[4,4,64,128]{3,2,1,0:T(8,128)(2,1)S(1)}, bf16[4,4,64,128]{3,2,1,0:T(8,128)(2,1)S(1)}, u32[]{:S(2)}, u32[]{:S(2)}) collective-permute-start(bf16[4,4,64,128]{3,2,1,0:T(8,128)(2,1)S(1)} %pad_maximum_fusion.mine_ref), channel_id=1, source_target_pairs={{0,16},{16,0},{1,17},{17,1},{2,18},{18,2},{3,19},{19,3},{4,20},{20... | collective-permute-start | bytes 786440 | tf_op jit(solution)/shard_map/ppermute | solution.py:433
  36.5 39.5 %copy-start = (bf16[2048,128]{1,0:T(8,128)(2,1)S(1)}, bf16[2048,128]{1,0:T(8,128)(2,1)}, u32[]{:S(2)}) copy-start(bf16[2048,128]{1,0:T(8,128)(2,1)} %refs_0_.1) | copy-start | bytes 1572868
  41.8 34.2 %copy-start.1 = (bf16[2048,128]{1,0:T(8,128)(2,1)S(1)}, bf16[2048,128]{1,0:T(8,128)(2,1)}, u32[]{:S(2)}) copy-start(bf16[2048,128]{1,0:T(8,128)(2,1)} %refs_1_.1) | copy-start | bytes 1572868
  41.8 34.2 %copy-start.2 = (bf16[2048,128]{1,0:T(8,128)(2,1)S(1)}, bf16[2048,128]{1,0:T(8,128)(2,1)}, u32[]{:S(2)}) copy-start(bf16[2048,128]{1,0:T(8,128)(2,1)} %refs_2_.1) | copy-start | bytes 1572868
  46.1 6.3 %collective-permute-start.7 = (bf16[3,128,128]{2,1,0:T(8,128)(2,1)S(1)}, bf16[3,128,128]{2,1,0:T(8,128)(2,1)S(1)}, u32[]{:S(2)}, u32[]{:S(2)}) collective-permute-start(bf16[3,128,128]{2,1,0:T(8,128)(2,1)S(1)} %get-tuple-element.55), channel_id=1, source_target_pairs={{0,8},{1,9},{2,10},{3,11},{4,12},{5,13},{6,14},{7,15},{8,0},{9,1},... | collective-permute-start | bytes 294920 | tf_op jit(solution)/shard_map/ppermute | solution.py:423
  46.5 6.9 %collective-permute-start.8 = (bf16[3,128,128]{2,1,0:T(8,128)(2,1)S(1)}, bf16[3,128,128]{2,1,0:T(8,128)(2,1)S(1)}, u32[]{:S(2)}, u32[]{:S(2)}) collective-permute-start(bf16[3,128,128]{2,1,0:T(8,128)(2,1)S(1)} %get-tuple-element.58), channel_id=1, source_target_pairs={{0,4},{1,5},{2,6},{3,7},{4,0},{5,1},{6,2},{7,3},{8,12},{9,13},{10,... | collective-permute-start | bytes 294920 | tf_op jit(solution)/shard_map/ppermute | solution.py:423
  48.4 9.4 %collective-permute-start.9 = (bf16[3,128,128]{2,1,0:T(8,128)(2,1)S(1)}, bf16[3,128,128]{2,1,0:T(8,128)(2,1)S(1)}, u32[]{:S(2)}, u32[]{:S(2)}) collective-permute-start(bf16[3,128,128]{2,1,0:T(8,128)(2,1)S(1)} %get-tuple-element.61), channel_id=1, source_target_pairs={{0,9},{1,8},{2,11},{3,10},{4,13},{5,12},{6,15},{7,14},{8,1},{9,0},... | collective-permute-start | bytes 294920 | tf_op jit(solution)/shard_map/ppermute | solution.py:423
  49.5 9.6 %collective-permute-start.10 = (bf16[3,128,128]{2,1,0:T(8,128)(2,1)S(1)}, bf16[3,128,128]{2,1,0:T(8,128)(2,1)S(1)}, u32[]{:S(2)}, u32[]{:S(2)}) collective-permute-start(bf16[3,128,128]{2,1,0:T(8,128)(2,1)S(1)} %get-tuple-element.64), channel_id=1, source_target_pairs={{0,5},{1,4},{2,7},{3,6},{4,1},{5,0},{6,3},{7,2},{8,13},{9,12},{10,... | collective-permute-start | bytes 294920 | tf_op jit(solution)/shard_map/ppermute | solution.py:423
  50.3 10.8 %collective-permute-start.11 = (bf16[3,128,128]{2,1,0:T(8,128)(2,1)S(1)}, bf16[3,128,128]{2,1,0:T(8,128)(2,1)S(1)}, u32[]{:S(2)}, u32[]{:S(2)}) collective-permute-start(bf16[3,128,128]{2,1,0:T(8,128)(2,1)S(1)} %get-tuple-element.67), channel_id=1, source_target_pairs={{0,10},{1,11},{2,8},{3,9},{4,14},{5,15},{6,12},{7,13},{8,2},{9,3},... | collective-permute-start | bytes 294920 | tf_op jit(solution)/shard_map/ppermute | solution.py:423
  52.5 9.9 %collective-permute-start.12 = (bf16[3,128,128]{2,1,0:T(8,128)(2,1)S(1)}, bf16[3,128,128]{2,1,0:T(8,128)(2,1)S(1)}, u32[]{:S(2)}, u32[]{:S(2)}) collective-permute-start(bf16[3,128,128]{2,1,0:T(8,128)(2,1)S(1)} %get-tuple-element.70), channel_id=1, source_target_pairs={{0,6},{1,7},{2,4},{3,5},{4,2},{5,3},{6,0},{7,1},{8,14},{9,15},{10,... | collective-permute-start | bytes 294920 | tf_op jit(solution)/shard_map/ppermute | solution.py:423
  53.4 13.2 %collective-permute-start.13 = (bf16[3,128,128]{2,1,0:T(8,128)(2,1)S(1)}, bf16[3,128,128]{2,1,0:T(8,128)(2,1)S(1)}, u32[]{:S(2)}, u32[]{:S(2)}) collective-permute-start(bf16[3,128,128]{2,1,0:T(8,128)(2,1)S(1)} %get-tuple-element.73), channel_id=1, source_target_pairs={{0,11},{1,10},{2,9},{3,8},{4,15},{5,14},{6,13},{7,12},{8,3},{9,2},... | collective-permute-start | bytes 294920 | tf_op jit(solution)/shard_map/ppermute | solution.py:423
  57.8 9.9 %collective-permute-start.14 = (bf16[3,128,128]{2,1,0:T(8,128)(2,1)S(1)}, bf16[3,128,128]{2,1,0:T(8,128)(2,1)S(1)}, u32[]{:S(2)}, u32[]{:S(2)}) collective-permute-start(bf16[3,128,128]{2,1,0:T(8,128)(2,1)S(1)} %get-tuple-element.76), channel_id=1, source_target_pairs={{0,7},{1,6},{2,5},{3,4},{4,3},{5,2},{6,1},{7,0},{8,15},{9,14},{10,... | collective-permute-start | bytes 294920 | tf_op jit(solution)/shard_map/ppermute | solution.py:423
  59.1 9.7 %collective-permute-start.15 = (bf16[3,128,128]{2,1,0:T(8,128)(2,1)S(1)}, bf16[3,128,128]{2,1,0:T(8,128)(2,1)S(1)}, u32[]{:S(2)}, u32[]{:S(2)}) collective-permute-start(bf16[3,128,128]{2,1,0:T(8,128)(2,1)S(1)} %get-tuple-element.79), channel_id=1, source_target_pairs={{0,12},{1,13},{2,14},{3,15},{4,8},{5,9},{6,10},{7,11},{8,4},{9,5},... | collective-permute-start | bytes 294920 | tf_op jit(solution)/shard_map/ppermute | solution.py:423
  61.2 13.7 %collective-permute-start.16 = (bf16[3,128,128]{2,1,0:T(8,128)(2,1)S(1)}, bf16[3,128,128]{2,1,0:T(8,128)(2,1)S(1)}, u32[]{:S(2)}, u32[]{:S(2)}) collective-permute-start(bf16[3,128,128]{2,1,0:T(8,128)(2,1)S(1)} %get-tuple-element.81), channel_id=1, source_target_pairs={{0,2},{1,3},{2,0},{3,1},{4,6},{5,7},{6,4},{7,5},{8,10},{9,11},{10,... | collective-permute-start | bytes 294920 | tf_op jit(solution)/shard_map/ppermute | solution.py:423
  62.3 17.9 %collective-permute-start.17 = (bf16[3,128,128]{2,1,0:T(8,128)(2,1)S(1)}, bf16[3,128,128]{2,1,0:T(8,128)(2,1)S(1)}, u32[]{:S(2)}, u32[]{:S(2)}) collective-permute-start(bf16[3,128,128]{2,1,0:T(8,128)(2,1)S(1)} %get-tuple-element.83), channel_id=1, source_target_pairs={{0,13},{1,12},{2,15},{3,14},{4,9},{5,8},{6,11},{7,10},{8,5},{9,4},... | collective-permute-start | bytes 294920 | tf_op jit(solution)/shard_map/ppermute | solution.py:423
  66.7 13.6 %collective-permute-start.18 = (bf16[3,128,128]{2,1,0:T(8,128)(2,1)S(1)}, bf16[3,128,128]{2,1,0:T(8,128)(2,1)S(1)}, u32[]{:S(2)}, u32[]{:S(2)}) collective-permute-start(bf16[3,128,128]{2,1,0:T(8,128)(2,1)S(1)} %get-tuple-element.84), channel_id=1, source_target_pairs={{0,3},{1,2},{2,1},{3,0},{4,7},{5,6},{6,5},{7,4},{8,11},{9,10},{10,... | collective-permute-start | bytes 294920 | tf_op jit(solution)/shard_map/ppermute | solution.py:423
  67.7 12.8 %collective-permute-start.19 = (bf16[3,128,128]{2,1,0:T(8,128)(2,1)S(1)}, bf16[3,128,128]{2,1,0:T(8,128)(2,1)S(1)}, u32[]{:S(2)}, u32[]{:S(2)}) collective-permute-start(bf16[3,128,128]{2,1,0:T(8,128)(2,1)S(1)} %get-tuple-element.85), channel_id=1, source_target_pairs={{0,14},{1,15},{2,12},{3,13},{4,10},{5,11},{6,8},{7,9},{8,6},{9,7},... | collective-permute-start | bytes 294920 | tf_op jit(solution)/shard_map/ppermute | solution.py:423
  68.8 11.7 %collective-permute-start.20 = (bf16[3,128,128]{2,1,0:T(8,128)(2,1)S(1)}, bf16[3,128,128]{2,1,0:T(8,128)(2,1)S(1)}, u32[]{:S(2)}, u32[]{:S(2)}) collective-permute-start(bf16[3,128,128]{2,1,0:T(8,128)(2,1)S(1)} %get-tuple-element.86), channel_id=1, source_target_pairs={{0,1},{1,0},{2,3},{3,2},{4,5},{5,4},{6,7},{7,6},{8,9},{9,8},{10,11... | collective-permute-start | bytes 294920 | tf_op jit(solution)/shard_map/ppermute | solution.py:423
  74.9 7.7 %collective-permute-start.21 = (bf16[3,128,128]{2,1,0:T(8,128)(2,1)S(1)}, bf16[3,128,128]{2,1,0:T(8,128)(2,1)S(1)}, u32[]{:S(2)}, u32[]{:S(2)}) collective-permute-start(bf16[3,128,128]{2,1,0:T(8,128)(2,1)S(1)} %get-tuple-element.87), channel_id=1, source_target_pairs={{0,15},{1,14},{2,13},{3,12},{4,11},{5,10},{6,9},{7,8},{8,7},{9,6},... | collective-permute-start | bytes 294920 | tf_op jit(solution)/shard_map/ppermute | solution.py:423
